TPU v7x, 32 devices: a whole 2x2x4 slice. The times are simulated.
32 devices in a mesh: shard: 4 (over z), ctx: 4 (over y, core), tp: 2 (over x).
Axes of the slice: x: 2, y: 2, z: 4, core: 2. Of those that a mesh axis runs over, the one named last changes fastest.
Arguments:
- inputs: bfloat16 [8, 2048, 1024], P('shard', 'ctx', 'tp'), may hold values from -6 to 6
- ln1_gain: bfloat16 [1024], replicated, may hold values from 0.099609375 to 1.8984375
- ln1_bias: bfloat16 [1024], replicated, may hold values from -3 to 3
- w_qkv: bfloat16 [1024, 3, 1024], P('shard', None, 'tp'), may hold values from -0.1875 to 0.1875
- b_qkv: bfloat16 [3, 1024], P(None, 'tp'), may hold values from -3 to 3
- w_out: bfloat16 [1024, 1024], P('tp', 'shard'), may hold values from -3 to 3
- b_out: bfloat16 [1024], P('tp'), may hold values from -3 to 3
- ln2_gain: bfloat16 [1024], replicated, may hold values from 0.099609375 to 1.8984375
- ln2_bias: bfloat16 [1024], replicated, may hold values from -3 to 3
- w_in: bfloat16 [1024, 4096], P('shard', 'tp'), may hold values from -0.1875 to 0.1875
- b_in: bfloat16 [4096], P('tp'), may hold values from -3 to 3
- w_back: bfloat16 [4096, 1024], P('tp', 'shard'), may hold values from -0.1875 to 0.1875
- b_back: bfloat16 [1024], P('tp'), may hold values from -3 to 3
- cotangent: bfloat16 [8, 2048, 1024], P('shard', 'ctx', 'tp'), may hold values from -6 to 6
Outputs:
- output: bfloat16 [8, 2048, 1024], P('shard', 'ctx', 'tp')
- input_grad: float32 [8, 2048, 1024], P('shard', 'ctx', 'tp')
- grad_ln1_gain: float32 [1024], replicated
- grad_ln1_bias: float32 [1024], replicated
- grad_w_qkv: float32 [1024, 3, 1024], P('shard', None, 'tp')
- grad_b_qkv: float32 [3, 1024], P(None, 'tp')
- grad_w_out: float32 [1024, 1024], P('tp', 'shard')
- grad_b_out: float32 [1024], P('tp')
- grad_ln2_gain: float32 [1024], replicated
- grad_ln2_bias: float32 [1024], replicated
- grad_w_in: float32 [1024, 4096], P('shard', 'tp')
- grad_b_in: float32 [4096], P('tp')
- grad_w_back: float32 [4096, 1024], P('tp', 'shard')
- grad_b_back: float32 [1024], P('tp')
All inputs are finite; a program needn't handle non-finite values.
Results may differ from a plain program's by a relative error of at most 0.023.
Values may be sent and summed in bfloat16 or wider, within the bound.
A program may use at most 192 MiB of HBM per device.

v0:
```python
import math

import jax
import jax.numpy as jnp
from jax import lax
from jax.sharding import PartitionSpec as P

HEAD_DIM = 64
GH = 16
GW = 16


EPSILON = 1e-06
NEG_LARGE = -1e30


def rotary_tables(first_row, row_count):
    segment = 2 * (HEAD_DIM // 3 // 2)
    halfway = segment // 2
    places = first_row + jnp.arange(row_count, dtype=jnp.int32)
    frames = places // (GH * GW)
    rows_at = places // GW % GH
    cols_at = places % GW
    column = jnp.arange(HEAD_DIM, dtype=jnp.int32)
    segment_of = column // segment
    within = column % segment
    frequency = jnp.power(10000.0, -(within % halfway).astype(jnp.float32) / halfway)
    position = jnp.where(
        segment_of[None, :] == 0,
        frames[:, None],
        jnp.where(segment_of[None, :] == 1, rows_at[:, None], cols_at[:, None]),
    )
    angles = position.astype(jnp.float32) * frequency[None, :]
    active = (column < 3 * segment)[None, :]
    cosines = jnp.where(active, jnp.cos(angles), 1.0)
    sine_table = jnp.where(
        active, jnp.where((within < halfway)[None, :], -jnp.sin(angles), jnp.sin(angles)), 0.0
    )
    return (cosines, sine_table)


def partner(tensor):
    segment = 2 * (HEAD_DIM // 3 // 2)
    halfway = segment // 2
    pieces = []
    for number in range(3):
        offset = number * segment
        pieces.append(tensor[..., offset + halfway : offset + segment])
        pieces.append(tensor[..., offset : offset + halfway])
    pieces.append(tensor[..., 3 * segment :])
    return jnp.concatenate(pieces, axis=-1)


def rotate(tensor, cosines, sine_table):
    return tensor * cosines + partner(tensor) * sine_table


def rotate_back(gradient, cosines, sine_table):
    return gradient * cosines + partner(gradient * sine_table)


def normalize(tensor, gain, shift):
    center = tensor - jnp.mean(tensor, axis=-1, keepdims=True)
    spread = jnp.mean(center * center, axis=-1, keepdims=True)
    inv_std = lax.rsqrt(spread + EPSILON)
    scaled = center * inv_std
    return (scaled * gain + shift, scaled, inv_std)


def norm_back(grad_out, scaled, inv_std, gain):
    grad_scaled = grad_out * gain
    mean_one = jnp.mean(grad_scaled, axis=-1, keepdims=True)
    mean_two = jnp.mean(grad_scaled * scaled, axis=-1, keepdims=True)
    return inv_std * (grad_scaled - mean_one - scaled * mean_two)


def tp_rows(sharded):
    return lax.all_gather(sharded, "tp", axis=2, tiled=True)


def tensor_sum(summand):
    return lax.psum_scatter(
        summand.astype(jnp.bfloat16), "tp", scatter_dimension=2, tiled=True
    ).astype(jnp.float32)


def back_total(summand):
    return lax.psum(summand.astype(jnp.bfloat16), "tp").astype(jnp.float32)


def fetch_weights(w_qkv, w_out, w_in, w_back):
    return (
        lax.all_gather(w_qkv, "shard", axis=0, tiled=True),
        lax.all_gather(w_out, "shard", axis=1, tiled=True),
        lax.all_gather(w_in, "shard", axis=0, tiled=True),
        lax.all_gather(w_back, "shard", axis=1, tiled=True),
    )


def forward(inputs, params, weights, cosines, sine_table):
    gain_one, shift_one, b_qkv, b_out, gain_two, shift_two, b_in, b_back = params
    w_qkv_all, w_out_all, w_in_all, w_back_all = weights
    clip_count, row_count, width_local = inputs.shape
    heads_local = width_local // HEAD_DIM
    score_scale = HEAD_DIM ** (-0.5)
    tokens = tp_rows(inputs).astype(jnp.float32)
    normed, scaled_one, inv_one = normalize(tokens, gain_one, shift_one)
    normed_low = normed.astype(jnp.bfloat16)
    joined = (
        jnp.einsum("csd,dkh->cskh", normed_low, w_qkv_all, preferred_element_type=jnp.float32)
        + b_qkv
    )
    shaped = joined.reshape(clip_count, row_count, 3, heads_local, HEAD_DIM)
    queries = rotate(shaped[:, :, 0], cosines, sine_table).astype(jnp.bfloat16)
    key_rows = rotate(shaped[:, :, 1], cosines, sine_table).astype(jnp.bfloat16)
    values = shaped[:, :, 2].astype(jnp.bfloat16)
    key_flat = key_rows.reshape(clip_count, row_count, width_local)
    value_flat = values.reshape(clip_count, row_count, width_local)

    def absorb_block(running, block_pair):
        row_max, row_sum, weighted = running
        key_piece, value_piece = block_pair
        scores = (
            jnp.einsum("cqhd,ckhd->chqk", queries, key_piece, preferred_element_type=jnp.float32)
            * score_scale
        )
        next_max = jnp.maximum(row_max, jnp.max(scores, axis=-1))
        factor = jnp.exp(row_max - next_max)
        weights_now = jnp.exp(scores - next_max[..., None])
        row_sum = row_sum * factor + jnp.sum(weights_now, axis=-1)
        weighted = weighted * factor[..., None] + jnp.einsum(
            "chqk,ckhd->chqd",
            weights_now.astype(jnp.bfloat16),
            value_piece,
            preferred_element_type=jnp.float32,
        )
        return ((next_max, row_sum, weighted), None)

    initial = (
        jnp.full((clip_count, heads_local, row_count), NEG_LARGE, jnp.float32),
        jnp.zeros((clip_count, heads_local, row_count), jnp.float32),
        jnp.zeros((clip_count, heads_local, row_count, HEAD_DIM), jnp.float32),
    )
    running = initial
    pieces = (
        lax.all_gather(key_flat, "ctx", axis=1, tiled=True),
        lax.all_gather(value_flat, "ctx", axis=1, tiled=True),
    )
    piece_rows = pieces[0].shape[1]
    block_size = math.gcd(piece_rows, 512)
    block_count = piece_rows // block_size
    key_blocks = jnp.moveaxis(
        pieces[0].reshape(clip_count, block_count, block_size, heads_local, HEAD_DIM), 1, 0
    )
    value_blocks = jnp.moveaxis(
        pieces[1].reshape(clip_count, block_count, block_size, heads_local, HEAD_DIM), 1, 0
    )
    running, unused = lax.scan(absorb_block, running, (key_blocks, value_blocks))
    row_max, row_sum, weighted = running
    log_total = row_max + jnp.log(row_sum)
    mixed_heads = jnp.transpose(weighted / row_sum[..., None], (0, 2, 1, 3))
    mixed_low = mixed_heads.reshape(clip_count, row_count, width_local).astype(jnp.bfloat16)
    branch = tensor_sum(
        jnp.einsum("csh,hd->csd", mixed_low, w_out_all, preferred_element_type=jnp.float32)
    )
    middle = inputs.astype(jnp.float32) + branch + b_out
    middle_all = lax.all_gather(middle.astype(jnp.bfloat16), "tp", axis=2, tiled=True).astype(
        middle.dtype
    )
    second, scaled_two, inv_two = normalize(middle_all, gain_two, shift_two)
    second_low = second.astype(jnp.bfloat16)
    inner_pre = (
        jnp.einsum("csd,df->csf", second_low, w_in_all, preferred_element_type=jnp.float32) + b_in
    )
    active_low = jax.nn.gelu(inner_pre, approximate=False).astype(jnp.bfloat16)
    return {
        "normed_low": normed_low,
        "scaled_one": scaled_one,
        "inv_one": inv_one,
        "queries": queries,
        "key_flat": key_flat,
        "value_flat": value_flat,
        "mixed_heads": mixed_heads,
        "mixed_low": mixed_low,
        "log_total": log_total,
        "middle": middle,
        "scaled_two": scaled_two,
        "inv_two": inv_two,
        "second_low": second_low,
        "inner_pre": inner_pre,
        "active_low": active_low,
    }


def per_device(
    inputs,
    ln1_gain,
    ln1_bias,
    w_qkv,
    b_qkv,
    w_out,
    b_out,
    ln2_gain,
    ln2_bias,
    w_in,
    b_in,
    w_back,
    b_back,
    cotangent,
):
    params = tuple(
        (
            parameter.astype(jnp.float32)
            for parameter in (ln1_gain, ln1_bias, b_qkv, b_out, ln2_gain, ln2_bias, b_in, b_back)
        )
    )
    gain_one = params[0]
    gain_two = params[4]
    clip_count, row_count, width_local = inputs.shape
    heads_local = width_local // HEAD_DIM
    score_scale = HEAD_DIM ** (-0.5)
    tp_index = lax.axis_index("tp")
    share_start = tp_index * width_local
    cosines, sine_table = rotary_tables(lax.axis_index("ctx") * row_count, row_count)
    cosines = cosines[:, None, :]
    sine_table = sine_table[:, None, :]
    weights = fetch_weights(w_qkv, w_out, w_in, w_back)
    stored_acts = forward(inputs, params, weights, cosines, sine_table)
    output = (
        stored_acts["middle"]
        + tensor_sum(
            jnp.einsum(
                "csf,fd->csd",
                stored_acts["active_low"],
                weights[3],
                preferred_element_type=jnp.float32,
            )
        )
        + params[7]
    ).astype(jnp.bfloat16)
    weights = fetch_weights(w_qkv, w_out, w_in, w_back)
    stored_acts = forward(inputs, params, weights, cosines, sine_table)
    w_qkv_all, w_out_all, w_in_all, w_back_all = weights
    grad_low = tp_rows(cotangent)
    grad_full = grad_low.astype(jnp.float32)
    grad_active = jnp.einsum(
        "csd,fd->csf", grad_low, w_back_all, preferred_element_type=jnp.float32
    )
    unused, gelu_back = jax.vjp(
        lambda argument: jax.nn.gelu(argument, approximate=False), stored_acts["inner_pre"]
    )
    grad_inner = gelu_back(grad_active)[0].astype(jnp.bfloat16)
    grad_w_back = jnp.einsum(
        "csf,csd->fd", stored_acts["active_low"], grad_low, preferred_element_type=jnp.float32
    )
    grad_b_back = jnp.sum(cotangent.astype(jnp.float32), axis=(0, 1))
    grad_w_in = jnp.einsum(
        "csd,csf->df", stored_acts["second_low"], grad_inner, preferred_element_type=jnp.float32
    )
    grad_b_in = jnp.sum(grad_inner.astype(jnp.float32), axis=(0, 1))
    grad_second = back_total(
        jnp.einsum("csf,df->csd", grad_inner, w_in_all, preferred_element_type=jnp.float32)
    )
    grad_gain_two = jnp.sum(grad_second * stored_acts["scaled_two"], axis=(0, 1))
    grad_shift_two = jnp.sum(grad_second, axis=(0, 1))
    grad_middle = grad_full + norm_back(
        grad_second, stored_acts["scaled_two"], stored_acts["inv_two"], gain_two
    )
    grad_branch = grad_middle.astype(jnp.bfloat16)
    grad_b_out = lax.dynamic_slice_in_dim(
        jnp.sum(grad_branch.astype(jnp.float32), axis=(0, 1)), share_start, width_local
    )
    grad_w_out = jnp.einsum(
        "csh,csd->hd", stored_acts["mixed_low"], grad_branch, preferred_element_type=jnp.float32
    )
    grad_mixed = jnp.einsum(
        "csd,hd->csh", grad_branch, w_out_all, preferred_element_type=jnp.float32
    ).astype(jnp.bfloat16)
    key_all, value_all = (
        lax.all_gather(stored_acts["key_flat"], "ctx", axis=1, tiled=True),
        lax.all_gather(stored_acts["value_flat"], "ctx", axis=1, tiled=True),
    )
    length = key_all.shape[1]
    block_size = math.gcd(length, 512)
    block_count = length // block_size
    grad_heads = grad_mixed.reshape(clip_count, row_count, heads_local, HEAD_DIM)
    queries = stored_acts["queries"]
    log_total = stored_acts["log_total"]
    row_delta = jnp.einsum(
        "cqhd,chqd->chq",
        grad_heads.astype(jnp.float32),
        jnp.transpose(stored_acts["mixed_heads"], (0, 2, 1, 3)),
    )
    key_blocks = jnp.moveaxis(
        key_all.reshape(clip_count, block_count, block_size, heads_local, HEAD_DIM), 1, 0
    )
    value_blocks = jnp.moveaxis(
        value_all.reshape(clip_count, block_count, block_size, heads_local, HEAD_DIM), 1, 0
    )

    def key_step(grad_query, block_pair):
        key_piece, value_piece = block_pair
        scores = (
            jnp.einsum("cqhd,ckhd->chqk", queries, key_piece, preferred_element_type=jnp.float32)
            * score_scale
        )
        prob_block = jnp.exp(scores - log_total[..., None])
        grad_probs = jnp.einsum(
            "cqhd,ckhd->chqk", grad_heads, value_piece, preferred_element_type=jnp.float32
        )
        grad_scores = (prob_block * (grad_probs - row_delta[..., None])).astype(jnp.bfloat16)
        grad_query = grad_query + jnp.einsum(
            "chqk,ckhd->cqhd", grad_scores, key_piece, preferred_element_type=jnp.float32
        )
        grad_key = (
            jnp.einsum("chqk,cqhd->ckhd", grad_scores, queries, preferred_element_type=jnp.float32)
            * score_scale
        )
        grad_value = jnp.einsum(
            "chqk,cqhd->ckhd",
            prob_block.astype(jnp.bfloat16),
            grad_heads,
            preferred_element_type=jnp.float32,
        )
        return (grad_query, (grad_key, grad_value))

    grad_query, (key_terms, value_terms) = lax.scan(
        key_step,
        jnp.zeros((clip_count, row_count, heads_local, HEAD_DIM), jnp.float32),
        (key_blocks, value_blocks),
    )
    grad_query = grad_query * score_scale
    key_terms = jnp.moveaxis(key_terms, 0, 1).reshape(clip_count, length, width_local)
    value_terms = jnp.moveaxis(value_terms, 0, 1).reshape(clip_count, length, width_local)
    grad_keys, grad_values = (
        lax.psum_scatter(
            key_terms.astype(jnp.bfloat16), "ctx", scatter_dimension=1, tiled=True
        ).astype(jnp.float32),
        lax.psum_scatter(
            value_terms.astype(jnp.bfloat16), "ctx", scatter_dimension=1, tiled=True
        ).astype(jnp.float32),
    )
    grad_q_pre = rotate_back(grad_query, cosines, sine_table).reshape(
        clip_count, row_count, width_local
    )
    grad_k_pre = rotate_back(
        grad_keys.reshape(clip_count, row_count, heads_local, HEAD_DIM), cosines, sine_table
    ).reshape(clip_count, row_count, width_local)
    grad_joined = jnp.stack([grad_q_pre, grad_k_pre, grad_values], axis=2).astype(jnp.bfloat16)
    grad_w_qkv = jnp.einsum(
        "csd,cskh->dkh", stored_acts["normed_low"], grad_joined, preferred_element_type=jnp.float32
    )
    grad_b_qkv = jnp.sum(grad_joined.astype(jnp.float32), axis=(0, 1))
    normed_term = jnp.einsum(
        "cskh,dkh->csd", grad_joined, w_qkv_all, preferred_element_type=jnp.float32
    )
    grad_normed = back_total(normed_term)
    grad_gain_one = jnp.sum(grad_normed * stored_acts["scaled_one"], axis=(0, 1))
    grad_shift_one = jnp.sum(grad_normed, axis=(0, 1))
    grad_tokens = grad_middle + norm_back(
        grad_normed, stored_acts["scaled_one"], stored_acts["inv_one"], gain_one
    )
    input_grad = lax.dynamic_slice_in_dim(grad_tokens, share_start, width_local, axis=2)
    summed = (
        lax.psum(grad_w_qkv.astype(jnp.bfloat16), "ctx").astype(jnp.float32),
        lax.psum(grad_w_out.astype(jnp.bfloat16), "ctx").astype(jnp.float32),
        lax.psum(grad_w_in.astype(jnp.bfloat16), "ctx").astype(jnp.float32),
        lax.psum(grad_w_back.astype(jnp.bfloat16), "ctx").astype(jnp.float32),
    )
    owned_grads = (
        lax.psum_scatter(
            summed[0].astype(jnp.bfloat16), "shard", scatter_dimension=0, tiled=True
        ).astype(jnp.float32),
        lax.psum_scatter(
            summed[1].astype(jnp.bfloat16), "shard", scatter_dimension=1, tiled=True
        ).astype(jnp.float32),
        lax.psum_scatter(
            summed[2].astype(jnp.bfloat16), "shard", scatter_dimension=0, tiled=True
        ).astype(jnp.float32),
        lax.psum_scatter(
            summed[3].astype(jnp.bfloat16), "shard", scatter_dimension=1, tiled=True
        ).astype(jnp.float32),
    )
    small_sums = lax.psum(
        (
            grad_gain_one,
            grad_shift_one,
            grad_b_qkv,
            grad_b_out,
            grad_gain_two,
            grad_shift_two,
            grad_b_in,
            grad_b_back,
        ),
        ("shard", "ctx"),
    )
    return (
        output,
        input_grad,
        small_sums[0],
        small_sums[1],
        owned_grads[0],
        small_sums[2],
        owned_grads[1],
        small_sums[3],
        small_sums[4],
        small_sums[5],
        owned_grads[2],
        small_sums[6],
        owned_grads[3],
        small_sums[7],
    )


def solution(mesh):
    placed = (
        P("shard", "ctx", "tp"),
        P(),
        P(),
        P("shard", None, "tp"),
        P(None, "tp"),
        P("tp", "shard"),
        P("tp"),
        P(),
        P(),
        P("shard", "tp"),
        P("tp"),
        P("tp", "shard"),
        P("tp"),
        P("shard", "ctx", "tp"),
    )
    return jax.shard_map(
        per_device,
        mesh=mesh,
        in_specs=placed,
        out_specs=(
            P("shard", "ctx", "tp"),
            P("shard", "ctx", "tp"),
            P(),
            P(),
            P("shard", None, "tp"),
            P(None, "tp"),
            P("tp", "shard"),
            P("tp"),
            P(),
            P(),
            P("shard", "tp"),
            P("tp"),
            P("tp", "shard"),
            P("tp"),
        ),
        check_vma=False,
    )
```

profile of v0, /device:TPU:8, one launch (start us, length us, event | category | flops | bytes accessed | tf_op | source)
XLA Modules:
  0.0 1377.3 jit_solution(10347059148901216098)
XLA Ops:
  12.4 31.5 %all-gather.10.cloned.1.call-done = bf16[2,512,1024]{2,1,0:T(8,128)(2,1)} async-done(((bf16[2,512,512]{2,1,0:T(8,128)(2,1)}), bf16[2,512,1024]{2,1,0:T(8,128)(2,1)}) %all-gather.10.cloned.1.call-update) | async-done | bytes 2097168 | tf_op jit(solution)/shard_map/all_gather | solution.py:78
  48.3 58.2 %all-gather.12.cloned.1.call-done = bf16[1024,3,512]{0,2,1:T(8,128)(2,1)} async-done(((bf16[256,3,512]{0,2,1:T(8,128)(2,1)}), bf16[1024,3,512]{0,2,1:T(8,128)(2,1)}) %all-gather.12.cloned.1.call-update) | async-done | bytes 3145744 | tf_op jit(solution)/shard_map/all_gather | solution.py:93
  106.5 5.6 broadcast_add_fusion
  119.3 5.2 slice_bitcast_fusion
  134.8 22.7 %concatenate.18 = f32[2,512,8,64]{1,3,2,0:T(8,128)} concatenate(f32[2,512,8,10]{1,3,2,0:T(8,128)} %get-tuple-element.305, f32[2,512,8,10]{1,3,2,0:T(8,128)} %get-tuple-element.306, f32[2,512,8,10]{1,3,2,0:T(8,128)} %get-tuple-element.307, f32[2,512,8,10]{1,3,2,0:T(8,128)} %get-tuple-element.308, f32[2,512,8,10]{1,3,2,0:T(8,128)} %get-tuple-element.309, ...), dimensions={3} | concatenate | bytes 4194304 | tf_op jit(solution)/shard_map/concatenate | solution.py:51
  166.1 22.7 %concatenate.20 = f32[2,512,8,64]{1,3,2,0:T(8,128)} concatenate(f32[2,512,8,10]{1,3,2,0:T(8,128)} %get-tuple-element.287, f32[2,512,8,10]{1,3,2,0:T(8,128)} %get-tuple-element.286, f32[2,512,8,10]{1,3,2,0:T(8,128)} %get-tuple-element.285, f32[2,512,8,10]{1,3,2,0:T(8,128)} %get-tuple-element.284, f32[2,512,8,10]{1,3,2,0:T(8,128)} %get-tuple-element.283, ...), dimensions={3} | concatenate | bytes 4194304 | tf_op jit(solution)/shard_map/concatenate | solution.py:51
  191.6 7.8 reshape.426
  204.6 6.3 copy.54
  210.9 7.9 reshape.425
  218.8 5.2 copy.56
  223.9 103.7 %while.36 = (s32[]{:T(128)}, f32[2,8,512]{2,1,0:T(8,128)S(1)}, f32[2,8,512]{2,1,0:T(8,128)S(1)}, f32[2,8,512,64]{2,3,1,0:T(8,128)S(1)}, bf16[4,2,512,8,64]{2,4,3...) while((s32[]{:T(128)}, f32[2,8,512]{2,1,0:T(8,128)S(1)}, ...), condition=%wide.region_5.6_spmd.clone, body=%wide.region_2.5_spmd.clone.sunk | while | flops 1108910080 | bytes 58196084 | solution.py:158
  223.9 9.4 bitcast_reduce_fusion.2
  233.3 8.6 fusion.152
  242.0 7.8 fusion.154
  249.8 9.4 bitcast_reduce_fusion.2
  259.2 8.6 fusion.152
  267.8 7.9 fusion.154
  275.7 9.4 bitcast_reduce_fusion.2
  285.1 8.6 fusion.152
  293.7 7.8 fusion.154
  301.6 9.4 bitcast_reduce_fusion.2
  311.0 8.6 fusion.152
  319.6 7.8 fusion.154
  333.5 33.1 %reduce-scatter.9.cloned.1.call-done = bf16[2,512,512]{2,1,0:T(8,128)(2,1)} async-done(((bf16[2,512,1024]{2,1,0:T(8,128)(2,1)}), bf16[2,512,512]{2,1,0:T(8,128)(2,1)}) %reduce-scatter.9.cloned.1.call-update) | async-done | bytes 1048592 | tf_op jit(solution)/shard_map/reduce_scatter | solution.py:82
  371.6 31.1 %all-gather.20.cloned.1.call-done = bf16[2,512,1024]{2,1,0:T(8,128)(2,1)} async-done(((bf16[2,512,512]{2,1,0:T(8,128)(2,1)}), bf16[2,512,1024]{2,1,0:T(8,128)(2,1)}) %all-gather.20.cloned.1.call-update) | async-done | bytes 2097168 | tf_op jit(solution)/shard_map/all_gather | solution.py:167
  407.1 75.4 %all-gather.22.cloned.1.call-done = bf16[1024,2048]{1,0:T(8,128)(2,1)} async-done(((bf16[256,2048]{1,0:T(8,128)(2,1)}), bf16[1024,2048]{1,0:T(8,128)(2,1)}) %all-gather.22.cloned.1.call-update) | async-done | bytes 4194320 | tf_op jit(solution)/shard_map/all_gather | solution.py:95
  482.5 9.1 fusion.80
  495.2 20.9 %multiply_convert_fusion.1 = (bf16[2,512,2048]{2,1,0:T(8,128)(2,1)}, f32[2,512,2048]{2,1,0:T(8,128)}) fusion(f32[2,512,2048]{2,1,0:T(8,128)S(1)} %get-tuple-element.298, f32[2048]{0:T(1024)S(1)} %convert_element_type.234, u8[512,2048]{1,0:T(8,128)(4,1)S(1)} %get-tuple-element.202, u8[512,2048]{1,0:T(8,128)(4,1)S(1)} %get-tuple-element.201), kind=kLoop, calls=%fused_computation.53 | loop fusion | flops 148897792 | bytes 23076864 | tf_op jit(solution)/shard_map/convert_element_type | solution.py:175
  518.4 79.1 %all-gather.24.cloned.1.call-done = bf16[2048,1024]{1,0:T(8,128)(2,1)} async-done(((bf16[2048,256]{1,0:T(8,128)(2,1)}), bf16[2048,1024]{1,0:T(8,128)(2,1)}) %all-gather.24.cloned.1.call-update) | async-done | bytes 4194320 | tf_op jit(solution)/shard_map/all_gather | solution.py:96
  597.5 14.0 %convert_reduce_fusion = (f32[2048]{0:T(1024)}, bf16[2,512,2048]{2,1,0:T(8,128)(2,1)S(1)}) fusion(f32[2,512,2048]{2,1,0:T(8,128)} %get-tuple-element.262, bf16[2,512,1024]{2,1,0:T(8,128)(2,1)} %all-gather.26.cloned.1.call-done, bf16[2048,1024]{1,0:T(8,128)(2,1)} %all-gather.24.cloned.1.call-done, f32[2,512,2048]{2,1,0:T(8,128)} %copy-done.16, ...), kind=kOutput, calls=%fused_computation.51 | convolution fusion | flops 4330616832 | bytes 27279360 | tf_op jit(solution)/shard_map/csd,fd->csf/dot_general | solution.py:246
  613.6 5.7 fusion.83
  619.4 64.2 %all-reduce.6.cloned.1.call-done = bf16[2,512,1024]{2,1,0:T(8,128)(2,1)} async-done(((bf16[2,512,1024]{2,1,0:T(8,128)(2,1)}), bf16[2,512,1024]{2,1,0:T(8,128)(2,1)}) %all-reduce.6.cloned.1.call-update) | async-done | bytes 2097168 | tf_op jit(solution)/shard_map/psum | solution.py:88
  692.9 131.3 %while.37 = (s32[]{:T(128)}, f32[2,512,8,64]{1,3,2,0:T(8,128)}, bf16[4,2,512,8,64]{2,4,3,1,0:T(8,128)(2,1)}, bf16[4,2,512,8,64]{2,4,3,1,0:T(8,128)(2,1)}, bf16[4...) while((s32[]{:T(128)}, f32[2,512,8,64]{1,3,2,0:T(8,128)}, ...), condition=%wide.region_14.15_spmd.clone, body=%wide.region_13.14_spmd.clone.sunk | while | flops 2719481856 | bytes 108101848 | solution.py:327
  692.9 9.3 fusion.165
  702.2 8.5 bitcast_dynamic-update-slice_fusion.5
  710.7 8.5 multiply_convert_fusion.3
  725.7 9.3 fusion.165
  735.1 8.5 bitcast_dynamic-update-slice_fusion.5
  743.6 8.5 multiply_convert_fusion.3
  758.6 9.3 fusion.165
  767.9 8.5 bitcast_dynamic-update-slice_fusion.5
  776.4 8.5 multiply_convert_fusion.3
  791.4 9.3 fusion.165
  800.7 8.5 bitcast_dynamic-update-slice_fusion.5
  809.2 8.5 multiply_convert_fusion.3
  824.2 10.2 copy.88
  834.4 11.8 reshape.444
  846.4 10.4 copy.89
  856.7 11.9 reshape.445
  874.4 8.5 bitcast_convert_fusion
  884.5 8.9 bitcast_convert_fusion.1
  896.7 21.9 %concatenate.21 = f32[2,512,8,64]{1,3,2,0:T(8,128)} concatenate(f32[2,512,8,10]{1,3,2,0:T(8,128)} %get-tuple-element.275, f32[2,512,8,10]{1,3,2,0:T(8,128)} %get-tuple-element.274, f32[2,512,8,10]{1,3,2,0:T(8,128)} %get-tuple-element.273, f32[2,512,8,10]{1,3,2,0:T(8,128)} %get-tuple-element.272, f32[2,512,8,10]{1,3,2,0:T(8,128)S(1)} %get-tuple-element.271, ...), dimensions={3} | concatenate | bytes 4194304 | tf_op jit(solution)/shard_map/concatenate | solution.py:51
  925.2 21.0 %concatenate.22 = f32[2,512,8,64]{1,3,2,0:T(8,128)} concatenate(f32[2,512,8,10]{1,3,2,0:T(8,128)} %get-tuple-element.281, f32[2,512,8,10]{1,3,2,0:T(8,128)} %get-tuple-element.280, f32[2,512,8,10]{1,3,2,0:T(8,128)S(1)} %get-tuple-element.279, f32[2,512,8,10]{1,3,2,0:T(8,128)S(1)} %get-tuple-element.278, f32[2,512,8,10]{1,3,2,0:T(8,128)S(1)} %get-tuple-element.277, ...), dimensions={3} | concatenate | bytes 4194304 | tf_op jit(solution)/shard_map/concatenate | solution.py:51
  952.7 7.3 bitcast_convert_fusion.2
  960.1 9.4 fusion.86
  969.9 7.3 bitcast_convert_fusion.3
  978.8 67.0 %reduce-scatter.23.cloned.1.call-done = bf16[2048,256]{1,0:T(8,128)(2,1)} async-done(((bf16[2048,1024]{1,0:T(8,128)(2,1)}), bf16[2048,256]{1,0:T(8,128)(2,1)}) %reduce-scatter.23.cloned.1.call-update) | async-done | bytes 1048592 | tf_op jit(solution)/shard_map/reduce_scatter | solution.py:380
  1045.8 79.5 %reduce-scatter.21.cloned.1.call-done = bf16[256,2048]{1,0:T(8,128)(2,1)} async-done(((bf16[1024,2048]{1,0:T(8,128)(2,1)}), bf16[256,2048]{1,0:T(8,128)(2,1)}) %reduce-scatter.21.cloned.1.call-update) | async-done | bytes 1048592 | tf_op jit(solution)/shard_map/reduce_scatter | solution.py:377
  1125.2 62.6 %reduce-scatter.17.cloned.1.call-done = bf16[256,3,512]{2,0,1:T(8,128)(2,1)} async-done(((bf16[1024,3,512]{2,0,1:T(8,128)(2,1)}), bf16[256,3,512]{2,0,1:T(8,128)(2,1)}) %reduce-scatter.17.cloned.1.call-update) | async-done | bytes 786448 | tf_op jit(solution)/shard_map/reduce_scatter | solution.py:371
  1187.8 35.1 %reduce-scatter.11.cloned.1.call-done = bf16[2,512,512]{2,1,0:T(8,128)(2,1)} async-done(((bf16[2,512,1024]{2,1,0:T(8,128)(2,1)}), bf16[2,512,512]{2,1,0:T(8,128)(2,1)}) %reduce-scatter.11.cloned.1.call-update) | async-done | bytes 1048592 | tf_op jit(solution)/shard_map/reduce_scatter | solution.py:82
  1226.7 62.1 %all-reduce.8.cloned.1.call-done = bf16[2,512,1024]{2,1,0:T(8,128)(2,1)} async-done(((bf16[2,512,1024]{2,1,0:T(8,128)(2,1)}), bf16[2,512,1024]{2,1,0:T(8,128)(2,1)}) %all-reduce.8.cloned.1.call-update) | async-done | bytes 2097168 | tf_op jit(solution)/shard_map/psum | solution.py:88
  1288.8 5.7 fusion.61
  1294.5 54.4 %all-reduce = (f32[1024]{0:T(1024)}, f32[1024]{0:T(1024)}, f32[3,512]{1,0:T(4,128)}, f32[512]{0:T(512)}, f32[1024]{0:T(1024)}, /*index=5*/f32[1024]{0:T(1024)}, f32[2048]{0:T(1024)}, f32[512]{0:T(512)}) all-reduce(f32[1024]{0:T(1024)S(1)} %get-tuple-element.205, ...), channel_id=1, replica_groups=mesh['shard'=4,'ctx'=4,'tp'=2] {'shard','ctx'}, use_global_device_ids=true, to_apply=%region_21.22 | all-reduce | flops 8704 | bytes 69632 | tf_op jit(solution)/shard_map/psum | solution.py:384
  1353.6 7.8 all-reduce.10.cloned.1.call-done
  (273 shorter events, 144.5 us)
Async XLA Ops:
  7.2 36.7 %all-gather.10.cloned.1.call-start = ((), (), s32[]{:S(2)}) async-start(), calls=%async_computation.8 | async-start | bytes 3145728 | tf_op jit(solution)/shard_map/all_gather | solution.py:78
  7.9 98.6 %all-gather.12.cloned.1.call-start = ((), (), s32[]{:S(2)}) async-start(), calls=%async_computation.9 | async-start | bytes 3932160 | tf_op jit(solution)/shard_map/all_gather | solution.py:93
  10.3 181.3 %all-gather.16.cloned.1.call-start = ((), (), s32[]{:S(2)}) async-start(), calls=%async_computation.11 | async-start | bytes 5242880 | tf_op jit(solution)/shard_map/all_gather | solution.py:147
  11.0 101.1 %copy-start.43 = (f32[1024]{0:T(1024)}, f32[1024]{0:T(1024)S(1)}, u32[]{:S(2)}) copy-start(f32[1024]{0:T(1024)S(1)} %convert_element_type.214) | copy-start | bytes 12292
  11.7 100.4 %copy-start.50 = (f32[1024]{0:T(1024)}, f32[1024]{0:T(1024)S(1)}, u32[]{:S(2)}) copy-start(f32[1024]{0:T(1024)S(1)} %convert_element_type.215) | copy-start | bytes 12292
  43.9 62.6 %copy-start.8 = (bf16[2,512,1024]{2,1,0:T(8,128)(2,1)S(1)}, bf16[2,512,1024]{2,1,0:T(8,128)(2,1)}, u32[]{:S(2)}) copy-start(bf16[2,512,1024]{2,1,0:T(8,128)(2,1)} %all-gather.10.cloned.1.call-done) | copy-start | bytes 6291460
  46.0 66.1 %copy-start.35 = (f32[2,512]{1,0:T(2,128)}, f32[2,512]{1,0:T(2,128)S(1)}, u32[]{:S(2)}) copy-start(f32[2,512]{1,0:T(2,128)S(1)} %broadcast_multiply_fusion.9) | copy-start | bytes 12292
  48.3 63.8 %copy-start.33 = (f32[2,512]{1,0:T(2,128)}, f32[2,512]{1,0:T(2,128)S(1)}, u32[]{:S(2)}) copy-start(f32[2,512]{1,0:T(2,128)S(1)} %add_rsqrt_fusion.1) | copy-start | bytes 12292
  115.9 88.7 %all-gather.14.cloned.1.call-start = ((), (), s32[]{:S(2)}) async-start(), calls=%async_computation.10 | async-start | bytes 5242880 | tf_op jit(solution)/shard_map/all_gather | solution.py:146
  117.4 71.4 %copy-start.21 = (f32[512,64]{0,1:T(8,128)}, f32[512,64]{0,1:T(8,128)S(1)}, u32[]{:S(2)}) copy-start(f32[512,64]{0,1:T(8,128)S(1)} %get-tuple-element.295) | copy-start | bytes 393220
  117.8 42.5 %copy-start.11 = (f32[512,512]{1,0:T(8,128)}, f32[512,512]{1,0:T(8,128)S(1)}, u32[]{:S(2)}) copy-start(f32[512,512]{1,0:T(8,128)S(1)} %copy.50) | copy-start | bytes 3145732
  124.5 10.3 copy-start.10
  134.8 25.6 %copy-start.15 = (f32[2,512,512]{2,1,0:T(8,128)S(1)}, f32[2,512,512]{2,1,0:T(8,128)}, u32[]{:S(2)}) copy-start(f32[2,512,512]{2,1,0:T(8,128)} %copy.51) | copy-start | bytes 6291460
  164.0 165.2 %all-gather.18.cloned.1.call-start = ((), (), s32[]{:S(2)}) async-start(), calls=%async_computation.12 | async-start | bytes 1310720 | tf_op jit(solution)/shard_map/all_gather | solution.py:94
  164.6 202.0 %reduce-scatter.9.cloned.1.call-start = ((), (), s32[]{:S(2)}) async-start(), calls=%async_computation.13 | async-start | bytes 3145728 | tf_op jit(solution)/shard_map/reduce_scatter | solution.py:82
  327.7 5.7 copy-start.3
  333.3 38.2 %copy-start.54 = (bf16[1024]{0:T(1024)(128)(2,1)S(1)}, bf16[1024]{0:T(1024)(128)(2,1)}, u32[]{:S(2)}) copy-start(bf16[1024]{0:T(1024)(128)(2,1)} %param.25) | copy-start | bytes 6148
  333.4 38.2 %copy-start.55 = (bf16[1024]{0:T(1024)(128)(2,1)S(1)}, bf16[1024]{0:T(1024)(128)(2,1)}, u32[]{:S(2)}) copy-start(bf16[1024]{0:T(1024)(128)(2,1)} %param.26) | copy-start | bytes 6148
  333.4 38.2 %copy-start.49 = (bf16[2048]{0:T(1024)(128)(2,1)S(1)}, bf16[2048]{0:T(1024)(128)(2,1)}, u32[]{:S(2)}) copy-start(bf16[2048]{0:T(1024)(128)(2,1)} %param.28) | copy-start | bytes 12292
  333.4 69.3 %all-gather.20.cloned.1.call-start = ((), (), s32[]{:S(2)}) async-start(), calls=%async_computation.14 | async-start | bytes 3145728 | tf_op jit(solution)/shard_map/all_gather | solution.py:167
  333.5 38.2 %copy-start.41 = (f32[512]{0:T(512)}, f32[512]{0:T(512)S(1)}, u32[]{:S(2)}) copy-start(f32[512]{0:T(512)S(1)} %convert_element_type.228) | copy-start | bytes 6148
  369.4 113.1 %all-gather.22.cloned.1.call-start = ((), (), s32[]{:S(2)}) async-start(), calls=%async_computation.15 | async-start | bytes 5242880 | tf_op jit(solution)/shard_map/all_gather | solution.py:95
  370.2 148.3 %all-gather.26.cloned.1.call-start = ((), (), s32[]{:S(2)}) async-start(), calls=%async_computation.18 | async-start | bytes 3145728 | tf_op jit(solution)/shard_map/all_gather | solution.py:78
  370.9 226.6 %all-gather.24.cloned.1.call-start = ((), (), s32[]{:S(2)}) async-start(), calls=%async_computation.16 | async-start | bytes 5242880 | tf_op jit(solution)/shard_map/all_gather | solution.py:96
  371.5 312.1 %all-reduce.6.cloned.1.call-start = ((), (), s32[]{:S(2)}) async-start(), calls=%async_computation.19 | async-start | bytes 4194304 | tf_op jit(solution)/shard_map/psum | solution.py:88
  371.6 316.8 %copy-start.37 = (f32[1024]{0:T(1024)}, f32[1024]{0:T(1024)S(1)}, u32[]{:S(2)}) copy-start(f32[1024]{0:T(1024)S(1)} %convert_element_type.231) | copy-start | bytes 12292
  371.6 120.0 %copy-start.52 = (f32[1024]{0:T(1024)}, f32[1024]{0:T(1024)S(1)}, u32[]{:S(2)}) copy-start(f32[1024]{0:T(1024)S(1)} %convert_element_type.232) | copy-start | bytes 12292
  402.7 79.8 %copy-start.5 = (bf16[2,512,1024]{2,1,0:T(8,128)(2,1)S(1)}, bf16[2,512,1024]{2,1,0:T(8,128)(2,1)}, u32[]{:S(2)}) copy-start(bf16[2,512,1024]{2,1,0:T(8,128)(2,1)} %all-gather.20.cloned.1.call-done) | copy-start | bytes 6291460
  404.8 283.5 %copy-start.31 = (f32[2,512]{1,0:T(2,128)}, f32[2,512]{1,0:T(2,128)S(1)}, u32[]{:S(2)}) copy-start(f32[2,512]{1,0:T(2,128)S(1)} %broadcast_multiply_fusion.8) | copy-start | bytes 12292
  407.1 281.2 %copy-start.39 = (f32[2,512]{1,0:T(2,128)}, f32[2,512]{1,0:T(2,128)S(1)}, u32[]{:S(2)}) copy-start(f32[2,512]{1,0:T(2,128)S(1)} %add_rsqrt_fusion) | copy-start | bytes 12292
  597.5 16.0 %copy-start.58 = (bf16[1024,2048]{1,0:T(8,128)(2,1)S(1)}, bf16[1024,2048]{1,0:T(8,128)(2,1)}, u32[]{:S(2)}) copy-start(bf16[1024,2048]{1,0:T(8,128)(2,1)} %all-gather.22.cloned.1.call-done) | copy-start | bytes 12582916
  619.3 302.8 %reduce-scatter.13.cloned.1.call-start = ((), (), s32[]{:S(2)}) async-start(), calls=%async_computation.20 | async-start | bytes 5242880 | tf_op jit(solution)/shard_map/reduce_scatter | solution.py:336
  683.6 4.8 copy-start.17
  683.6 4.8 copy-start.23
  710.7 8.5 copy-start
  743.6 8.5 copy-start
  776.4 8.5 copy-start
  809.2 8.5 copy-start
  846.3 106.4 %reduce-scatter.15.cloned.1.call-start = ((), (), s32[]{:S(2)}) async-start(), calls=%async_computation.21 | async-start | bytes 5242880 | tf_op jit(solution)/shard_map/reduce_scatter | solution.py:339
  868.7 5.7 copy-start.24
  868.7 110.1 %reduce-scatter.19.cloned.1.call-start = ((), (), s32[]{:S(2)}) async-start(), calls=%async_computation.24 | async-start | bytes 1310720 | tf_op jit(solution)/shard_map/reduce_scatter | solution.py:374
  874.3 171.5 %reduce-scatter.23.cloned.1.call-start = ((), (), s32[]{:S(2)}) async-start(), calls=%async_computation.26 | async-start | bytes 5242880 | tf_op jit(solution)/shard_map/reduce_scatter | solution.py:380
  882.9 242.3 %reduce-scatter.21.cloned.1.call-start = ((), (), s32[]{:S(2)}) async-start(), calls=%async_computation.25 | async-start | bytes 5242880 | tf_op jit(solution)/shard_map/reduce_scatter | solution.py:377
  893.4 294.4 %reduce-scatter.17.cloned.1.call-start = ((), (), s32[]{:S(2)}) async-start(), calls=%async_computation.23 | async-start | bytes 3932160 | tf_op jit(solution)/shard_map/reduce_scatter | solution.py:371
  896.7 21.9 %copy-start.30 = (f32[512,64]{0,1:T(8,128)S(1)}, f32[512,64]{0,1:T(8,128)}, u32[]{:S(2)}) copy-start(f32[512,64]{0,1:T(8,128)} %get-tuple-element.296) | copy-start | bytes 393220
  918.6 5.0 copy-start.22
  925.2 24.2 %copy-start.12 = (f32[512,512]{1,0:T(8,128)S(1)}, f32[512,512]{1,0:T(8,128)}, u32[]{:S(2)}) copy-start(f32[512,512]{1,0:T(8,128)} %copy-done.11) | copy-start | bytes 3145732
  946.2 6.5 copy-start.9
  946.2 6.5 copy-start.34
  946.2 6.5 copy-start.36
  946.2 6.5 copy-start.44
  946.2 6.5 copy-start.51
  960.1 9.8 copy-start.18
  960.1 262.9 %reduce-scatter.11.cloned.1.call-start = ((), (), s32[]{:S(2)}) async-start(), calls=%async_computation.17 | async-start | bytes 3145728 | tf_op jit(solution)/shard_map/reduce_scatter | solution.py:82
  969.5 7.7 copy-start.57
  969.5 9.2 copy-start.47
  969.5 319.2 %all-reduce.8.cloned.1.call-start = ((), (), s32[]{:S(2)}) async-start(), calls=%async_computation.22 | async-start | bytes 4194304 | tf_op jit(solution)/shard_map/psum | solution.py:88
  977.1 245.8 %copy-start.13 = (bf16[2,512,512]{2,1,0:T(8,128)(2,1)S(1)}, bf16[2,512,512]{2,1,0:T(8,128)(2,1)}, u32[]{:S(2)}) copy-start(bf16[2,512,512]{2,1,0:T(8,128)(2,1)} %param.18) | copy-start | bytes 3145732
  977.1 245.8 %copy-start.42 = (f32[512]{0:T(512)S(1)}, f32[512]{0:T(512)}, u32[]{:S(2)}) copy-start(f32[512]{0:T(512)} %copy-done.41) | copy-start | bytes 6148
  977.2 384.2 %all-reduce.10.cloned.1.call-start = ((), (), s32[]{:S(2)}) async-start(), calls=%async_computation.27 | async-start | bytes 6291456 | tf_op jit(solution)/shard_map/psum | solution.py:365
  1226.6 67.8 %copy-start.45 = (f32[1024]{0:T(1024)S(1)}, f32[1024]{0:T(1024)}, u32[]{:S(2)}) copy-start(f32[1024]{0:T(1024)} %get-tuple-element.203) | copy-start | bytes 12292
  1226.7 67.8 %copy-start.46 = (f32[1024]{0:T(1024)S(1)}, f32[1024]{0:T(1024)}, u32[]{:S(2)}) copy-start(f32[1024]{0:T(1024)} %get-tuple-element.209) | copy-start | bytes 12292
  1226.7 67.8 %copy-start.48 = (f32[2048]{0:T(1024)S(1)}, f32[2048]{0:T(1024)}, u32[]{:S(2)}) copy-start(f32[2048]{0:T(1024)} %get-tuple-element.301) | copy-start | bytes 24580
  1361.4 7.1 copy-start.27
  (22 other events, 56.2 us)
Sparse Core Ops, SparseCore 0:
  9.6 34.2 all-gather.9
  46.0 60.4 all-gather.11
  116.0 35.6 all-gather.15
  164.1 35.7 all-gather.13
  201.3 31.2 all-gather.17
  333.5 33.0 reduce-scatter.8
  369.5 33.1 all-gather.19
  404.3 78.1 all-gather.21
  484.1 34.2 all-gather.25
  519.9 77.5 all-gather.23
  619.4 64.0 all-reduce.5
  846.4 44.5 reduce-scatter.12
  893.7 44.5 reduce-scatter.14
  941.0 25.0 reduce-scatter.18
  968.3 77.4 reduce-scatter.22
  1047.9 77.2 reduce-scatter.20
  1127.5 60.2 reduce-scatter.16
  1190.6 32.3 reduce-scatter.10
  1225.8 62.8 all-reduce.7
  1291.4 69.9 all-reduce.9
where the time goes:
time: 1390 us; the launch traced here: 1380 us
  waiting for transfers between devices  692 us (50%)
  matrix products  286 us (21%)
  local copies, waits for them, and re-layouts  212 us (15%)
  other arithmetic  116 us (8%)
  blocking collectives  54.4 us (4%)
  between operations  15.5 us (1%)
    psum x2, waiting for transfers between devices, back_total(): return lax.psum(summand.astype(jnp.bfloat16), 'tp').astype(jnp.float32)  126 us
    concatenate x6, local copies, waits for them, and re-layouts, partner(): return jnp.concatenate(pieces, axis=-1)  94.2 us
    reduce_scatter x1, waiting for transfers between devices, per_device(): lax.psum_scatter(summed[2].astype(jnp.bfloat16), 'shard', scatter_dimensi...  79.5 us
    all_gather x1, waiting for transfers between devices, fetch_weights(): lax.all_gather(w_back, 'shard', axis=1, tiled=True)  79.1 us
    all_gather x1, waiting for transfers between devices, fetch_weights(): lax.all_gather(w_in, 'shard', axis=0, tiled=True)  75.4 us
    reduce_scatter x2, waiting for transfers between devices, tensor_sum(): lax.psum_scatter(summand.astype(jnp.bfloat16), 'tp', scatter_dimension=2,...  68.2 us
    reduce_scatter x1, waiting for transfers between devices, per_device(): lax.psum_scatter(summed[3].astype(jnp.bfloat16), 'shard', scatter_dimensi...  67 us
    reduce_scatter x1, waiting for transfers between devices, per_device(): lax.psum_scatter(summed[0].astype(jnp.bfloat16), 'shard', scatter_dimensi...  62.6 us
  transfers between devices with their start and end apart: 20, of which 14 were waited for; matrix products, arithmetic and copies ran while one was open for 29% of the time, Pallas kernels for 0%

commit v1 on v0

--- a/solution.py
+++ b/solution.py
@@ -1,8 +1,11 @@
+import functools
 import math
 
 import jax
 import jax.numpy as jnp
 from jax import lax
+from jax.experimental import pallas as pl
+from jax.experimental.pallas import tpu as pltpu
 from jax.sharding import PartitionSpec as P
 
 HEAD_DIM = 64
@@ -412,6 +415,763 @@
     )
 
 
+LOG2E = 1.4426950408889634
+BF = jnp.bfloat16
+F32 = jnp.float32
+VMEM_BYTES = 56 * 2**20
+
+
+def dot_nt(a, b):
+    return lax.dot_general(a, b, (((1,), (1,)), ((), ())), preferred_element_type=F32)
+
+
+def dot_nn(a, b):
+    return lax.dot_general(a, b, (((1,), (0,)), ((), ())), preferred_element_type=F32)
+
+
+def dot_tn(a, b):
+    return lax.dot_general(a, b, (((0,), (0,)), ((), ())), preferred_element_type=F32)
+
+
+def whole(shape):
+    return pl.BlockSpec(shape, lambda *_: (0,) * len(shape))
+
+
+SMEM = pl.BlockSpec(memory_space=pltpu.SMEM)
+
+
+def call(body, args, outs, name, scratch=(), flops=0, grid=None, in_specs=None, out_specs=None):
+    shapes = [jax.ShapeDtypeStruct(shape, kind) for shape, kind in outs]
+    moved = sum(a.size * a.dtype.itemsize for a in args)
+    moved += sum(math.prod(s.shape) * jnp.dtype(s.dtype).itemsize for s in shapes)
+    extra = {} if grid is None else {"grid": grid}
+    return pl.pallas_call(
+        body,
+        in_specs=in_specs or [SMEM] + [whole(a.shape) for a in args[1:]],
+        out_specs=out_specs or [whole(s.shape) for s in shapes],
+        out_shape=shapes,
+        scratch_shapes=list(scratch),
+        compiler_params=pltpu.CompilerParams(vmem_limit_bytes=VMEM_BYTES),
+        cost_estimate=pl.CostEstimate(
+            flops=int(flops), bytes_accessed=int(moved), transcendentals=0
+        ),
+        name=name,
+        **extra,
+    )(*args)
+
+
+def piece_index(ids_ref, half, part):
+    shard, tp = ids_ref[0], ids_ref[2]
+    return shard ^ (2 * (tp ^ half) + part)
+
+
+CHUNKS = ((0, 0), (0, 1), (1, 0), (1, 1))
+
+
+def partner_lanes(tensor):
+    segment = 2 * (HEAD_DIM // 3 // 2)
+    halfway = segment // 2
+    width = tensor.shape[1]
+    lane = lax.broadcasted_iota(jnp.int32, tensor.shape, 1) % HEAD_DIM
+    first = lane % segment < halfway
+    return jnp.where(
+        first, pltpu.roll(tensor, width - halfway, 1), pltpu.roll(tensor, halfway, 1)
+    )
+
+
+def norm_parts(own, other):
+    total = 2 * own.shape[1]
+    mean = (jnp.sum(own, 1, keepdims=True) + jnp.sum(other, 1, keepdims=True)) / total
+    own, other = own - mean, other - mean
+    spread = (
+        jnp.sum(own * own, 1, keepdims=True) + jnp.sum(other * other, 1, keepdims=True)
+    ) / total
+    inv = lax.rsqrt(spread + EPSILON)
+    return own * inv, other * inv, inv
+
+
+def qkv_body(ids_ref, *refs):
+    blocks, (w_ref, b_ref, ln_ref, cos_ref, sin_ref, n_ref, q_ref, k_ref, v_ref) = (
+        refs[:10],
+        refs[10:],
+    )
+    step = pl.program_id(0)
+    own = [blocks[m][...] for m in range(4)]
+    other = [
+        blocks[4][...],
+        blocks[5][...],
+        jnp.where(step == 0, blocks[6][...], blocks[7][...]),
+        jnp.where(step == 0, blocks[8][...], blocks[9][...]),
+    ]
+    half = own[0].shape[1]
+    width = half // 2
+    for m in range(4):
+        one, two, unused = norm_parts(own[m].astype(F32), other[m].astype(F32))
+        n_ref[m, :, :half] = (one * ln_ref[0:1, :half] + ln_ref[1:2, :half]).astype(BF)
+        n_ref[m, :, half:] = (two * ln_ref[0:1, half:] + ln_ref[1:2, half:]).astype(BF)
+    for m in range(4):
+        acc = b_ref[...]
+        for h, j in CHUNKS:
+            at = (2 * h + j) * width
+            acc = acc + dot_nn(n_ref[m, :, at : at + width], w_ref[piece_index(ids_ref, h, j)])
+        cosines, sines = cos_ref[m], sin_ref[m]
+        lanes = cosines.shape[1]
+        q, k = acc[:, :lanes], acc[:, lanes : 2 * lanes]
+        q_ref[m] = (q * cosines + partner_lanes(q) * sines).astype(BF)
+        k_ref[m] = (k * cosines + partner_lanes(k) * sines).astype(BF)
+        v_ref[m] = acc[:, 2 * lanes :].astype(BF)
+
+
+def qkv_call(ids, blocks, w, b, ln, cosines, sines):
+    rows, half = blocks[0].shape
+    lanes = cosines.shape[2]
+    block = rows // 2
+    row_spec = pl.BlockSpec((block, half), lambda i: (i, 0))
+    held = whole((block, half))
+    four = lambda cols: pl.BlockSpec((4, block, cols), lambda i: (0, i, 0))
+    args = [ids, *blocks, w, b, ln, cosines, sines]
+    return call(
+        qkv_body,
+        args,
+        [((4, rows, 2 * half), BF)] + [((4, rows, lanes), BF)] * 3,
+        "qkv",
+        grid=(2,),
+        in_specs=[SMEM]
+        + [row_spec] * 6
+        + [held] * 4
+        + [whole(w.shape), whole(b.shape), whole(ln.shape), four(lanes), four(lanes)],
+        out_specs=[four(2 * half), four(lanes), four(lanes), four(lanes)],
+        flops=2 * 4 * rows * 2 * half * 3 * lanes * 3,
+    )
+
+
+def attend_body(block, q_ref, k_ref, v_ref, o0, o1, o2, o3, ot_ref, lse_ref, vt_ref):
+    step = pl.program_id(0)
+    keys, width = k_ref.shape
+    rows = q_ref.shape[0]
+
+    @pl.when(step == 0)
+    def _():
+        vt_ref[:width, :] = v_ref[...].T
+        vt_ref[width:, :] = jnp.ones((vt_ref.shape[0] - width, keys), BF)
+
+    q = q_ref[...]
+    head = lax.broadcasted_iota(jnp.int32, (rows, width), 1) // HEAD_DIM
+    scale = HEAD_DIM ** (-0.5) * LOG2E
+    outs = []
+    for h in range(width // HEAD_DIM):
+        q_head = jnp.where(head == h, q, jnp.zeros_like(q))
+        top = None
+        for start in range(0, keys, block):
+            part = slice(start, start + block)
+            scores = dot_nt(k_ref[part, :], q_head)
+            latest = jnp.max(scores, axis=0, keepdims=True)
+            latest = latest if top is None else jnp.maximum(top, latest)
+            probs = jnp.exp2(scores * scale - latest * scale).astype(BF)
+            term = dot_nn(vt_ref[:, part], probs)
+            acc = term if top is None else acc * jnp.exp2((top - latest) * scale) + term
+            top = latest
+        total = acc[width : width + 1, :]
+        outs.append(acc[h * HEAD_DIM : (h + 1) * HEAD_DIM, :] / total)
+        lse_ref[h : h + 1, :] = top * scale + jnp.log2(total)
+    result = jnp.concatenate(outs, axis=0)
+    ot_ref[...] = result
+    low = result.T.astype(BF)
+
+    @pl.when(step == 0)
+    def _():
+        o0[...] = low[: rows // 2]
+        o1[...] = low[rows // 2 :]
+
+    @pl.when(step == 1)
+    def _():
+        o2[...] = low[: rows // 2]
+        o3[...] = low[rows // 2 :]
+
+
+def attend_call(q, k, v):
+    count, width = q.shape
+    rows = count // 2
+    heads = width // HEAD_DIM
+    piece = (count // 4, width)
+    return call(
+        functools.partial(attend_body, count),
+        [q, k, v],
+        [(piece, BF)] * 4 + [((width, count), F32), ((heads, count), F32)],
+        "attend",
+        scratch=[pltpu.VMEM((width + 16, count), BF)],
+        grid=(2,),
+        in_specs=[pl.BlockSpec((rows, width), lambda i: (i, 0)), whole(k.shape), whole(v.shape)],
+        out_specs=[whole(piece)] * 4
+        + [
+            pl.BlockSpec((width, rows), lambda i: (0, i)),
+            pl.BlockSpec((heads, rows), lambda i: (0, i)),
+        ],
+        flops=4 * count * count * 256 * heads,
+    )
+
+
+def block_body(ids_ref, *refs):
+    (x_ref, xp_ref, mo_ref, mp_ref, c_ref, cp_ref, ln_ref, bin_ref) = refs[:8]
+    wo, wi, wb = refs[8:12], refs[12:16], refs[16:20]
+    mid_ref, sec_ref, act_ref, gin_ref, out_own, out_other, gs_ref, sums_ref = refs[20:]
+    rows, half = x_ref.shape
+    width = half // 2
+    hidden = wi[0].shape[2]
+    ctx = ids_ref[1]
+    mixed = jnp.concatenate([mo_ref[...], mp_ref[...]], axis=1)
+    for h, j in CHUNKS:
+        k = piece_index(ids_ref, h, j)
+        at = (2 * h + j) * width
+        source = (x_ref, xp_ref)[h][:, j * width : (j + 1) * width].astype(F32)
+        weight = jnp.concatenate([wo[m][k, side] for side in range(2) for m in range(4)], axis=0)
+        mid_ref[:, at : at + width] = (
+            source + dot_nn(mixed, weight) + ln_ref[4:5, at : at + width]
+        )
+    one, two, unused = norm_parts(mid_ref[:, :half], mid_ref[:, half:])
+    sec_ref[:, :half] = (one * ln_ref[2:3, :half] + ln_ref[3:4, :half]).astype(BF)
+    sec_ref[:, half:] = (two * ln_ref[2:3, half:] + ln_ref[3:4, half:]).astype(BF)
+    for m in range(4):
+        at = m * hidden
+        inner = bin_ref[pl.ds(ctx ^ m, 1), :]
+        grad = None
+        for h, j in CHUNKS:
+            k = piece_index(ids_ref, h, j)
+            cols = slice((2 * h + j) * width, (2 * h + j + 1) * width)
+            inner = inner + dot_nn(sec_ref[:, cols], wi[m][k])
+            part = (c_ref, cp_ref)[h][:, j * width : (j + 1) * width]
+            term = dot_nt(part, wb[m][k])
+            grad = term if grad is None else grad + term
+        phi = 0.5 + 0.5 * lax.erf(inner * (0.5**0.5))
+        act_ref[:, at : at + hidden] = (inner * phi).astype(BF)
+        slope = phi + inner * (jnp.exp(-0.5 * inner * inner) * ((2 * math.pi) ** -0.5))
+        grad = (grad * slope).astype(BF)
+        gin_ref[:, at : at + hidden] = grad
+        sums_ref[0:1, at : at + hidden] = jnp.sum(grad.astype(F32), axis=0, keepdims=True)
+    for h, j in CHUNKS:
+        k = piece_index(ids_ref, h, j)
+        cols = slice((2 * h + j) * width, (2 * h + j + 1) * width)
+        back = None
+        out = None
+        for m in range(4):
+            wide = slice(m * hidden, (m + 1) * hidden)
+            term = dot_nt(gin_ref[:, wide], wi[m][k])
+            back = term if back is None else back + term
+            term = dot_nn(act_ref[:, wide], wb[m][k])
+            out = term if out is None else out + term
+        gs_ref[:, cols] = back.astype(BF)
+        (out_own, out_other)[h][:, j * width : (j + 1) * width] = out.astype(BF)
+
+
+def block_call(ids, x, xp, mo, mp, c, cp, ln, b_in, wo, wi, wb):
+    rows, half = x.shape
+    hidden = 4 * wi[0].shape[2]
+    return call(
+        block_body,
+        [ids, x, xp, mo, mp, c, cp, ln, b_in, *wo, *wi, *wb],
+        [
+            ((rows, 2 * half), F32),
+            ((rows, 2 * half), BF),
+            ((rows, hidden), BF),
+            ((rows, hidden), BF),
+            ((rows, half), BF),
+            ((rows, half), BF),
+            ((rows, 2 * half), BF),
+            ((1, hidden), F32),
+        ],
+        "block",
+        flops=2 * rows * 2 * half * (2 * half + 4 * hidden) * 2,
+    )
+
+
+def branch_body(ids_ref, gs_ref, gsp_ref, c_ref, cp_ref, mid_ref, ln_ref, *refs):
+    wo = refs[:4]
+    gmid_ref, gb_ref, m0, m1, m2, m3, sums_ref = refs[4:]
+    half = c_ref.shape[1]
+    width = half // 2
+    own_u, other_u, inv = norm_parts(mid_ref[:, :half], mid_ref[:, half:])
+    own = gs_ref[:, :half].astype(F32) + gsp_ref[:, half:].astype(F32)
+    other = gs_ref[:, half:].astype(F32) + gsp_ref[:, :half].astype(F32)
+    sums_ref[0:1, :half] = jnp.sum(own * own_u, 0, keepdims=True)
+    sums_ref[0:1, half:] = jnp.sum(other * other_u, 0, keepdims=True)
+    sums_ref[1:2, :half] = jnp.sum(own, 0, keepdims=True)
+    sums_ref[1:2, half:] = jnp.sum(other, 0, keepdims=True)
+    own = own * ln_ref[2:3, :half]
+    other = other * ln_ref[2:3, half:]
+    total = 2 * half
+    mean_one = (jnp.sum(own, 1, keepdims=True) + jnp.sum(other, 1, keepdims=True)) / total
+    mean_two = (
+        jnp.sum(own * own_u, 1, keepdims=True) + jnp.sum(other * other_u, 1, keepdims=True)
+    ) / total
+    cot = c_ref[...].astype(F32)
+    own = cot + inv * (own - mean_one - own_u * mean_two)
+    other = cp_ref[...].astype(F32) + inv * (other - mean_one - other_u * mean_two)
+    gmid_ref[...] = own
+    gb_ref[:, :half] = own.astype(BF)
+    gb_ref[:, half:] = other.astype(BF)
+    sums_ref[2:3, :half] = jnp.sum(own.astype(BF).astype(F32), 0, keepdims=True)
+    sums_ref[2:3, half:] = jnp.sum(cot, 0, keepdims=True)
+    mixed = None
+    for h, j in CHUNKS:
+        k = piece_index(ids_ref, h, j)
+        at = (2 * h + j) * width
+        weight = jnp.concatenate([wo[m][k, 0] for m in range(4)], axis=0)
+        term = dot_nt(gb_ref[:, at : at + width], weight)
+        mixed = term if mixed is None else mixed + term
+    mixed = mixed.astype(BF)
+    lanes = m0.shape[1]
+    for m, ref in enumerate((m0, m1, m2, m3)):
+        ref[...] = mixed[:, m * lanes : (m + 1) * lanes]
+
+
+def branch_call(ids, gs, gsp, c, cp, mid, ln, wo):
+    rows, half = c.shape
+    lanes = wo[0].shape[2]
+    return call(
+        branch_body,
+        [ids, gs, gsp, c, cp, mid, ln, *wo],
+        [((rows, half), F32), ((rows, 2 * half), BF)]
+        + [((rows, lanes), BF)] * 4
+        + [((3, 2 * half), F32)],
+        "branch",
+        flops=2 * rows * 2 * half * 4 * lanes * 3,
+    )
+
+
+def attend_back_body(rows, q_ref, k_ref, v_ref, d0, d1, d2, d3, ot_ref, lse_ref, *refs):
+    dq_ref, dk_ref, dv_ref, qh_ref, dh_ref, delta_ref, dqt_ref = refs
+    step = pl.program_id(0)
+    count, width = q_ref.shape
+    heads = width // HEAD_DIM
+    scale = HEAD_DIM ** (-0.5)
+
+    @pl.when(step == 0)
+    def _():
+        quarter = count // 4
+        head = lax.broadcasted_iota(jnp.int32, (quarter, width), 1) // HEAD_DIM
+        for m, d_ref in enumerate((d0, d1, d2, d3)):
+            part = slice(m * quarter, (m + 1) * quarter)
+            q, d = q_ref[part, :], d_ref[...]
+            for h in range(heads):
+                qh_ref[h, part, :] = jnp.where(head == h, q, jnp.zeros_like(q))
+                dh_ref[h, part, :] = jnp.where(head == h, d, jnp.zeros_like(d))
+            products = d.astype(F32).T * ot_ref[:, part]
+            for h in range(heads):
+                delta_ref[h : h + 1, part] = jnp.sum(
+                    products[h * HEAD_DIM : (h + 1) * HEAD_DIM], axis=0, keepdims=True
+                )
+        dqt_ref[...] = jnp.zeros_like(dqt_ref)
+
+    keys, values = k_ref[...], v_ref[...]
+    turned = keys.T
+    row = lax.broadcasted_iota(jnp.int32, turned.shape, 0) // HEAD_DIM
+    dk = dv = None
+    for h in range(heads):
+        turned_head = jnp.where(row == h, turned, jnp.zeros_like(turned))
+        for start in range(0, count, rows):
+            part = slice(start, start + rows)
+            q, d = qh_ref[h, part, :], dh_ref[h, part, :]
+            probs = jnp.exp2(dot_nt(keys, q) * (scale * LOG2E) - lse_ref[h : h + 1, part])
+            grad = (probs * (dot_nt(values, d) - delta_ref[h : h + 1, part])).astype(BF)
+            value_term, key_term = dot_nn(probs.astype(BF), d), dot_nn(grad, q)
+            dk = key_term if dk is None else dk + key_term
+            dv = value_term if dv is None else dv + value_term
+            dqt_ref[:, part] += dot_nn(turned_head, grad)
+    dk_ref[...] = dk * scale
+    dv_ref[...] = dv
+
+    @pl.when(step == pl.num_programs(0) - 1)
+    def _():
+        dq_ref[...] = (dqt_ref[...] * scale).T
+
+
+def attend_back_call(q, k, v, d, ot, lse):
+    count, width = q.shape
+    heads = width // HEAD_DIM
+    rows = 512
+    block = 512
+    part = pl.BlockSpec((block, width), lambda i: (i, 0))
+    return call(
+        functools.partial(attend_back_body, rows),
+        [q, k, v, *d, ot, lse],
+        [((count, width), F32)] * 3,
+        "attend_back",
+        scratch=[
+            pltpu.VMEM((heads, count, width), BF),
+            pltpu.VMEM((heads, count, width), BF),
+            pltpu.VMEM((heads, count), F32),
+            pltpu.VMEM((width, count), F32),
+        ],
+        grid=(count // block,),
+        in_specs=[whole(q.shape), part, part]
+        + [whole(d[0].shape)] * 4
+        + [whole(ot.shape), whole(lse.shape)],
+        out_specs=[whole(q.shape), part, part],
+        flops=10 * count * count * 256 * heads,
+    )
+
+
+def joined_body(ids_ref, dq_ref, dk_ref, dv_ref, cos_ref, sin_ref, w_ref, *refs):
+    gj_ref, keep_ref, send_ref, sums_ref = refs
+    lanes = dq_ref.shape[2]
+    half = keep_ref.shape[2]
+    width = half // 2
+    sums = [0.0, 0.0, 0.0]
+    for m in range(4):
+        cosines, sines = cos_ref[m], sin_ref[m]
+        dq, dk = dq_ref[m], dk_ref[m]
+        parts = (
+            dq * cosines + partner_lanes(dq * sines),
+            dk * cosines + partner_lanes(dk * sines),
+            dv_ref[m],
+        )
+        for i, part in enumerate(parts):
+            low = part.astype(BF)
+            gj_ref[m, :, i * lanes : (i + 1) * lanes] = low
+            sums[i] = sums[i] + jnp.sum(low.astype(F32), axis=0, keepdims=True)
+    for i in range(3):
+        sums_ref[i : i + 1, :] = sums[i]
+    for m in range(4):
+        target = (keep_ref, send_ref)[m % 2]
+        for h, j in CHUNKS:
+            term = dot_nt(gj_ref[m], w_ref[piece_index(ids_ref, h, j)])
+            target[2 * (m // 2) + h, :, j * width : (j + 1) * width] = term.astype(BF)
+
+
+def joined_call(ids, dq, dk, dv, cosines, sines, w):
+    four, rows, lanes = dq.shape
+    half = 2 * w.shape[1]
+    return call(
+        joined_body,
+        [ids, dq, dk, dv, cosines, sines, w],
+        [
+            ((4, rows, 3 * lanes), BF),
+            ((4, rows, half), BF),
+            ((4, rows, half), BF),
+            ((3, lanes), F32),
+        ],
+        "joined_back",
+        flops=2 * 4 * rows * 3 * lanes * 2 * half * 2,
+    )
+
+
+def qkv_grad_body(ids_ref, na_ref, ga_ref, nb_ref, gb_ref, out_ref):
+    width = out_ref.shape[1]
+    for h, j in CHUNKS:
+        at = (2 * h + j) * width
+        total = dot_tn(na_ref[:, at : at + width], ga_ref[...]) + dot_tn(
+            nb_ref[:, at : at + width], gb_ref[...]
+        )
+        out_ref[piece_index(ids_ref, h, j)] = total.astype(BF)
+
+
+def weight_grad_body(ids_ref, *refs):
+    act, gin, mo = refs[0:2], refs[2:4], refs[4:6]
+    c, cp, sec, gb = refs[6:8], refs[8:10], refs[10:12], refs[12:14]
+    keep_ref, send_ref = refs[14:]
+    half = c[0].shape[1]
+    width = half // 2
+    hidden = act[0].shape[1] // 2
+    lanes = mo[0].shape[1] // 2
+    for side, out_ref in enumerate((keep_ref, send_ref)):
+        wide = slice(side * hidden, (side + 1) * hidden)
+        narrow = slice(side * lanes, (side + 1) * lanes)
+        for h, j in CHUNKS:
+            k = piece_index(ids_ref, h, j)
+            cols = slice((2 * h + j) * width, (2 * h + j + 1) * width)
+            part = slice(j * width, (j + 1) * width)
+            back = own = out = 0.0
+            for b in range(2):
+                cot = (c[b], cp[b])[h][:, part]
+                back = back + dot_tn(act[b][:, wide], cot)
+                own = own + dot_tn(sec[b][:, cols], gin[b][:, wide])
+                out = out + dot_tn(mo[b][:, narrow], gb[b][:, cols])
+            out_ref[0, k, :hidden, :] = back.astype(BF)
+            out_ref[0, k, hidden : hidden + width, :] = own[:, :width].astype(BF)
+            out_ref[0, k, hidden + width : hidden + 2 * width, :] = own[:, width:].astype(BF)
+            out_ref[0, k, hidden + 2 * width :, :] = out.astype(BF)
+
+
+def weight_grad_call(ids, act, gin, mo, c, cp, sec, gb):
+    rows, half = c[0].shape
+    width = half // 2
+    hidden = act[0].shape[1] // 4
+    lanes = mo[0].shape[1] // 4
+    shape = (2, 4, hidden + 2 * width + lanes, width)
+    pair = lambda cols: pl.BlockSpec((rows, cols), lambda i: (0, i))
+    args = [ids, *act, *gin, *mo, *c, *cp, *sec, *gb]
+    out = pl.BlockSpec((1,) + shape[1:], lambda i: (i, 0, 0, 0))
+    return call(
+        weight_grad_body,
+        args,
+        [(shape, BF)] * 2,
+        "weight_grads",
+        grid=(2,),
+        in_specs=[SMEM]
+        + [pair(2 * hidden)] * 4
+        + [pair(2 * lanes)] * 2
+        + [whole(a.shape) for a in args[7:]],
+        out_specs=[out, out],
+        flops=2 * 2 * rows * 2 * half * (8 * hidden + 4 * lanes) * 1.5,
+    )
+
+
+def across(axis, size, distance):
+    pairs = [(i, i ^ distance) for i in range(size)]
+    return lambda value: lax.ppermute(value, axis, pairs)
+
+
+def fast_device(
+    inputs,
+    ln1_gain,
+    ln1_bias,
+    w_qkv,
+    b_qkv,
+    w_out,
+    b_out,
+    ln2_gain,
+    ln2_bias,
+    w_in,
+    b_in,
+    w_back,
+    b_back,
+    cotangent,
+):
+    clips, rows, half = inputs.shape
+    width = half // 2
+    lanes = half // 4
+    hidden = w_in.shape[1] // 4
+    shard, ctx, tp = (lax.axis_index(name) for name in ("shard", "ctx", "tp"))
+    ids = jnp.stack([shard, ctx, tp]).astype(jnp.int32)
+    px = across("tp", 2, 1)
+    p1, p2, p3 = (across("ctx", 4, k) for k in (1, 2, 3))
+    pz = [across("shard", 4, k) for k in (1, 2, 3)]
+
+    def from_shards(piece):
+        return jnp.stack([piece] + [p(piece) for p in pz])
+
+    def from_ctx(stack):
+        far = p2(stack)
+        return [stack, p1(stack), far, p1(far)]
+
+    blocks = []
+    for b in range(clips):
+        own = inputs[b]
+        other = px(own)
+        far = p2(own)
+        low = p2(other[: rows // 2])
+        high = px(far[rows // 2 :])
+        near = p1(own)
+        other_near = p1(other)
+        far_near = p1(far)
+        low_near, high_near = p1(low), p1(high)
+        blocks.append(
+            (own, near, far, far_near, other, other_near, low, high, low_near, high_near)
+        )
+
+    qkv_piece = lax.dynamic_slice_in_dim(w_qkv, ctx * lanes, lanes, axis=2).reshape(
+        width, 3 * lanes
+    )
+    wq = from_shards(qkv_piece)
+    out_piece = lax.dynamic_slice_in_dim(w_out, ctx * lanes, lanes, axis=0)
+    wo = from_ctx(from_shards(jnp.stack([out_piece, px(out_piece)])))
+    wi = from_ctx(from_shards(lax.dynamic_slice_in_dim(w_in, ctx * hidden, hidden, axis=1)))
+    wb = from_ctx(from_shards(lax.dynamic_slice_in_dim(w_back, ctx * hidden, hidden, axis=0)))
+
+    def halves(vector):
+        vector = vector.astype(F32)
+        return jnp.concatenate(
+            [
+                lax.dynamic_slice_in_dim(vector, tp * half, half),
+                lax.dynamic_slice_in_dim(vector, (1 - tp) * half, half),
+            ]
+        )
+
+    bias_out = jnp.concatenate([b_out, px(b_out)]).astype(F32)
+    ln_qkv = jnp.stack([halves(ln1_gain), halves(ln1_bias)])
+    ln = jnp.stack(
+        [ln_qkv[0], ln_qkv[1], halves(ln2_gain), halves(ln2_bias), bias_out]
+    )
+    bias_qkv = (
+        lax.dynamic_slice_in_dim(b_qkv, ctx * lanes, lanes, axis=1)
+        .reshape(1, 3 * lanes)
+        .astype(F32)
+    )
+    bias_in = b_in.reshape(4, hidden).astype(F32)
+
+    tables = [rotary_tables((ctx ^ m) * rows, rows) for m in range(4)]
+    cosines = jnp.stack([jnp.tile(one, (1, lanes // HEAD_DIM)) for one, _ in tables])
+    sines = jnp.stack([jnp.tile(two, (1, lanes // HEAD_DIM)) for _, two in tables])
+
+    cots = [(cotangent[b], px(cotangent[b])) for b in range(clips)]
+
+    flat = lambda a: a.reshape(4 * rows, -1)
+    stage = []
+    for b in range(clips):
+        normed, q, k, v = qkv_call(ids, blocks[b], wq, bias_qkv, ln_qkv, cosines, sines)
+        q, k, v = flat(q), flat(k), flat(v)
+        o0, o1, o2, o3, ot, lse = attend_call(q, k, v)
+        mo = jnp.concatenate([o0, p1(o1), p2(o2), p3(o3)], axis=1)
+        stage.append((normed, q, k, v, ot, lse, mo, px(mo)))
+    mids, acts, gins, secs, gbs, gmids, backs = [], [], [], [], [], [], []
+    outputs, in_sums, mid_sums = [], [], []
+    for b in range(clips):
+        mo, mp = stage[b][6:]
+        mid, sec, act, gin, out_own, out_other, gs, in_sum = block_call(
+            ids, blocks[b][0], blocks[b][4], mo, mp, *cots[b], ln, bias_in, wo, wi, wb
+        )
+        gsp = px(gs)
+        arrived = px(out_other)
+        outputs.append(
+            (
+                mid[:, :half]
+                + out_own.astype(F32)
+                + arrived.astype(F32)
+                + b_back.astype(F32)
+            ).astype(BF)
+        )
+        gmid, gb, g0, g1, g2, g3, sums = branch_call(ids, gs, gsp, *cots[b], mid, ln, wo)
+        backs.append((g0, p1(g1), p2(g2), p3(g3)))
+        for group, item in zip(
+            (mids, acts, gins, secs, gbs, gmids, in_sums, mid_sums),
+            (mid, act, gin, sec, gb, gmid, in_sum, sums),
+        ):
+            group.append(item)
+
+    keep, send = weight_grad_call(
+        ids,
+        acts,
+        gins,
+        [s[6] for s in stage],
+        [c for c, _ in cots],
+        [c for _, c in cots],
+        secs,
+        gbs,
+    )
+
+    def add(*terms):
+        return sum(term.astype(F32) for term in terms)
+
+    def over_ctx(keep, send):
+        near = p1(send)
+        far = p2(add(keep[1], near[1]).astype(BF))
+        return add(keep[0], near[0], far).astype(BF)
+
+    def over_shards(stack):
+        return add(stack[0], *(p(stack[k + 1]) for k, p in enumerate(pz)))
+
+    def spread(piece):
+        far = p2(piece)
+        return [piece, p1(piece), far, p1(far)]
+
+    dense = spread(over_shards(over_ctx(keep, send)).astype(BF))
+
+    joins, q_sums, grads_normed = [], [], []
+    for b in range(clips):
+        normed, q, k, v, ot, lse, mo, mp = stage[b]
+        dq, dk, dv = attend_back_call(q, k, v, backs[b], ot, lse)
+        gj, kept, sent, q_sum = joined_call(
+            ids, *(a.reshape(4, rows, lanes) for a in (dq, dk, dv)), cosines, sines, wq
+        )
+        near = p1(sent)
+        cut = rows // 2
+        across_low = px(add(kept[3, :cut], near[3, :cut]).astype(BF))
+        across_high = p2(add(kept[3, cut:], near[3, cut:]).astype(BF))
+        far = add(kept[2], near[2])
+        far = jnp.concatenate([far[:cut] + across_low.astype(F32), far[cut:]]).astype(BF)
+        other = add(kept[1], near[1])
+        other = jnp.concatenate([other[:cut], other[cut:] + across_high.astype(F32)]).astype(BF)
+        grads_normed.append(add(kept[0], near[0], p2(far), px(other)))
+        joins.append(gj)
+        q_sums.append(q_sum)
+
+    qkv_sum = call(
+        qkv_grad_body,
+        [ids, flat(stage[0][0]), flat(joins[0]), flat(stage[1][0]), flat(joins[1])],
+        [((4, width, 3 * lanes), BF)],
+        "qkv_grad",
+        flops=2 * 8 * rows * 2 * half * 3 * lanes * 1.5,
+    )[0]
+    qkv_dense = spread(over_shards(qkv_sum).astype(BF))
+
+    gain_own = ln_qkv[0, :half]
+    input_grads, gain_sum, shift_sum = [], 0.0, 0.0
+    for b in range(clips):
+        one, unused, inv = norm_parts(blocks[b][0].astype(F32), blocks[b][4].astype(F32))
+        grad = grads_normed[b]
+        gain_sum = gain_sum + jnp.sum(grad * one, axis=0)
+        shift_sum = shift_sum + jnp.sum(grad, axis=0)
+        scaled = grad * gain_own
+        stats = jnp.stack([jnp.sum(scaled, axis=1), jnp.sum(scaled * one, axis=1)])
+        stats = (stats + px(stats)) / (2 * half)
+        input_grads.append(
+            gmids[b] + inv * (scaled - stats[0][:, None] - one * stats[1][:, None])
+        )
+
+    def all_sum(vector):
+        vector = vector + sum(p(vector) for p in pz)
+        return vector + p1(vector) + p2(vector) + p3(vector)
+
+    def unroll(pieces):
+        return [lax.dynamic_index_in_dim(pieces, ctx ^ m, 0, False) for m in range(4)]
+
+    in_total = in_sums[0] + in_sums[1]
+    in_total = jnp.concatenate(unroll(in_total.reshape(4, hidden)))
+    mid_total = mid_sums[0] + mid_sums[1]
+    q_total = q_sums[0] + q_sums[1]
+    q_total = lax.dynamic_update_slice(
+        jnp.zeros((4, 3, lanes), F32), q_total[None], (ctx, 0, 0)
+    )
+    early = all_sum(jnp.concatenate([in_total, mid_total.reshape(-1)]))
+    late = all_sum(jnp.concatenate([gain_sum, shift_sum, q_total.reshape(-1)]))
+    grad_b_in = early[: 4 * hidden]
+    mid_total = early[4 * hidden :].reshape(3, 2 * half)
+    grad_b_out, grad_b_back = mid_total[2, :half], mid_total[2, half:]
+    grad_b_qkv = (
+        late[2 * half :].reshape(4, 3, lanes).transpose(1, 0, 2).reshape(3, 4 * lanes)
+    )
+    own_ln1 = late[: 2 * half].reshape(2, half)
+    other_ln1 = px(own_ln1)
+
+    def in_order(own, other):
+        return jnp.where(tp == 0, jnp.concatenate([own, other]), jnp.concatenate([other, own]))
+
+    grad_ln1 = [in_order(own_ln1[i], other_ln1[i]) for i in range(2)]
+    grad_ln2 = [in_order(mid_total[i, :half], mid_total[i, half:]) for i in range(2)]
+
+    ordered = unroll(jnp.stack(dense))
+    grad_w_back = jnp.concatenate([p[:hidden] for p in ordered], axis=0).astype(F32)
+    grad_w_in = jnp.concatenate(
+        [p[hidden + i * width : hidden + (i + 1) * width] for p in ordered for i in range(2)],
+        axis=1,
+    ).astype(F32)
+    grad_w_out = jnp.concatenate([p[hidden + 2 * width :] for p in ordered], axis=0).astype(F32)
+    ordered = unroll(jnp.stack(qkv_dense))
+    grad_w_qkv = jnp.concatenate(
+        [p.reshape(width, 3, lanes) for p in ordered], axis=2
+    ).astype(F32)
+    return (
+        jnp.stack(outputs),
+        jnp.stack(input_grads),
+        grad_ln1[0],
+        grad_ln1[1],
+        grad_w_qkv,
+        grad_b_qkv,
+        grad_w_out,
+        grad_b_out,
+        grad_ln2[0],
+        grad_ln2[1],
+        grad_w_in,
+        grad_b_in,
+        grad_w_back,
+        grad_b_back,
+    )
+
+
+def quick_form_fits(mesh):
+    return (mesh.shape["shard"], mesh.shape["ctx"], mesh.shape["tp"]) == (4, 4, 2)
+
+
 def solution(mesh):
     placed = (
         P("shard", "ctx", "tp"),
@@ -430,7 +1190,7 @@
         P("shard", "ctx", "tp"),
     )
     return jax.shard_map(
-        per_device,
+        fast_device if quick_form_fits(mesh) else per_device,
         mesh=mesh,
         in_specs=placed,
         out_specs=(

time: 1390 us -> 688 us (0.49)
  waiting for transfers between devices: 692 us -> 271 us
  matrix products: 286 us -> 0 us
  Pallas kernels: 0 us -> 202 us
  local copies, waits for them, and re-layouts: 212 us -> 35.9 us
  starting transfers between devices: 1.53 us -> 105 us
  other arithmetic: 116 us -> 60 us
  blocking collectives: 54.4 us -> 0 us
    dot_general x40 -> x0, matrix products: 286 us -> none  [the longest x4 37.5 us: absorb_block(): jnp.einsum('cqhd,ckhd->chqk', queries, key_piece, preferred_element_type=...]
    all_gather x9 -> x0, waiting for transfers between devices: 278 us -> none  [the longest x1 79.1 us: fetch_weights(): lax.all_gather(w_back, 'shard', axis=1, tiled=True)]
    reduce_scatter x8 -> x0, waiting for transfers between devices: 277 us -> none  [the longest x1 79.5 us: per_device(): lax.psum_scatter(summed[2].astype(jnp.bfloat16), 'shard', scatter_dimensi...]
    ppermute x0 -> x100, waiting for transfers between devices: none -> 271 us  [across(): return lambda value: lax.ppermute(value, axis, pairs)]
    pallas_call x0 -> x14, Pallas kernels: none -> 202 us  [call(): pl.pallas_call(body, in_specs=in_specs or [SMEM] + [whole(a.shape) for a...]
    psum x3 -> x0, waiting for transfers between devices: 134 us -> none  [the longest x2 126 us: back_total(): return lax.psum(summand.astype(jnp.bfloat16), 'tp').astype(jnp.float32)]
    ppermute x0 -> x100, starting transfers between devices: none -> 105 us  [across(): return lambda value: lax.ppermute(value, axis, pairs)]
    concatenate x6, local copies, waits for them, and re-layouts: 94.2 us -> 1.46 us  [the longest x2 1.37 us: fast_device(): bias_out = jnp.concatenate([b_out, px(b_out)]).astype(F32)]
  transfers between devices with their start and end apart: 20 -> 100, of which waited for: 14 -> 39; matrix products, arithmetic and copies ran while one was open for 29% -> 13% of each run, Pallas kernels for 0% -> 26%
where the time goes in v1:
time: 688 us; the launch traced here: 677 us
  waiting for transfers between devices  271 us (39%)
  Pallas kernels  202 us (29%)
  starting transfers between devices  105 us (15%)
  other arithmetic  60 us (9%)
  local copies, waits for them, and re-layouts  35.9 us (5%)
    ppermute x100, waiting for transfers between devices, across(): return lambda value: lax.ppermute(value, axis, pairs)  271 us
    pallas_call x14, Pallas kernels, call(): pl.pallas_call(body, in_specs=in_specs or [SMEM] + [whole(a.shape) for a...  202 us
    ppermute x100, starting transfers between devices, across(): return lambda value: lax.ppermute(value, axis, pairs)  105 us
  transfers between devices with their start and end apart: 100, of which 39 were waited for; matrix products, arithmetic and copies ran while one was open for 13% of the time, Pallas kernels for 26%

profile of v1, /device:TPU:8, one launch (start us, length us, event | category | flops | bytes accessed | tf_op | source)
XLA Modules:
  0.0 676.8 jit_solution(225192157298200086)
XLA Ops:
  18.8 2.1 fusion.56
  28.2 2.6 pad_maximum_fusion.2.refs_13_.cos_ref
  38.7 2.9 collective-permute-done.20
  41.7 8.5 %collective-permute-start.9 = (bf16[256,384]{1,0:T(8,128)(2,1)}, bf16[256,384]{1,0:T(8,128)(2,1)S(1)}, u32[]{:S(2)}, u32[]{:S(2)}) collective-permute-start(bf16[256,384]{1,0:T(8,128)(2,1)} %copy.31), channel_id=1, source_target_pairs={{0,8},{8,0},{16,24},{24,16},{1,9},{9,1},{17,25},{25,17},{2,10},{10... | collective-permute-start | bytes 589832 | tf_op jit(solution)/shard_map/ppermute | solution.py:921
  50.2 3.4 collective-permute-done.21
  55.8 3.3 collective-permute-done.10
  59.1 5.3 collective-permute-start.26
  71.0 5.0 collective-permute-done.32
  78.7 5.9 collective-permute-done.33
  88.9 2.1 pad_maximum_fusion.7.refs_10_.w_ref
  93.8 6.8 collective-permute-done.27
  107.1 3.5 collective-permute-done.44.refs_7_
  117.5 9.0 %qkv.3 = (bf16[4,512,1024]{2,1,0:T(8,128)(2,1)}, bf16[4,512,128]{2,1,0:T(8,128)(2,1)}, bf16[4,512,128]{2,1,0:T(8,128)(2,1)}, bf16[4,512,128]{2,1,0:T(8,128)(2,1)}) custom-call(s32[3]{0:T(128)} %pad_add_fusion.ids_ref, bf16[512,512]{1,0:T(8,128)(2,1)} %get-tuple-element.201.refs_0_, bf16[512,512]{1,0:T(8,128)(2,1)} %copy-done.74, ...), custom_call_target="tpu_custom_call" | custom-call | flops 4831838208 | bytes 12854796 | tf_op jit(solution)/shard_map/qkv/pallas_call | solution.py:448
  126.6 6.1 collective-permute-done.6.refs_7_
  133.2 14.4 %attend.3 = (bf16[512,128]{1,0:T(8,128)(2,1)}, bf16[512,128]{1,0:T(8,128)(2,1)}, bf16[512,128]{1,0:T(8,128)(2,1)}, bf16[512,128]{1,0:T(8,128)(2,1)}, f32[128,2048]{1,0:T(8,128)}, /*index=5*/f32[2,2048]{1,0:T(2,128)}) custom-call(bf16[2048,128]{1,0:T(8,128)(2,1)} %bitcast.336, bf16[2048,128]{1,0:T(8,128)(2,1)} %bitcast.338, bf16[2048,128]{1,0:T(8,128)(2,1)} %bitcast.340), custom_call_target="tpu_custom_call" | custom-call | flops 8589934592 | bytes 3162112 | tf_op jit(solution)/shard_map/attend/pallas_call | solution.py:448
  151.5 8.7 %qkv.2 = (bf16[4,512,1024]{2,1,0:T(8,128)(2,1)}, bf16[4,512,128]{2,1,0:T(8,128)(2,1)}, bf16[4,512,128]{2,1,0:T(8,128)(2,1)}, bf16[4,512,128]{2,1,0:T(8,128)(2,1)}) custom-call(s32[3]{0:T(128)} %pad_add_fusion.ids_ref, bf16[512,512]{1,0:T(8,128)(2,1)} %get-tuple-element.200.refs_0_, bf16[512,512]{1,0:T(8,128)(2,1)} %copy-done.73, ...), custom_call_target="tpu_custom_call" | custom-call | flops 4831838208 | bytes 12854796 | tf_op jit(solution)/shard_map/qkv/pallas_call | solution.py:448
  160.3 26.8 %attend.2 = (bf16[512,128]{1,0:T(8,128)(2,1)}, bf16[512,128]{1,0:T(8,128)(2,1)}, bf16[512,128]{1,0:T(8,128)(2,1)}, bf16[512,128]{1,0:T(8,128)(2,1)}, f32[128,2048]{1,0:T(8,128)}, /*index=5*/f32[2,2048]{1,0:T(2,128)}) custom-call(bf16[2048,128]{1,0:T(8,128)(2,1)} %bitcast.342, bf16[2048,128]{1,0:T(8,128)(2,1)} %bitcast.344, bf16[2048,128]{1,0:T(8,128)(2,1)} %bitcast.346), custom_call_target="tpu_custom_call" | custom-call | flops 8589934592 | bytes 3162112 | tf_op jit(solution)/shard_map/attend/pallas_call | solution.py:448
  189.5 20.8 %collective-permute-done.48 = bf16[512,128]{1,0:T(8,128)(2,1)S(1)} collective-permute-done((bf16[512,128]{1,0:T(8,128)(2,1)S(1)}, bf16[512,128]{1,0:T(8,128)(2,1)S(1)}, u32[]{:S(2)}, u32[]{:S(2)}) %collective-permute-start.48) | collective-permute-done | bytes 131104 | tf_op jit(solution)/shard_map/ppermute | solution.py:921
  213.8 4.0 collective-permute-done.13
  217.9 2.3 collective-permute-done.14
  225.0 11.7 %collective-permute-done.15.refs_3_ = bf16[512,512]{1,0:T(8,128)(2,1)S(1)} collective-permute-done((bf16[512,512]{1,0:T(8,128)(2,1)S(1)}, bf16[512,512]{1,0:T(8,128)(2,1)S(1)}, u32[]{:S(2)}, u32[]{:S(2)}) %collective-permute-start.15) | collective-permute-done | bytes 524320 | tf_op jit(solution)/shard_map/ppermute | solution.py:921
  237.9 18.9 %block.2 = (f32[512,1024]{1,0:T(8,128)}, bf16[512,1024]{1,0:T(8,128)(2,1)}, bf16[512,2048]{1,0:T(8,128)(2,1)}, bf16[512,2048]{1,0:T(8,128)(2,1)}, bf16[512,512]{...) custom-call(s32[3]{0:T(128)} %pad_add_fusion.ids_ref, ...), custom_call_target="tpu_custom_call" | custom-call | flops 19327352832 | bytes 23105548 | tf_op jit(solution)/shard_map/block/pallas_call | solution.py:448
  256.9 1.8 collective-permute-done.50.refs_3_
  259.5 19.1 %block.3 = (f32[512,1024]{1,0:T(8,128)}, bf16[512,1024]{1,0:T(8,128)(2,1)}, bf16[512,2048]{1,0:T(8,128)(2,1)}, bf16[512,2048]{1,0:T(8,128)(2,1)}, bf16[512,512]{...) custom-call(s32[3]{0:T(128)} %pad_add_fusion.ids_ref, ...), custom_call_target="tpu_custom_call" | custom-call | flops 19327352832 | bytes 23105548 | tf_op jit(solution)/shard_map/block/pallas_call | solution.py:448
  283.6 10.7 %collective-permute-done.37 = bf16[512,512]{1,0:T(8,128)(2,1)S(1)} collective-permute-done((bf16[512,512]{1,0:T(8,128)(2,1)S(1)}, bf16[512,512]{1,0:T(8,128)(2,1)S(1)}, u32[]{:S(2)}, u32[]{:S(2)}) %collective-permute-start.37) | collective-permute-done | bytes 524320 | tf_op jit(solution)/shard_map/ppermute | solution.py:921
  294.3 11.2 %collective-permute-done.52 = bf16[512,512]{1,0:T(8,128)(2,1)S(1)} collective-permute-done((bf16[512,512]{1,0:T(8,128)(2,1)}, bf16[512,512]{1,0:T(8,128)(2,1)S(1)}, u32[]{:S(2)}, u32[]{:S(2)}) %collective-permute-start.52) | collective-permute-done | bytes 524320 | tf_op jit(solution)/shard_map/ppermute | solution.py:921
  305.6 2.2 fusion.35
  308.8 19.2 %collective-permute-done.53.gsp_ref = bf16[512,1024]{1,0:T(8,128)(2,1)S(1)} collective-permute-done((bf16[512,1024]{1,0:T(8,128)(2,1)}, bf16[512,1024]{1,0:T(8,128)(2,1)S(1)}, u32[]{:S(2)}, u32[]{:S(2)}) %collective-permute-start.53) | collective-permute-done | bytes 1048608 | tf_op jit(solution)/shard_map/ppermute | solution.py:921
  329.0 6.7 branch.2
  335.8 13.4 %collective-permute-done.63.gsp_ref = bf16[512,1024]{1,0:T(8,128)(2,1)S(1)} collective-permute-done((bf16[512,1024]{1,0:T(8,128)(2,1)}, bf16[512,1024]{1,0:T(8,128)(2,1)S(1)}, u32[]{:S(2)}, u32[]{:S(2)}) %collective-permute-start.63) | collective-permute-done | bytes 1048608 | tf_op jit(solution)/shard_map/ppermute | solution.py:921
  350.2 6.7 branch.3
  359.2 1.8 collective-permute-start.95
  363.0 17.2 %weight_grads.1 = (bf16[2,4,1152,256]{3,2,1,0:T(8,128)(2,1)}, bf16[2,4,1152,256]{3,2,1,0:T(8,128)(2,1)}) custom-call(s32[3]{0:T(128)} %pad_add_fusion.ids_ref, bf16[512,2048]{1,0:T(8,128)(2,1)} %get-tuple-element.132.refs_0_, bf16[512,2048]{1,0:T(8,128)(2,1)} %get-tuple-element.133.refs_1_, bf16[512,2048]{1,0:T(8,128)(2,1)} %get-tuple-element.134.refs_2_, ...), custom_call_target="tpu_custom_call" | custom-call | flops 14495514624 | bytes 25165836 | tf_op jit(solution)/shard_map/weight_grads/pallas_call | solution.py:448
  382.7 4.0 collective-permute-done.65.d2
  389.7 25.0 %attend_back.3 = (f32[2048,128]{1,0:T(8,128)}, f32[2048,128]{1,0:T(8,128)}, f32[2048,128]{1,0:T(8,128)}) custom-call(bf16[2048,128]{1,0:T(8,128)(2,1)} %bitcast.337, bf16[2048,128]{1,0:T(8,128)(2,1)} %bitcast.339, bf16[2048,128]{1,0:T(8,128)(2,1)} %bitcast.341, bf16[512,128]{1,0:T(8,128)(2,1)} %get-tuple-element.115.d0, bf16[512,128]{1,0:T(8,128)(2,1)} %copy-done.99, ...), custom_call_target="tpu_custom_call" | custom-call | flops 21474836480 | bytes 6307840 | tf_op jit(solution)/shard_map/attend_back/pallas_call | solution.py:448
  414.7 7.4 %joined_back.3 = (bf16[4,512,384]{2,1,0:T(8,128)(2,1)}, bf16[4,512,512]{2,1,0:T(8,128)(2,1)}, bf16[4,512,512]{2,1,0:T(8,128)(2,1)}, f32[3,128]{1,0:T(4,128)}) custom-call(s32[3]{0:T(128)} %pad_add_fusion.ids_ref, f32[4,512,128]{2,1,0:T(8,128)} %bitcast.333, f32[4,512,128]{2,1,0:T(8,128)} %bitcast.334, f32[4,512,128]{2,1,0:T(8,128)} %bitcast.335, ...), custom_call_target="tpu_custom_call" | custom-call | flops 3221225472 | bytes 11798028 | tf_op jit(solution)/shard_map/joined_back/pallas_call | solution.py:448
  424.5 25.1 %attend_back.2 = (f32[2048,128]{1,0:T(8,128)}, f32[2048,128]{1,0:T(8,128)}, f32[2048,128]{1,0:T(8,128)}) custom-call(bf16[2048,128]{1,0:T(8,128)(2,1)} %bitcast.343, bf16[2048,128]{1,0:T(8,128)(2,1)} %bitcast.345, bf16[2048,128]{1,0:T(8,128)(2,1)} %bitcast.347, bf16[512,128]{1,0:T(8,128)(2,1)} %get-tuple-element.102.d0, bf16[512,128]{1,0:T(8,128)(2,1)} %copy-done.90, ...), custom_call_target="tpu_custom_call" | custom-call | flops 21474836480 | bytes 6307840 | tf_op jit(solution)/shard_map/attend_back/pallas_call | solution.py:448
  449.6 7.3 %joined_back.2 = (bf16[4,512,384]{2,1,0:T(8,128)(2,1)}, bf16[4,512,512]{2,1,0:T(8,128)(2,1)}, bf16[4,512,512]{2,1,0:T(8,128)(2,1)}, f32[3,128]{1,0:T(4,128)}) custom-call(s32[3]{0:T(128)} %pad_add_fusion.ids_ref, f32[4,512,128]{2,1,0:T(8,128)} %bitcast.330, f32[4,512,128]{2,1,0:T(8,128)} %bitcast.331, f32[4,512,128]{2,1,0:T(8,128)} %bitcast.332, ...), custom_call_target="tpu_custom_call" | custom-call | flops 3221225472 | bytes 11798028 | tf_op jit(solution)/shard_map/joined_back/pallas_call | solution.py:448
  456.9 9.8 %qkv_grad.1 = bf16[4,256,384]{2,1,0:T(8,128)(2,1)} custom-call(s32[3]{0:T(128)} %pad_add_fusion.ids_ref, bf16[2048,1024]{1,0:T(8,128)(2,1)} %bitcast.327, bf16[2048,384]{1,0:T(8,128)(2,1)} %bitcast.329, bf16[2048,1024]{1,0:T(8,128)(2,1)} %bitcast.326, bf16[2048,384]{1,0:T(8,128)(2,1)} %bitcast.328), custom_call_target="tpu_custom_call" | custom-call | flops 4831838208 | bytes 12320780 | tf_op jit(solution)/shard_map/qkv_grad/pallas_call | solution.py:448
  468.4 1.7 collective-permute-start.80
  470.8 1.9 collective-permute-start.82
  472.6 3.6 collective-permute-done.80
  476.2 5.8 collective-permute-start.81
  482.6 4.1 collective-permute-done.82
  486.7 2.7 collective-permute-done.81
  492.4 4.0 collective-permute-done.84
  498.8 2.0 convert_add_fusion.2
  504.5 2.0 collective-permute-done.68
  507.6 1.8 collective-permute-done.70
  511.9 2.5 collective-permute-done.58
  517.9 3.6 fusion.1
  529.5 3.0 copy.47
  532.5 6.1 collective-permute-done.61
  538.6 52.8 %collective-permute-done.59 = bf16[512,512]{1,0:T(8,128)(2,1)} collective-permute-done((bf16[512,512]{1,0:T(8,128)(2,1)}, bf16[512,512]{1,0:T(8,128)(2,1)}, u32[]{:S(2)}, u32[]{:S(2)}) %collective-permute-start.59) | collective-permute-done | bytes 524320 | tf_op jit(solution)/shard_map/ppermute | solution.py:921
  591.4 3.2 fusion.27
  595.4 4.3 collective-permute-start.74
  604.3 4.0 fusion
  610.1 2.8 collective-permute-start.89
  613.9 14.8 %collective-permute-done.88 = bf16[1152,256]{1,0:T(8,128)(2,1)S(1)} collective-permute-done((bf16[1152,256]{1,0:T(8,128)(2,1)S(1)}, bf16[1152,256]{1,0:T(8,128)(2,1)S(1)}, u32[]{:S(2)}, u32[]{:S(2)}) %collective-permute-start.88) | collective-permute-done | bytes 589856 | tf_op jit(solution)/shard_map/ppermute | solution.py:921
  628.7 2.6 collective-permute-start.73
  631.3 18.8 %collective-permute-done.90 = bf16[1152,256]{1,0:T(8,128)(2,1)S(1)} collective-permute-done((bf16[1152,256]{1,0:T(8,128)(2,1)S(1)}, bf16[1152,256]{1,0:T(8,128)(2,1)S(1)}, u32[]{:S(2)}, u32[]{:S(2)}) %collective-permute-start.90) | collective-permute-done | bytes 589856 | tf_op jit(solution)/shard_map/ppermute | solution.py:921
  650.1 6.2 collective-permute-done.89
  661.0 4.3 collective-permute-done.78
  665.4 1.8 collective-permute-done.77
  (532 shorter events, 150.9 us)
Async XLA Ops:
  0.7 36.5 %collective-permute-start.17 = (bf16[512]{0:T(512)(128)(2,1)}, bf16[512]{0:T(512)(128)(2,1)}, u32[]{:S(2)}, u32[]{:S(2)}) collective-permute-start(bf16[512]{0:T(512)(128)(2,1)} %param.20), channel_id=1, source_target_pairs={{0,1},{1,0},{2,3},{3,2},{4,5},{5,4},{6,7},{7,6},{8,9},{9,8},{10,11... | collective-permute-start | bytes 3080 | tf_op jit(solution)/shard_map/ppermute | solution.py:921
  3.1 29.5 %collective-permute-start.18 = (bf16[128,256]{1,0:T(8,128)(2,1)S(1)}, bf16[128,256]{1,0:T(8,128)(2,1)S(1)}, u32[]{:S(2)}, u32[]{:S(2)}) collective-permute-start(bf16[128,256]{1,0:T(8,128)(2,1)S(1)} %constant_dynamic-slice_fusion.10), channel_id=1, source_target_pairs={{0,1},{1,0},{2,3},{3,2},{4,5},{5,4},{6,7},{7,6},{8,9},{9,8},{10,11... | collective-permute-start | bytes 196616 | tf_op jit(solution)/shard_map/ppermute | solution.py:921
  5.6 48.0 %collective-permute-start.11 = (bf16[256,384]{1,0:T(8,128)(2,1)}, bf16[256,384]{1,0:T(8,128)(2,1)}, u32[]{:S(2)}, u32[]{:S(2)}) collective-permute-start(bf16[256,384]{1,0:T(8,128)(2,1)} %copy.31), channel_id=1, source_target_pairs={{0,24},{8,16},{16,8},{24,0},{1,25},{9,17},{17,9},{25,1},{2,26},{10... | collective-permute-start | bytes 589832 | tf_op jit(solution)/shard_map/ppermute | solution.py:921
  34.3 15.9 %collective-permute-start.19 = (bf16[2,128,256]{2,1,0:T(8,128)(2,1)S(1)}, bf16[2,128,256]{2,1,0:T(8,128)(2,1)}, u32[]{:S(2)}, u32[]{:S(2)}) collective-permute-start(bf16[2,128,256]{2,1,0:T(8,128)(2,1)S(1)} %get-tuple-element.210), channel_id=1, source_target_pairs={{0,8},{8,0},{16,24},{24,16},{1,9},{9,1},{17,25},{25,17},{2,10},{10... | collective-permute-start | bytes 393224 | tf_op jit(solution)/shard_map/ppermute | solution.py:921
  35.7 17.9 %collective-permute-start.21 = (bf16[2,128,256]{2,1,0:T(8,128)(2,1)S(1)}, bf16[2,128,256]{2,1,0:T(8,128)(2,1)}, u32[]{:S(2)}, u32[]{:S(2)}) collective-permute-start(bf16[2,128,256]{2,1,0:T(8,128)(2,1)S(1)} %get-tuple-element.210), channel_id=1, source_target_pairs={{0,24},{8,16},{16,8},{24,0},{1,25},{9,17},{17,9},{25,1},{2,26},{10... | collective-permute-start | bytes 393224 | tf_op jit(solution)/shard_map/ppermute | solution.py:921
  37.2 21.9 %collective-permute-start.10 = (bf16[256,384]{1,0:T(8,128)(2,1)}, bf16[256,384]{1,0:T(8,128)(2,1)S(1)}, u32[]{:S(2)}, u32[]{:S(2)}) collective-permute-start(bf16[256,384]{1,0:T(8,128)(2,1)} %copy.31), channel_id=1, source_target_pairs={{0,16},{8,24},{16,0},{24,8},{1,17},{9,25},{17,1},{25,9},{2,18},{10... | collective-permute-start | bytes 589832 | tf_op jit(solution)/shard_map/ppermute | solution.py:921
  41.7 28.6 %collective-permute-start.9 = (bf16[256,384]{1,0:T(8,128)(2,1)}, bf16[256,384]{1,0:T(8,128)(2,1)S(1)}, u32[]{:S(2)}, u32[]{:S(2)}) collective-permute-start(bf16[256,384]{1,0:T(8,128)(2,1)} %copy.31), channel_id=1, source_target_pairs={{0,8},{8,0},{16,24},{24,16},{1,9},{9,1},{17,25},{25,17},{2,10},{10... | collective-permute-start | bytes 589832 | tf_op jit(solution)/shard_map/ppermute | solution.py:921
  50.2 25.7 %collective-permute-start.32 = (bf16[512,256]{1,0:T(8,128)(2,1)}, bf16[512,256]{1,0:T(8,128)(2,1)S(1)}, u32[]{:S(2)}, u32[]{:S(2)}) collective-permute-start(bf16[512,256]{1,0:T(8,128)(2,1)} %constant_dynamic-slice_fusion.8), channel_id=1, source_target_pairs={{0,16},{8,24},{16,0},{24,8},{1,17},{9,25},{17,1},{25,9},{2,18},{10... | collective-permute-start | bytes 786440 | tf_op jit(solution)/shard_map/ppermute | solution.py:921
  53.6 23.9 %collective-permute-start.31 = (bf16[512,256]{1,0:T(8,128)(2,1)}, bf16[512,256]{1,0:T(8,128)(2,1)S(1)}, u32[]{:S(2)}, u32[]{:S(2)}) collective-permute-start(bf16[512,256]{1,0:T(8,128)(2,1)} %constant_dynamic-slice_fusion.8), channel_id=1, source_target_pairs={{0,8},{8,0},{16,24},{24,16},{1,9},{9,1},{17,25},{25,17},{2,10},{10... | collective-permute-start | bytes 786440 | tf_op jit(solution)/shard_map/ppermute | solution.py:921
  53.6 31.0 %collective-permute-start.33 = (bf16[512,256]{1,0:T(8,128)(2,1)}, bf16[512,256]{1,0:T(8,128)(2,1)}, u32[]{:S(2)}, u32[]{:S(2)}) collective-permute-start(bf16[512,256]{1,0:T(8,128)(2,1)} %constant_dynamic-slice_fusion.8), channel_id=1, source_target_pairs={{0,24},{8,16},{16,8},{24,0},{1,25},{9,17},{17,9},{25,1},{2,26},{10... | collective-permute-start | bytes 786440 | tf_op jit(solution)/shard_map/ppermute | solution.py:921
  59.1 28.3 %collective-permute-start.26 = (bf16[256,512]{1,0:T(8,128)(2,1)}, bf16[256,512]{1,0:T(8,128)(2,1)}, u32[]{:S(2)}, u32[]{:S(2)}) collective-permute-start(bf16[256,512]{1,0:T(8,128)(2,1)} %constant_dynamic-slice_fusion.9), channel_id=1, source_target_pairs={{0,16},{8,24},{16,0},{24,8},{1,17},{9,25},{17,1},{25,9},{2,18},{10... | collective-permute-start | bytes 786440 | tf_op jit(solution)/shard_map/ppermute | solution.py:921
  70.2 20.8 %collective-permute-start.25 = (bf16[256,512]{1,0:T(8,128)(2,1)}, bf16[256,512]{1,0:T(8,128)(2,1)}, u32[]{:S(2)}, u32[]{:S(2)}) collective-permute-start(bf16[256,512]{1,0:T(8,128)(2,1)} %constant_dynamic-slice_fusion.9), channel_id=1, source_target_pairs={{0,8},{8,0},{16,24},{24,16},{1,9},{9,1},{17,25},{25,17},{2,10},{10... | collective-permute-start | bytes 786440 | tf_op jit(solution)/shard_map/ppermute | solution.py:921
  75.9 25.8 %collective-permute-start.40 = (bf16[512,512]{1,0:T(8,128)(2,1)}, bf16[512,512]{1,0:T(8,128)(2,1)S(1)}, u32[]{:S(2)}, u32[]{:S(2)}) collective-permute-start(bf16[512,512]{1,0:T(8,128)(2,1)} %get-tuple-element.201.refs_0_), channel_id=1, source_target_pairs={{0,4},{2,6},{4,0},{6,2},{1,5},{3,7},{5,1},{7,3},{8,12},{10,14},{12... | collective-permute-start | bytes 1572872 | tf_op jit(solution)/shard_map/ppermute | solution.py:921
  77.5 25.7 %collective-permute-start.38 = (bf16[512,512]{1,0:T(8,128)(2,1)}, bf16[512,512]{1,0:T(8,128)(2,1)S(1)}, u32[]{:S(2)}, u32[]{:S(2)}) collective-permute-start(bf16[512,512]{1,0:T(8,128)(2,1)} %get-tuple-element.201.refs_0_), channel_id=1, source_target_pairs={{0,1},{1,0},{2,3},{3,2},{4,5},{5,4},{6,7},{7,6},{8,9},{9,8},{10,11... | collective-permute-start | bytes 1572872 | tf_op jit(solution)/shard_map/ppermute | solution.py:921
  84.6 20.1 %collective-permute-start = (bf16[512,512]{1,0:T(8,128)(2,1)}, bf16[512,512]{1,0:T(8,128)(2,1)S(1)}, u32[]{:S(2)}, u32[]{:S(2)}) collective-permute-start(bf16[512,512]{1,0:T(8,128)(2,1)} %get-tuple-element.200.refs_0_), channel_id=1, source_target_pairs={{0,1},{1,0},{2,3},{3,2},{4,5},{5,4},{6,7},{7,6},{8,9},{9,8},{10,11... | collective-permute-start | bytes 1572872 | tf_op jit(solution)/shard_map/ppermute | solution.py:921
  113.0 47.1 %collective-permute-start.16 = (bf16[512,512]{1,0:T(8,128)(2,1)S(1)}, bf16[512,512]{1,0:T(8,128)(2,1)S(1)}, u32[]{:S(2)}, u32[]{:S(2)}) collective-permute-start(bf16[512,512]{1,0:T(8,128)(2,1)S(1)} %get-tuple-element.198.refs_4_.c_ref.refs_6_), channel_id=1, source_target_pairs={{0,1},{1,0},{2,3},{3,2},{4,5},{5,4},{6,7},{7,6},{8,9},{9,8},{10,11... | collective-permute-start | bytes 1572872 | tf_op jit(solution)/shard_map/ppermute | solution.py:921
  113.8 18.9 %collective-permute-start.6 = (bf16[256,512]{1,0:T(8,128)(2,1)S(1)}, bf16[256,512]{1,0:T(8,128)(2,1)}, u32[]{:S(2)}, u32[]{:S(2)}) collective-permute-start(bf16[256,512]{1,0:T(8,128)(2,1)S(1)} %slice.469), channel_id=1, source_target_pairs={{0,1},{1,0},{2,3},{3,2},{4,5},{5,4},{6,7},{7,6},{8,9},{9,8},{10,11... | collective-permute-start | bytes 786440 | tf_op jit(solution)/shard_map/ppermute | solution.py:921
  115.1 17.6 %collective-permute-start.5 = (bf16[256,512]{1,0:T(8,128)(2,1)S(1)}, bf16[256,512]{1,0:T(8,128)(2,1)}, u32[]{:S(2)}, u32[]{:S(2)}) collective-permute-start(bf16[256,512]{1,0:T(8,128)(2,1)S(1)} %slice.468), channel_id=1, source_target_pairs={{0,4},{2,6},{4,0},{6,2},{1,5},{3,7},{5,1},{7,3},{8,12},{10,14},{12... | collective-permute-start | bytes 786440 | tf_op jit(solution)/shard_map/ppermute | solution.py:921
  116.7 32.6 %collective-permute-start.3 = (bf16[512,512]{1,0:T(8,128)(2,1)}, bf16[512,512]{1,0:T(8,128)(2,1)S(1)}, u32[]{:S(2)}, u32[]{:S(2)}) collective-permute-start(bf16[512,512]{1,0:T(8,128)(2,1)} %collective-permute-done.2.refs_2_), channel_id=1, source_target_pairs={{0,2},{2,0},{4,6},{6,4},{1,3},{3,1},{5,7},{7,5},{8,10},{10,8},{12,... | collective-permute-start | bytes 1572872 | tf_op jit(solution)/shard_map/ppermute | solution.py:921
  126.6 23.4 %collective-permute-start.4 = (bf16[512,512]{1,0:T(8,128)(2,1)S(1)}, bf16[512,512]{1,0:T(8,128)(2,1)S(1)}, u32[]{:S(2)}, u32[]{:S(2)}) collective-permute-start(bf16[512,512]{1,0:T(8,128)(2,1)S(1)} %collective-permute-done.refs_4_.refs_1_), channel_id=1, source_target_pairs={{0,2},{2,0},{4,6},{6,4},{1,3},{3,1},{5,7},{7,5},{8,10},{10,8},{12,... | collective-permute-start | bytes 1572872 | tf_op jit(solution)/shard_map/ppermute | solution.py:921
  132.7 15.0 %collective-permute-start.8 = (bf16[256,512]{1,0:T(8,128)(2,1)}, bf16[256,512]{1,0:T(8,128)(2,1)S(1)}, u32[]{:S(2)}, u32[]{:S(2)}) collective-permute-start(bf16[256,512]{1,0:T(8,128)(2,1)} %collective-permute-done.6.refs_7_), channel_id=1, source_target_pairs={{0,2},{2,0},{4,6},{6,4},{1,3},{3,1},{5,7},{7,5},{8,10},{10,8},{12,... | collective-permute-start | bytes 786440 | tf_op jit(solution)/shard_map/ppermute | solution.py:921
  132.7 16.7 %collective-permute-start.7 = (bf16[256,512]{1,0:T(8,128)(2,1)}, bf16[256,512]{1,0:T(8,128)(2,1)}, u32[]{:S(2)}, u32[]{:S(2)}) collective-permute-start(bf16[256,512]{1,0:T(8,128)(2,1)} %collective-permute-done.5.refs_6_), channel_id=1, source_target_pairs={{0,2},{2,0},{4,6},{6,4},{1,3},{3,1},{5,7},{7,5},{8,10},{10,8},{12,... | collective-permute-start | bytes 786440 | tf_op jit(solution)/shard_map/ppermute | solution.py:921
  147.7 39.4 %collective-permute-start.23 = (bf16[4,2,128,256]{3,2,1,0:T(8,128)(2,1)S(1)}, bf16[4,2,128,256]{3,2,1,0:T(8,128)(2,1)S(1)}, u32[]{:S(2)}, u32[]{:S(2)}) collective-permute-start(bf16[4,2,128,256]{3,2,1,0:T(8,128)(2,1)S(1)} %pad_maximum_fusion.9.refs_8_.refs_0_), channel_id=1, source_target_pairs={{0,4},{2,6},{4,0},{6,2},{1,5},{3,7},{5,1},{7,3},{8,12},{10,14},{12... | collective-permute-start | bytes 1572872 | tf_op jit(solution)/shard_map/ppermute | solution.py:921
  149.3 38.8 %collective-permute-start.22 = (bf16[4,2,128,256]{3,2,1,0:T(8,128)(2,1)S(1)}, bf16[4,2,128,256]{3,2,1,0:T(8,128)(2,1)S(1)}, u32[]{:S(2)}, u32[]{:S(2)}) collective-permute-start(bf16[4,2,128,256]{3,2,1,0:T(8,128)(2,1)S(1)} %pad_maximum_fusion.9.refs_8_.refs_0_), channel_id=1, source_target_pairs={{0,2},{2,0},{4,6},{6,4},{1,3},{3,1},{5,7},{7,5},{8,10},{10,8},{12,... | collective-permute-start | bytes 1572872 | tf_op jit(solution)/shard_map/ppermute | solution.py:921
  149.4 70.9 %collective-permute-start.29 = (bf16[4,256,512]{2,1,0:T(8,128)(2,1)S(1)}, bf16[4,256,512]{2,1,0:T(8,128)(2,1)}, u32[]{:S(2)}, u32[]{:S(2)}) collective-permute-start(bf16[4,256,512]{2,1,0:T(8,128)(2,1)S(1)} %pad_maximum_fusion.4.refs_12_), channel_id=1, source_target_pairs={{0,4},{2,6},{4,0},{6,2},{1,5},{3,7},{5,1},{7,3},{8,12},{10,14},{12... | collective-permute-start | bytes 3145736 | tf_op jit(solution)/shard_map/ppermute | solution.py:921
  150.0 70.8 %collective-permute-start.35 = (bf16[4,512,256]{2,1,0:T(8,128)(2,1)S(1)}, bf16[4,512,256]{2,1,0:T(8,128)(2,1)}, u32[]{:S(2)}, u32[]{:S(2)}) collective-permute-start(bf16[4,512,256]{2,1,0:T(8,128)(2,1)S(1)} %pad_maximum_fusion.5.refs_16_), channel_id=1, source_target_pairs={{0,4},{2,6},{4,0},{6,2},{1,5},{3,7},{5,1},{7,3},{8,12},{10,14},{12... | collective-permute-start | bytes 3145736 | tf_op jit(solution)/shard_map/ppermute | solution.py:921
  160.2 29.0 %collective-permute-start.47 = (bf16[512,128]{1,0:T(8,128)(2,1)S(1)}, bf16[512,128]{1,0:T(8,128)(2,1)S(1)}, u32[]{:S(2)}, u32[]{:S(2)}) collective-permute-start(bf16[512,128]{1,0:T(8,128)(2,1)S(1)} %copy-done.97), channel_id=1, source_target_pairs={{0,2},{2,0},{4,6},{6,4},{1,3},{3,1},{5,7},{7,5},{8,10},{10,8},{12,... | collective-permute-start | bytes 393224 | tf_op jit(solution)/shard_map/ppermute | solution.py:921
  187.2 23.1 %collective-permute-start.48 = (bf16[512,128]{1,0:T(8,128)(2,1)S(1)}, bf16[512,128]{1,0:T(8,128)(2,1)S(1)}, u32[]{:S(2)}, u32[]{:S(2)}) collective-permute-start(bf16[512,128]{1,0:T(8,128)(2,1)S(1)} %copy-done.95), channel_id=1, source_target_pairs={{0,4},{2,6},{4,0},{6,2},{1,5},{3,7},{5,1},{7,3},{8,12},{10,14},{12... | collective-permute-start | bytes 393224 | tf_op jit(solution)/shard_map/ppermute | solution.py:921
  188.2 23.1 %collective-permute-start.49 = (bf16[512,128]{1,0:T(8,128)(2,1)S(1)}, bf16[512,128]{1,0:T(8,128)(2,1)S(1)}, u32[]{:S(2)}, u32[]{:S(2)}) collective-permute-start(bf16[512,128]{1,0:T(8,128)(2,1)S(1)} %copy-done.93), channel_id=1, source_target_pairs={{0,6},{2,4},{4,2},{6,0},{1,7},{3,5},{5,3},{7,1},{8,14},{10,12},{12... | collective-permute-start | bytes 393224 | tf_op jit(solution)/shard_map/ppermute | solution.py:921
  189.2 23.7 %collective-permute-start.12 = (bf16[512,128]{1,0:T(8,128)(2,1)}, bf16[512,128]{1,0:T(8,128)(2,1)S(1)}, u32[]{:S(2)}, u32[]{:S(2)}) collective-permute-start(bf16[512,128]{1,0:T(8,128)(2,1)} %get-tuple-element.84), channel_id=1, source_target_pairs={{0,2},{2,0},{4,6},{6,4},{1,3},{3,1},{5,7},{7,5},{8,10},{10,8},{12,... | collective-permute-start | bytes 393224 | tf_op jit(solution)/shard_map/ppermute | solution.py:921
  220.3 16.4 %collective-permute-start.30 = (bf16[4,256,512]{2,1,0:T(8,128)(2,1)}, bf16[4,256,512]{2,1,0:T(8,128)(2,1)S(1)}, u32[]{:S(2)}, u32[]{:S(2)}) collective-permute-start(bf16[4,256,512]{2,1,0:T(8,128)(2,1)} %collective-permute-done.29.refs_14_), channel_id=1, source_target_pairs={{0,2},{2,0},{4,6},{6,4},{1,3},{3,1},{5,7},{7,5},{8,10},{10,8},{12,... | collective-permute-start | bytes 3145736 | tf_op jit(solution)/shard_map/ppermute | solution.py:921
  220.7 17.1 %collective-permute-start.36 = (bf16[4,512,256]{2,1,0:T(8,128)(2,1)}, bf16[4,512,256]{2,1,0:T(8,128)(2,1)}, u32[]{:S(2)}, u32[]{:S(2)}) collective-permute-start(bf16[4,512,256]{2,1,0:T(8,128)(2,1)} %collective-permute-done.35.refs_18_), channel_id=1, source_target_pairs={{0,2},{2,0},{4,6},{6,4},{1,3},{3,1},{5,7},{7,5},{8,10},{10,8},{12,... | collective-permute-start | bytes 3145736 | tf_op jit(solution)/shard_map/ppermute | solution.py:921
  221.9 14.8 %collective-permute-start.15 = (bf16[512,512]{1,0:T(8,128)(2,1)S(1)}, bf16[512,512]{1,0:T(8,128)(2,1)S(1)}, u32[]{:S(2)}, u32[]{:S(2)}) collective-permute-start(bf16[512,512]{1,0:T(8,128)(2,1)S(1)} %constant_dynamic-update-slice_fusion.refs_2_.refs_4_), channel_id=1, source_target_pairs={{0,1},{1,0},{2,3},{3,2},{4,5},{5,4},{6,7},{7,6},{8,9},{9,8},{10,11... | collective-permute-start | bytes 1572872 | tf_op jit(solution)/shard_map/ppermute | solution.py:921
  222.9 33.9 %collective-permute-start.51 = (bf16[512,512]{1,0:T(8,128)(2,1)S(1)}, bf16[512,512]{1,0:T(8,128)(2,1)S(1)}, u32[]{:S(2)}, u32[]{:S(2)}) collective-permute-start(bf16[512,512]{1,0:T(8,128)(2,1)S(1)} %get-tuple-element.199.refs_4_.c_ref.refs_7_), channel_id=1, source_target_pairs={{0,1},{1,0},{2,3},{3,2},{4,5},{5,4},{6,7},{7,6},{8,9},{9,8},{10,11... | collective-permute-start | bytes 1572872 | tf_op jit(solution)/shard_map/ppermute | solution.py:921
  224.3 34.4 %collective-permute-start.50 = (bf16[512,512]{1,0:T(8,128)(2,1)S(1)}, bf16[512,512]{1,0:T(8,128)(2,1)S(1)}, u32[]{:S(2)}, u32[]{:S(2)}) collective-permute-start(bf16[512,512]{1,0:T(8,128)(2,1)S(1)} %constant_dynamic-update-slice_fusion.4.refs_2_.refs_5_), channel_id=1, source_target_pairs={{0,1},{1,0},{2,3},{3,2},{4,5},{5,4},{6,7},{7,6},{8,9},{9,8},{10,11... | collective-permute-start | bytes 1572872 | tf_op jit(solution)/shard_map/ppermute | solution.py:921
  279.4 14.9 %collective-permute-start.37 = (bf16[512,512]{1,0:T(8,128)(2,1)S(1)}, bf16[512,512]{1,0:T(8,128)(2,1)S(1)}, u32[]{:S(2)}, u32[]{:S(2)}) collective-permute-start(bf16[512,512]{1,0:T(8,128)(2,1)S(1)} %copy-done.76), channel_id=1, source_target_pairs={{0,1},{1,0},{2,3},{3,2},{4,5},{5,4},{6,7},{7,6},{8,9},{9,8},{10,11... | collective-permute-start | bytes 1572872 | tf_op jit(solution)/shard_map/ppermute | solution.py:921
  280.2 25.4 %collective-permute-start.52 = (bf16[512,512]{1,0:T(8,128)(2,1)}, bf16[512,512]{1,0:T(8,128)(2,1)S(1)}, u32[]{:S(2)}, u32[]{:S(2)}) collective-permute-start(bf16[512,512]{1,0:T(8,128)(2,1)} %get-tuple-element.99), channel_id=1, source_target_pairs={{0,1},{1,0},{2,3},{3,2},{4,5},{5,4},{6,7},{7,6},{8,9},{9,8},{10,11... | collective-permute-start | bytes 1572872 | tf_op jit(solution)/shard_map/ppermute | solution.py:921
  281.5 46.5 %collective-permute-start.53 = (bf16[512,1024]{1,0:T(8,128)(2,1)}, bf16[512,1024]{1,0:T(8,128)(2,1)S(1)}, u32[]{:S(2)}, u32[]{:S(2)}) collective-permute-start(bf16[512,1024]{1,0:T(8,128)(2,1)} %get-tuple-element.100.gs_ref), channel_id=1, source_target_pairs={{0,1},{1,0},{2,3},{3,2},{4,5},{5,4},{6,7},{7,6},{8,9},{9,8},{10,11... | collective-permute-start | bytes 3145736 | tf_op jit(solution)/shard_map/ppermute | solution.py:921
  282.2 67.0 %collective-permute-start.63 = (bf16[512,1024]{1,0:T(8,128)(2,1)}, bf16[512,1024]{1,0:T(8,128)(2,1)S(1)}, u32[]{:S(2)}, u32[]{:S(2)}) collective-permute-start(bf16[512,1024]{1,0:T(8,128)(2,1)} %get-tuple-element.113.gs_ref), channel_id=1, source_target_pairs={{0,1},{1,0},{2,3},{3,2},{4,5},{5,4},{6,7},{7,6},{8,9},{9,8},{10,11... | collective-permute-start | bytes 3145736 | tf_op jit(solution)/shard_map/ppermute | solution.py:921
  357.6 22.6 %collective-permute-start.96 = (f32[5120]{0:T(1024)S(1)}, f32[5120]{0:T(1024)S(1)}, u32[]{:S(2)}, u32[]{:S(2)}) collective-permute-start(f32[5120]{0:T(1024)S(1)} %constant_dynamic-update-slice_fusion.11), channel_id=1, source_target_pairs={{0,24},{8,16},{16,8},{24,0},{1,25},{9,17},{17,9},{25,1},{2,26},{10... | collective-permute-start | bytes 61448 | tf_op jit(solution)/shard_map/ppermute | solution.py:921
  359.2 21.2 %collective-permute-start.95 = (f32[5120]{0:T(1024)S(1)}, f32[5120]{0:T(1024)S(1)}, u32[]{:S(2)}, u32[]{:S(2)}) collective-permute-start(f32[5120]{0:T(1024)S(1)} %constant_dynamic-update-slice_fusion.11), channel_id=1, source_target_pairs={{0,16},{8,24},{16,0},{24,8},{1,17},{9,25},{17,1},{25,9},{2,18},{10... | collective-permute-start | bytes 61448 | tf_op jit(solution)/shard_map/ppermute | solution.py:921
  361.0 19.9 %collective-permute-start.94 = (f32[5120]{0:T(1024)S(1)}, f32[5120]{0:T(1024)S(1)}, u32[]{:S(2)}, u32[]{:S(2)}) collective-permute-start(f32[5120]{0:T(1024)S(1)} %constant_dynamic-update-slice_fusion.11), channel_id=1, source_target_pairs={{0,8},{8,0},{16,24},{24,16},{1,9},{9,1},{17,25},{25,17},{2,10},{10... | collective-permute-start | bytes 61448 | tf_op jit(solution)/shard_map/ppermute | solution.py:921
  361.3 60.8 %collective-permute-start.54 = (bf16[512,128]{1,0:T(8,128)(2,1)S(1)}, bf16[512,128]{1,0:T(8,128)(2,1)S(1)}, u32[]{:S(2)}, u32[]{:S(2)}) collective-permute-start(bf16[512,128]{1,0:T(8,128)(2,1)S(1)} %copy-done.89), channel_id=1, source_target_pairs={{0,2},{2,0},{4,6},{6,4},{1,3},{3,1},{5,7},{7,5},{8,10},{10,8},{12,... | collective-permute-start | bytes 393224 | tf_op jit(solution)/shard_map/ppermute | solution.py:921
  361.4 62.4 %collective-permute-start.55 = (bf16[512,128]{1,0:T(8,128)(2,1)S(1)}, bf16[512,128]{1,0:T(8,128)(2,1)S(1)}, u32[]{:S(2)}, u32[]{:S(2)}) collective-permute-start(bf16[512,128]{1,0:T(8,128)(2,1)S(1)} %copy-done.88), channel_id=1, source_target_pairs={{0,4},{2,6},{4,0},{6,2},{1,5},{3,7},{5,1},{7,3},{8,12},{10,14},{12... | collective-permute-start | bytes 393224 | tf_op jit(solution)/shard_map/ppermute | solution.py:921
  382.2 41.6 %collective-permute-start.56 = (bf16[512,128]{1,0:T(8,128)(2,1)S(1)}, bf16[512,128]{1,0:T(8,128)(2,1)S(1)}, u32[]{:S(2)}, u32[]{:S(2)}) collective-permute-start(bf16[512,128]{1,0:T(8,128)(2,1)S(1)} %copy-done.87), channel_id=1, source_target_pairs={{0,6},{2,4},{4,2},{6,0},{1,7},{3,5},{5,3},{7,1},{8,14},{10,12},{12... | collective-permute-start | bytes 393224 | tf_op jit(solution)/shard_map/ppermute | solution.py:921
  386.8 131.1 %collective-permute-start.86 = (bf16[2,4,1152,256]{3,2,1,0:T(8,128)(2,1)}, bf16[2,4,1152,256]{3,2,1,0:T(8,128)(2,1)}, u32[]{:S(2)}, u32[]{:S(2)}) collective-permute-start(bf16[2,4,1152,256]{3,2,1,0:T(8,128)(2,1)} %get-tuple-element.141), channel_id=1, source_target_pairs={{0,2},{2,0},{4,6},{6,4},{1,3},{3,1},{5,7},{7,5},{8,10},{10,8},{12,... | collective-permute-start | bytes 14155784 | tf_op jit(solution)/shard_map/ppermute | solution.py:921
  388.4 78.3 %collective-permute-start.99 = (f32[5120]{0:T(1024)S(1)}, f32[5120]{0:T(1024)S(1)}, u32[]{:S(2)}, u32[]{:S(2)}) collective-permute-start(f32[5120]{0:T(1024)S(1)} %add_add_fusion.1), channel_id=1, source_target_pairs={{0,6},{2,4},{4,2},{6,0},{1,7},{3,5},{5,3},{7,1},{8,14},{10,12},{12... | collective-permute-start | bytes 61448 | tf_op jit(solution)/shard_map/ppermute | solution.py:921
  422.1 46.3 %collective-permute-start.98 = (f32[5120]{0:T(1024)S(1)}, f32[5120]{0:T(1024)S(1)}, u32[]{:S(2)}, u32[]{:S(2)}) collective-permute-start(f32[5120]{0:T(1024)S(1)} %add_add_fusion.1), channel_id=1, source_target_pairs={{0,4},{2,6},{4,0},{6,2},{1,5},{3,7},{5,1},{7,3},{8,12},{10,14},{12... | collective-permute-start | bytes 61448 | tf_op jit(solution)/shard_map/ppermute | solution.py:921
  423.8 46.4 %collective-permute-start.97 = (f32[5120]{0:T(1024)S(1)}, f32[5120]{0:T(1024)S(1)}, u32[]{:S(2)}, u32[]{:S(2)}) collective-permute-start(f32[5120]{0:T(1024)S(1)} %add_add_fusion.1), channel_id=1, source_target_pairs={{0,2},{2,0},{4,6},{6,4},{1,3},{3,1},{5,7},{7,5},{8,10},{10,8},{12,... | collective-permute-start | bytes 61448 | tf_op jit(solution)/shard_map/ppermute | solution.py:921
  423.8 72.5 %collective-permute-start.67 = (bf16[4,512,512]{2,1,0:T(8,128)(2,1)}, bf16[4,512,512]{2,1,0:T(8,128)(2,1)}, u32[]{:S(2)}, u32[]{:S(2)}) collective-permute-start(bf16[4,512,512]{2,1,0:T(8,128)(2,1)} %get-tuple-element.125), channel_id=1, source_target_pairs={{0,2},{2,0},{4,6},{6,4},{1,3},{3,1},{5,7},{7,5},{8,10},{10,8},{12,... | collective-permute-start | bytes 6291464 | tf_op jit(solution)/shard_map/ppermute | solution.py:921
  466.7 34.1 %collective-permute-start.57 = (bf16[4,512,512]{2,1,0:T(8,128)(2,1)}, bf16[4,512,512]{2,1,0:T(8,128)(2,1)}, u32[]{:S(2)}, u32[]{:S(2)}) collective-permute-start(bf16[4,512,512]{2,1,0:T(8,128)(2,1)} %get-tuple-element.112), channel_id=1, source_target_pairs={{0,2},{2,0},{4,6},{6,4},{1,3},{3,1},{5,7},{7,5},{8,10},{10,8},{12,... | collective-permute-start | bytes 6291464 | tf_op jit(solution)/shard_map/ppermute | solution.py:921
  470.8 15.9 %collective-permute-start.82 = (bf16[256,384]{1,0:T(8,128)(2,1)S(1)}, bf16[256,384]{1,0:T(8,128)(2,1)S(1)}, u32[]{:S(2)}, u32[]{:S(2)}) collective-permute-start(bf16[256,384]{1,0:T(8,128)(2,1)S(1)} %get-tuple-element.207), channel_id=1, source_target_pairs={{0,24},{8,16},{16,8},{24,0},{1,25},{9,17},{17,9},{25,1},{2,26},{10... | collective-permute-start | bytes 589832 | tf_op jit(solution)/shard_map/ppermute | solution.py:921
  492.4 32.1 %collective-permute-start.83 = (bf16[256,384]{1,0:T(8,128)(2,1)S(1)}, bf16[256,384]{1,0:T(8,128)(2,1)S(1)}, u32[]{:S(2)}, u32[]{:S(2)}) collective-permute-start(bf16[256,384]{1,0:T(8,128)(2,1)S(1)} %fusion.47), channel_id=1, source_target_pairs={{0,2},{2,0},{4,6},{6,4},{1,3},{3,1},{5,7},{7,5},{8,10},{10,8},{12,... | collective-permute-start | bytes 589832 | tf_op jit(solution)/shard_map/ppermute | solution.py:921
  496.3 29.1 %collective-permute-start.85 = (bf16[256,384]{1,0:T(8,128)(2,1)S(1)}, bf16[256,384]{1,0:T(8,128)(2,1)S(1)}, u32[]{:S(2)}, u32[]{:S(2)}) collective-permute-start(bf16[256,384]{1,0:T(8,128)(2,1)S(1)} %collective-permute-done.84), channel_id=1, source_target_pairs={{0,2},{2,0},{4,6},{6,4},{1,3},{3,1},{5,7},{7,5},{8,10},{10,8},{12,... | collective-permute-start | bytes 589832 | tf_op jit(solution)/shard_map/ppermute | solution.py:921
  514.4 18.1 %collective-permute-start.71 = (bf16[512,512]{1,0:T(8,128)(2,1)}, bf16[512,512]{1,0:T(8,128)(2,1)S(1)}, u32[]{:S(2)}, u32[]{:S(2)}) collective-permute-start(bf16[512,512]{1,0:T(8,128)(2,1)} %pad_maximum_fusion.13), channel_id=1, source_target_pairs={{0,1},{1,0},{2,3},{3,2},{4,5},{5,4},{6,7},{7,6},{8,9},{9,8},{10,11... | collective-permute-start | bytes 1572872 | tf_op jit(solution)/shard_map/ppermute | solution.py:921
  517.0 15.6 %collective-permute-start.69 = (bf16[512,512]{1,0:T(8,128)(2,1)}, bf16[512,512]{1,0:T(8,128)(2,1)}, u32[]{:S(2)}, u32[]{:S(2)}) collective-permute-start(bf16[512,512]{1,0:T(8,128)(2,1)} %pad_maximum_fusion.12), channel_id=1, source_target_pairs={{0,4},{2,6},{4,0},{6,2},{1,5},{3,7},{5,1},{7,3},{8,12},{10,14},{12... | collective-permute-start | bytes 1572872 | tf_op jit(solution)/shard_map/ppermute | solution.py:921
  521.5 82.8 %collective-permute-start.87 = (bf16[4,1152,256]{2,1,0:T(8,128)(2,1)}, bf16[4,1152,256]{2,1,0:T(8,128)(2,1)}, u32[]{:S(2)}, u32[]{:S(2)}) collective-permute-start(bf16[4,1152,256]{2,1,0:T(8,128)(2,1)} %fusion.1), channel_id=1, source_target_pairs={{0,4},{2,6},{4,0},{6,2},{1,5},{3,7},{5,1},{7,3},{8,12},{10,14},{12... | collective-permute-start | bytes 7077896 | tf_op jit(solution)/shard_map/ppermute | solution.py:921
  525.4 66.0 %collective-permute-start.59 = (bf16[512,512]{1,0:T(8,128)(2,1)}, bf16[512,512]{1,0:T(8,128)(2,1)}, u32[]{:S(2)}, u32[]{:S(2)}) collective-permute-start(bf16[512,512]{1,0:T(8,128)(2,1)} %pad_maximum_fusion.10), channel_id=1, source_target_pairs={{0,4},{2,6},{4,0},{6,2},{1,5},{3,7},{5,1},{7,3},{8,12},{10,14},{12... | collective-permute-start | bytes 1572872 | tf_op jit(solution)/shard_map/ppermute | solution.py:921
  594.7 62.9 %collective-permute-start.75 = (f32[2560]{0:T(1024)S(1)}, f32[2560]{0:T(1024)S(1)}, u32[]{:S(2)}, u32[]{:S(2)}) collective-permute-start(f32[2560]{0:T(1024)S(1)} %pad_maximum_fusion.15), channel_id=1, source_target_pairs={{0,24},{8,16},{16,8},{24,0},{1,25},{9,17},{17,9},{25,1},{2,26},{10... | collective-permute-start | bytes 30728 | tf_op jit(solution)/shard_map/ppermute | solution.py:921
  595.4 62.2 %collective-permute-start.74 = (f32[2560]{0:T(1024)S(1)}, f32[2560]{0:T(1024)S(1)}, u32[]{:S(2)}, u32[]{:S(2)}) collective-permute-start(f32[2560]{0:T(1024)S(1)} %pad_maximum_fusion.15), channel_id=1, source_target_pairs={{0,16},{8,24},{16,0},{24,8},{1,17},{9,25},{17,1},{25,9},{2,18},{10... | collective-permute-start | bytes 30728 | tf_op jit(solution)/shard_map/ppermute | solution.py:921
  608.5 20.3 %collective-permute-start.88 = (bf16[1152,256]{1,0:T(8,128)(2,1)S(1)}, bf16[1152,256]{1,0:T(8,128)(2,1)S(1)}, u32[]{:S(2)}, u32[]{:S(2)}) collective-permute-start(bf16[1152,256]{1,0:T(8,128)(2,1)S(1)} %get-tuple-element.193), channel_id=1, source_target_pairs={{0,8},{8,0},{16,24},{24,16},{1,9},{9,1},{17,25},{25,17},{2,10},{10... | collective-permute-start | bytes 1769480 | tf_op jit(solution)/shard_map/ppermute | solution.py:921
  608.6 41.6 %collective-permute-start.90 = (bf16[1152,256]{1,0:T(8,128)(2,1)S(1)}, bf16[1152,256]{1,0:T(8,128)(2,1)S(1)}, u32[]{:S(2)}, u32[]{:S(2)}) collective-permute-start(bf16[1152,256]{1,0:T(8,128)(2,1)S(1)} %get-tuple-element.194), channel_id=1, source_target_pairs={{0,24},{8,16},{16,8},{24,0},{1,25},{9,17},{17,9},{25,1},{2,26},{10... | collective-permute-start | bytes 1769480 | tf_op jit(solution)/shard_map/ppermute | solution.py:921
  610.1 46.2 %collective-permute-start.89 = (bf16[1152,256]{1,0:T(8,128)(2,1)S(1)}, bf16[1152,256]{1,0:T(8,128)(2,1)S(1)}, u32[]{:S(2)}, u32[]{:S(2)}) collective-permute-start(bf16[1152,256]{1,0:T(8,128)(2,1)S(1)} %get-tuple-element.195), channel_id=1, source_target_pairs={{0,16},{8,24},{16,0},{24,8},{1,17},{9,25},{17,1},{25,9},{2,18},{10... | collective-permute-start | bytes 1769480 | tf_op jit(solution)/shard_map/ppermute | solution.py:921
  628.7 28.9 %collective-permute-start.73 = (f32[2560]{0:T(1024)S(1)}, f32[2560]{0:T(1024)S(1)}, u32[]{:S(2)}, u32[]{:S(2)}) collective-permute-start(f32[2560]{0:T(1024)S(1)} %pad_maximum_fusion.15), channel_id=1, source_target_pairs={{0,8},{8,0},{16,24},{24,16},{1,9},{9,1},{17,25},{25,17},{2,10},{10... | collective-permute-start | bytes 30728 | tf_op jit(solution)/shard_map/ppermute | solution.py:921
  (140 other events, 2175.5 us)

commit v2 on v0

--- a/solution.py
+++ b/solution.py
@@ -1,8 +1,11 @@
+import functools
 import math
 
 import jax
 import jax.numpy as jnp
 from jax import lax
+from jax.experimental import pallas as pl
+from jax.experimental.pallas import tpu as pltpu
 from jax.sharding import PartitionSpec as P
 
 HEAD_DIM = 64
@@ -412,6 +415,1024 @@
     )
 
 
+LOG2E = 1.4426950408889634
+BF = jnp.bfloat16
+F32 = jnp.float32
+VMEM_BYTES = 56 * 2**20
+
+
+def dot_nt(a, b):
+    return lax.dot_general(a, b, (((1,), (1,)), ((), ())), preferred_element_type=F32)
+
+
+def dot_nn(a, b):
+    return lax.dot_general(a, b, (((1,), (0,)), ((), ())), preferred_element_type=F32)
+
+
+def dot_tn(a, b):
+    return lax.dot_general(a, b, (((0,), (0,)), ((), ())), preferred_element_type=F32)
+
+
+def whole(shape):
+    return pl.BlockSpec(shape, lambda *_: (0,) * len(shape))
+
+
+SMEM = pl.BlockSpec(memory_space=pltpu.SMEM)
+
+
+def call(body, args, outs, name, scratch=(), flops=0, grid=None, in_specs=None, out_specs=None):
+    shapes = [jax.ShapeDtypeStruct(shape, kind) for shape, kind in outs]
+    moved = sum(a.size * a.dtype.itemsize for a in args)
+    moved += sum(math.prod(s.shape) * jnp.dtype(s.dtype).itemsize for s in shapes)
+    extra = {} if grid is None else {"grid": grid}
+    return pl.pallas_call(
+        body,
+        in_specs=in_specs or [SMEM] + [whole(a.shape) for a in args[1:]],
+        out_specs=out_specs or [whole(s.shape) for s in shapes],
+        out_shape=shapes,
+        scratch_shapes=list(scratch),
+        compiler_params=pltpu.CompilerParams(vmem_limit_bytes=VMEM_BYTES),
+        cost_estimate=pl.CostEstimate(
+            flops=int(flops), bytes_accessed=int(moved), transcendentals=0
+        ),
+        name=name,
+        **extra,
+    )(*args)
+
+
+def piece_index(ids_ref, half, part):
+    shard, tp = ids_ref[0], ids_ref[2]
+    return shard ^ (2 * (tp ^ half) + part)
+
+
+CHUNKS = ((0, 0), (0, 1), (1, 0), (1, 1))
+
+
+def partner_lanes(tensor):
+    segment = 2 * (HEAD_DIM // 3 // 2)
+    halfway = segment // 2
+    width = tensor.shape[1]
+    lane = lax.broadcasted_iota(jnp.int32, tensor.shape, 1) % HEAD_DIM
+    first = lane % segment < halfway
+    return jnp.where(
+        first, pltpu.roll(tensor, width - halfway, 1), pltpu.roll(tensor, halfway, 1)
+    )
+
+
+def norm_parts(own, other):
+    total = 2 * own.shape[1]
+    mean = (jnp.sum(own, 1, keepdims=True) + jnp.sum(other, 1, keepdims=True)) / total
+    own, other = own - mean, other - mean
+    spread = (
+        jnp.sum(own * own, 1, keepdims=True) + jnp.sum(other * other, 1, keepdims=True)
+    ) / total
+    inv = lax.rsqrt(spread + EPSILON)
+    return own * inv, other * inv, inv
+
+
+def attend_back_body(rows, q_ref, k_ref, v_ref, d0, d1, d2, d3, ot_ref, lse_ref, *refs):
+    dq_ref, dk_ref, dv_ref, qh_ref, dh_ref, delta_ref, dqt_ref = refs
+    step = pl.program_id(0)
+    count, width = q_ref.shape
+    heads = width // HEAD_DIM
+    scale = HEAD_DIM ** (-0.5)
+
+    @pl.when(step == 0)
+    def _():
+        quarter = count // 4
+        head = lax.broadcasted_iota(jnp.int32, (quarter, width), 1) // HEAD_DIM
+        for m, d_ref in enumerate((d0, d1, d2, d3)):
+            part = slice(m * quarter, (m + 1) * quarter)
+            q, d = q_ref[part, :], d_ref[...]
+            for h in range(heads):
+                qh_ref[h, part, :] = jnp.where(head == h, q, jnp.zeros_like(q))
+                dh_ref[h, part, :] = jnp.where(head == h, d, jnp.zeros_like(d))
+            products = d.astype(F32).T * ot_ref[:, part]
+            for h in range(heads):
+                delta_ref[h : h + 1, part] = jnp.sum(
+                    products[h * HEAD_DIM : (h + 1) * HEAD_DIM], axis=0, keepdims=True
+                )
+        dqt_ref[...] = jnp.zeros_like(dqt_ref)
+
+    keys, values = k_ref[...], v_ref[...]
+    turned = keys.T
+    row = lax.broadcasted_iota(jnp.int32, turned.shape, 0) // HEAD_DIM
+    dk = dv = None
+    for h in range(heads):
+        turned_head = jnp.where(row == h, turned, jnp.zeros_like(turned))
+        for start in range(0, count, rows):
+            part = slice(start, start + rows)
+            q, d = qh_ref[h, part, :], dh_ref[h, part, :]
+            probs = jnp.exp2(dot_nt(keys, q) * (scale * LOG2E) - lse_ref[h : h + 1, part])
+            grad = (probs * (dot_nt(values, d) - delta_ref[h : h + 1, part])).astype(BF)
+            value_term, key_term = dot_nn(probs.astype(BF), d), dot_nn(grad, q)
+            dk = key_term if dk is None else dk + key_term
+            dv = value_term if dv is None else dv + value_term
+            dqt_ref[:, part] += dot_nn(turned_head, grad)
+    dk_ref[...] = dk * scale
+    dv_ref[...] = dv
+
+    @pl.when(step == pl.num_programs(0) - 1)
+    def _():
+        dq_ref[...] = (dqt_ref[...] * scale).T
+
+
+def attend_back_call(q, k, v, d, ot, lse):
+    count, width = q.shape
+    heads = width // HEAD_DIM
+    rows = 512
+    block = 512
+    part = pl.BlockSpec((block, width), lambda i: (i, 0))
+    return call(
+        functools.partial(attend_back_body, rows),
+        [q, k, v, *d, ot, lse],
+        [((count, width), F32)] * 3,
+        "attend_back",
+        scratch=[
+            pltpu.VMEM((heads, count, width), BF),
+            pltpu.VMEM((heads, count, width), BF),
+            pltpu.VMEM((heads, count), F32),
+            pltpu.VMEM((width, count), F32),
+        ],
+        grid=(count // block,),
+        in_specs=[whole(q.shape), part, part]
+        + [whole(d[0].shape)] * 4
+        + [whole(ot.shape), whole(lse.shape)],
+        out_specs=[whole(q.shape), part, part],
+        flops=10 * count * count * 256 * heads,
+    )
+
+
+def joined_body(ids_ref, dq_ref, dk_ref, dv_ref, cos_ref, sin_ref, w_ref, *refs):
+    gj_ref, keep_ref, send_ref, sums_ref = refs
+    lanes = dq_ref.shape[2]
+    half = keep_ref.shape[2]
+    width = half // 2
+    sums = [0.0, 0.0, 0.0]
+    for m in range(4):
+        cosines, sines = cos_ref[m], sin_ref[m]
+        dq, dk = dq_ref[m], dk_ref[m]
+        parts = (
+            dq * cosines + partner_lanes(dq * sines),
+            dk * cosines + partner_lanes(dk * sines),
+            dv_ref[m],
+        )
+        for i, part in enumerate(parts):
+            low = part.astype(BF)
+            gj_ref[m, :, i * lanes : (i + 1) * lanes] = low
+            sums[i] = sums[i] + jnp.sum(low.astype(F32), axis=0, keepdims=True)
+    for i in range(3):
+        sums_ref[i : i + 1, :] = sums[i]
+    for m in range(4):
+        target = (keep_ref, send_ref)[m % 2]
+        for h, j in CHUNKS:
+            term = dot_nt(gj_ref[m], w_ref[piece_index(ids_ref, h, j)])
+            target[2 * (m // 2) + h, :, j * width : (j + 1) * width] = term.astype(BF)
+
+
+def joined_call(ids, dq, dk, dv, cosines, sines, w):
+    four, rows, lanes = dq.shape
+    half = 2 * w.shape[1]
+    return call(
+        joined_body,
+        [ids, dq, dk, dv, cosines, sines, w],
+        [
+            ((4, rows, 3 * lanes), BF),
+            ((4, rows, half), BF),
+            ((4, rows, half), BF),
+            ((3, lanes), F32),
+        ],
+        "joined_back",
+        flops=2 * 4 * rows * 3 * lanes * 2 * half * 2,
+    )
+
+
+def qkv_grad_body(ids_ref, na_ref, ga_ref, nb_ref, gb_ref, out_ref):
+    width = out_ref.shape[1]
+    for h, j in CHUNKS:
+        at = (2 * h + j) * width
+        total = dot_tn(na_ref[:, at : at + width], ga_ref[...]) + dot_tn(
+            nb_ref[:, at : at + width], gb_ref[...]
+        )
+        out_ref[piece_index(ids_ref, h, j)] = total.astype(BF)
+
+
+def flip(value, bit):
+    if bit == 1:
+        return value + 1 - 2 * lax.rem(value, 2)
+    return lax.rem(value + 2, 4)
+
+
+def place():
+    return tuple(lax.axis_index(name) for name in ("shard", "ctx", "tp"))
+
+
+def piece_at(shard, tp, half, part):
+    found = lax.rem(shard + 2 * lax.rem(tp + half, 2), 4)
+    return flip(found, 1) if part else found
+
+
+class Movers:
+    def __init__(self, send_sems, recv_sems, local_sems):
+        shard, ctx, tp = place()
+        self.sems = (send_sems, recv_sems, local_sems)
+        self.sent, self.kept = [], []
+        self.partners = {
+            "x": {"tp": 1 - tp},
+            "core": {"ctx": flip(ctx, 1)},
+            "y": {"ctx": flip(ctx, 2)},
+            "ycore": {"ctx": flip(flip(ctx, 2), 1)},
+            "z1": {"shard": flip(shard, 1)},
+            "z2": {"shard": flip(shard, 2)},
+            "z3": {"shard": flip(flip(shard, 2), 1)},
+        }
+
+    def barrier(self, names):
+        barrier = pltpu.get_barrier_semaphore()
+        for name in names:
+            pl.semaphore_signal(
+                barrier,
+                inc=1,
+                device_id=self.partners[name],
+                device_id_type=pl.DeviceIdType.MESH,
+            )
+        pl.semaphore_wait(barrier, len(names))
+
+    def send(self, source, target, name):
+        at = len(self.sent)
+        copy = pltpu.make_async_remote_copy(
+            src_ref=source,
+            dst_ref=target,
+            send_sem=self.sems[0].at[at],
+            recv_sem=self.sems[1].at[at],
+            device_id=self.partners[name],
+            device_id_type=pl.DeviceIdType.MESH,
+        )
+        copy.start()
+        self.sent.append([copy, False])
+        return at
+
+    def arrive(self, *which):
+        for at in which:
+            if not self.sent[at][1]:
+                self.sent[at][0].wait_recv()
+                self.sent[at][1] = True
+
+    def keep(self, source, target):
+        at = len(self.kept)
+        copy = pltpu.make_async_copy(source, target, self.sems[2].at[at])
+        copy.start()
+        self.kept.append([copy, False])
+        return at
+
+    def kept_done(self, *which):
+        for at in which:
+            if not self.kept[at][1]:
+                self.kept[at][0].wait()
+                self.kept[at][1] = True
+
+    def finish(self):
+        self.arrive(*range(len(self.sent)))
+        for copy, _ in self.sent:
+            copy.wait_send()
+        self.kept_done(*range(len(self.kept)))
+
+
+def first_body(*refs):
+    (x_ref, cot_ref, wq_piece, wout_ref, win_ref, wback_ref, b_ref, ln_ref, bout_ref) = refs[:9]
+    (xp_out, cp_out, n_out, qkv_out, ot_out, lse_out, mo_out, mp_out, wq_out, wo, wi, wb, boutp_out, table_out) = refs[
+        9:23
+    ]
+    (xall, nbuf, qkv, ot, vt, osc, wq, tables, send_sems, recv_sems, local_sems) = refs[23:]
+    clips, rows, half = x_ref.shape
+    width = half // 2
+    lanes = tables.shape[3]
+    hidden = wi.shape[3]
+    shard, ctx, tp = place()
+    mv = Movers(send_sems, recv_sems, local_sems)
+    mv.barrier(["x", "core", "y", "ycore", "z1", "z2", "z3"])
+    zs = ("z1", "z2", "z3")
+    cut = rows // 2
+
+    x0 = [mv.send(x_ref.at[0], xall.at[0, 1, 0], "x")]
+    y0 = [mv.send(x_ref.at[0], xall.at[0, 0, 2], "y")]
+    wqz = [mv.send(wq_piece, wq.at[k + 1], name) for k, name in enumerate(zs)]
+    c0 = [mv.send(x_ref.at[0], xall.at[0, 0, 1], "core")]
+    own = [mv.keep(x_ref.at[b], xall.at[b, 0, 0]) for b in range(clips)]
+    wq_own = mv.keep(wq_piece, wq.at[0])
+    out_piece = wout_ref.at[pl.ds(pl.multiple_of(ctx * lanes, lanes), lanes), :]
+    back_piece = wback_ref.at[pl.ds(pl.multiple_of(ctx * hidden, hidden), hidden), :]
+    far_ctx = flip(ctx, 2)
+    in_pieces = [
+        win_ref.at[:, pl.ds(pl.multiple_of(at * hidden, hidden), hidden)] for at in (ctx, far_ctx)
+    ]
+    wo_x = mv.send(out_piece, wo.at[0, 0, 1], "x")
+    mv.send(bout_ref, boutp_out, "x")
+    wo_own = mv.keep(out_piece, wo.at[0, 0, 0])
+    wi_own = [mv.keep(in_pieces[i], wi.at[2 * i, 0]) for i in range(2)]
+    wb_own = mv.keep(back_piece, wb.at[0, 0])
+
+    def forward(b, x, y):
+        mv.arrive(x)
+        low = mv.send(xall.at[b, 1, 0, :cut], xall.at[b, 1, 2, :cut], "y")
+        near = [mv.send(xall.at[b, 1, 0], xall.at[b, 1, 1], "core")]
+        mv.arrive(y)
+        high = mv.send(xall.at[b, 0, 2, cut:], xall.at[b, 1, 2, cut:], "x")
+        near.append(mv.send(xall.at[b, 0, 2], xall.at[b, 0, 3], "core"))
+        return low, high, near
+
+    def project(b, m):
+        slot = m % 2
+        for start in range(0, rows, cut):
+            part = slice(start, start + cut)
+            one, two, unused = norm_parts(
+                xall[b, 0, m, part, :].astype(F32), xall[b, 1, m, part, :].astype(F32)
+            )
+            nbuf[slot, part, :half] = (one * ln_ref[0:1, :half] + ln_ref[1:2, :half]).astype(BF)
+            nbuf[slot, part, half:] = (two * ln_ref[0:1, half:] + ln_ref[1:2, half:]).astype(BF)
+        acc = b_ref[...]
+        for h, j in CHUNKS:
+            at = (2 * h + j) * width
+            acc = acc + dot_nn(nbuf[slot, :, at : at + width], wq[piece_at(shard, tp, h, j)])
+        cosines, sines = tables[0, m], tables[1, m]
+        q, k = acc[:, :lanes], acc[:, lanes : 2 * lanes]
+        place_rows = slice(m * rows, (m + 1) * rows)
+        qkv[b, 0, place_rows, :] = (q * cosines + partner_lanes(q) * sines).astype(BF)
+        qkv[b, 1, place_rows, :] = (k * cosines + partner_lanes(k) * sines).astype(BF)
+        qkv[b, 2, place_rows, :] = acc[:, 2 * lanes :].astype(BF)
+        return mv.keep(nbuf.at[slot], n_out.at[b, m])
+
+    scale = HEAD_DIM ** (-0.5) * LOG2E
+    head = lax.broadcasted_iota(jnp.int32, (rows, lanes), 1) // HEAD_DIM
+
+    def turn_values(b):
+        vt[:lanes, :] = qkv[b, 2].T
+        vt[lanes:, :] = jnp.ones((vt.shape[0] - lanes, 4 * rows), BF)
+
+    def attend(b, m):
+        part = slice(m * rows, (m + 1) * rows)
+        q = qkv[b, 0, part, :]
+        keys = qkv[b, 1]
+        outs = []
+        for h in range(lanes // HEAD_DIM):
+            q_head = jnp.where(head == h, q, jnp.zeros_like(q))
+            scores = dot_nt(keys, q_head)
+            top = jnp.max(scores, axis=0, keepdims=True) * scale
+            probs = jnp.exp2(scores * scale - top).astype(BF)
+            acc = dot_nn(vt[...], probs)
+            total = acc[lanes : lanes + 1, :]
+            outs.append(acc[h * HEAD_DIM : (h + 1) * HEAD_DIM, :] / total)
+            lse_out[b, h : h + 1, part] = top + jnp.log2(total)
+        result = jnp.concatenate(outs, axis=0)
+        ot[b, :, part] = result
+        osc[b, m] = result.T.astype(BF)
+        if m == 0:
+            return mv.keep(osc.at[b, 0], mo_out.at[b, 0])
+        return mv.send(osc.at[b, m], mo_out.at[b, m], ("", "core", "y", "ycore")[m])
+
+    token = lax.broadcasted_iota(jnp.int32, (rows, lanes), 0)
+    column = lax.broadcasted_iota(jnp.int32, (rows, lanes), 1) % HEAD_DIM
+    segment = 2 * (HEAD_DIM // 3 // 2)
+    halfway = segment // 2
+    within = column % segment
+    frequency = jnp.exp(
+        (within % halfway).astype(F32) * (-math.log(10000.0) / halfway)
+    )
+    sign = jnp.where(within < halfway, -1.0, 1.0)
+    active = column < 3 * segment
+
+    def turn(position):
+        angle = position.astype(F32) * frequency
+        return jnp.where(active, jnp.cos(angle), 1.0), jnp.where(active, jnp.sin(angle) * sign, 0.0)
+
+    def turn_frame(frame):
+        angle = frame.astype(F32) * frequency[:8]
+        cosine, sine = jnp.cos(angle)[:1], (jnp.sin(angle) * sign[:8])[:1]
+        return cosine, sine
+
+    start = [at * rows for at in (ctx, flip(ctx, 1), flip(ctx, 2), flip(flip(ctx, 2), 1))]
+    if rows % (GH * GW) == 0:
+        tables_in = turn(
+            jnp.where(column < 2 * segment, token // GW % GH, token % GW)
+        )
+        for m in range(4):
+            for at in range(0, rows, GH * GW):
+                part = slice(at, at + GH * GW)
+                frame = turn_frame((start[m] + at) // (GH * GW))
+                first = column[part] < segment
+                for i in range(2):
+                    tables[i, m, part, :] = jnp.where(first, frame[i], tables_in[i][part])
+    else:
+        for m in range(4):
+            at = start[m] + token
+            both = turn(
+                jnp.where(
+                    column < segment,
+                    at // (GH * GW),
+                    jnp.where(column < 2 * segment, at // GW % GH, at % GW),
+                )
+            )
+            for i in range(2):
+                tables[i, m] = both[i]
+    mv.keep(tables, table_out)
+
+    low0, high0, near0 = forward(0, x0[0], y0[0])
+    x1 = mv.send(x_ref.at[1], xall.at[1, 1, 0], "x")
+    y1 = mv.send(x_ref.at[1], xall.at[1, 0, 2], "y")
+    c1 = mv.send(x_ref.at[1], xall.at[1, 0, 1], "core")
+    mv.keep(xall.at[0, 1, 0], xp_out.at[0])
+    mv.arrive(*wqz)
+    wbz = [mv.send(back_piece, wb.at[0, k + 1], name) for k, name in enumerate(zs)]
+    mv.kept_done(own[0], wq_own)
+    mv.keep(wq, wq_out)
+    n_copy = [project(0, 0)]
+    mv.arrive(c0[0], near0[0])
+    n_copy.append(project(0, 1))
+    mv.arrive(low0, high0)
+    near0.append(mv.send(xall.at[0, 1, 2], xall.at[0, 1, 3], "core"))
+    mv.kept_done(n_copy[0])
+    n_copy.append(project(0, 2))
+    mv.arrive(wo_x)
+    mv.kept_done(wo_own)
+    woz = [mv.send(wo.at[0, 0], wo.at[0, k + 1], name) for k, name in enumerate(zs)]
+    mv.arrive(near0[1], near0[2])
+    mv.kept_done(n_copy[1])
+    n_copy.append(project(0, 3))
+    mv.keep(qkv.at[0], qkv_out.at[0])
+    low1, high1, near1 = forward(1, x1, y1)
+    mv.keep(xall.at[1, 1, 0], xp_out.at[1])
+    cots = [mv.send(cot_ref.at[b], cp_out.at[b], "x") for b in range(clips)]
+    turn_values(0)
+    m0 = {2: attend(0, 2)}
+    mv.arrive(low1, high1)
+    near1.append(mv.send(xall.at[1, 1, 2], xall.at[1, 1, 3], "core"))
+    mv.arrive(*wbz)
+    mv.kept_done(wb_own)
+    wiz = [
+        mv.send(in_pieces[i], wi.at[2 * i, k + 1], name)
+        for i in range(2)
+        for k, name in enumerate(zs)
+    ]
+    wb_far = mv.send(wb.at[0], wb.at[2], "y")
+    mv.send(wb.at[0], wb.at[1], "core")
+    m0[3] = attend(0, 3)
+    mv.arrive(*woz)
+    wo_far = mv.send(wo.at[0], wo.at[2], "y")
+    mv.send(wo.at[0], wo.at[1], "core")
+    m0[1] = attend(0, 1)
+    m0[0] = attend(0, 0)
+    mv.keep(ot.at[0], ot_out.at[0])
+    mv.arrive(c1, *near1)
+    mv.kept_done(own[1], n_copy[2])
+    n_copy.append(project(1, 0))
+    mv.arrive(m0[2], m0[1], m0[3])
+    mv.kept_done(m0[0])
+    mv.send(mo_out.at[0], mp_out.at[0], "x")
+    mv.kept_done(n_copy[3])
+    n_copy.append(project(1, 1))
+    mv.kept_done(n_copy[4])
+    n_copy.append(project(1, 2))
+    mv.kept_done(n_copy[5])
+    n_copy.append(project(1, 3))
+    mv.keep(qkv.at[1], qkv_out.at[1])
+    turn_values(1)
+    m1 = {2: attend(1, 2)}
+    m1[3] = attend(1, 3)
+    mv.arrive(wb_far)
+    mv.send(wb.at[2], wb.at[3], "core")
+    mv.arrive(wo_far)
+    mv.send(wo.at[2], wo.at[3], "core")
+    m1[1] = attend(1, 1)
+    mv.arrive(*wiz[:3])
+    mv.kept_done(wi_own[0])
+    mv.send(wi.at[0], wi.at[1], "core")
+    m1[0] = attend(1, 0)
+    mv.keep(ot.at[1], ot_out.at[1])
+    mv.kept_done(m1[0])
+    mv.send(mo_out.at[1, 0], mp_out.at[1, 0], "x")
+    for m in (1, 2, 3):
+        mv.arrive(m1[m])
+        mv.send(mo_out.at[1, m], mp_out.at[1, m], "x")
+    mv.arrive(*wiz[3:])
+    mv.kept_done(wi_own[1])
+    mv.send(wi.at[2], wi.at[3], "core")
+    mv.finish()
+
+
+ANY = pl.BlockSpec(memory_space=pl.ANY)
+
+
+def first_call(x, cot, wq_piece, w_out, w_in, w_back, b, ln, b_out):
+    clips, rows, half = x.shape
+    width = half // 2
+    lanes = wq_piece.shape[1] // 3
+    hidden = w_in.shape[1] // 4
+    outs = [
+        ((clips, rows, half), BF),
+        ((clips, rows, half), BF),
+        ((clips, 4, rows, 2 * half), BF),
+        ((clips, 3, 4 * rows, lanes), BF),
+        ((clips, lanes, 4 * rows), F32),
+        ((clips, lanes // HEAD_DIM, 4 * rows), F32),
+        ((clips, 4, rows, lanes), BF),
+        ((clips, 4, rows, lanes), BF),
+        ((4, width, 3 * lanes), BF),
+        ((4, 4, 2, lanes, width), BF),
+        ((4, 4, width, hidden), BF),
+        ((4, 4, hidden, width), BF),
+        (b_out.shape, BF),
+        ((2, 4, rows, lanes), F32),
+    ]
+    out_specs = [ANY] * len(outs)
+    out_specs[5] = whole(outs[5][0])
+    return pl.pallas_call(
+        first_body,
+        in_specs=[ANY] * 6 + [whole(b.shape), whole(ln.shape), ANY],
+        out_specs=out_specs,
+        out_shape=[jax.ShapeDtypeStruct(shape, kind) for shape, kind in outs],
+        scratch_shapes=[
+            pltpu.VMEM((clips, 2, 4, rows, half), BF),
+            pltpu.VMEM((2, rows, 2 * half), BF),
+            pltpu.VMEM((clips, 3, 4 * rows, lanes), BF),
+            pltpu.VMEM((clips, lanes, 4 * rows), F32),
+            pltpu.VMEM((lanes + 16, 4 * rows), BF),
+            pltpu.VMEM((clips, 4, rows, lanes), BF),
+            pltpu.VMEM((4, width, 3 * lanes), BF),
+            pltpu.VMEM((2, 4, rows, lanes), F32),
+            pltpu.SemaphoreType.DMA((64,)),
+            pltpu.SemaphoreType.DMA((64,)),
+            pltpu.SemaphoreType.DMA((40,)),
+        ],
+        compiler_params=pltpu.CompilerParams(
+            vmem_limit_bytes=VMEM_BYTES, collective_id=1, has_side_effects=True
+        ),
+        name="project_and_attend",
+    )(x, cot, wq_piece, w_out, w_in, w_back, b, ln, b_out)
+
+
+def chunk_of(shard, k):
+    found = flip(shard, 2) if k & 2 else shard
+    return flip(found, 1) if k & 1 else found
+
+
+def side_by_side(parts):
+    return jnp.concatenate(parts, axis=1)
+
+
+def second_body(*refs):
+    (x_ref, xp_ref, c_ref, cp_ref, mo_ref, mp_ref, wo_hbm, wi_hbm, wb_hbm) = refs[:9]
+    (ln_ref, bin_ref, bout_ref, boutp_ref, bback_ref) = refs[9:14]
+    (y_out, gmid_out, d_out, g_out, go_out, midsum_out, insum_out, backsum_out) = refs[14:22]
+    (xs, cs, ms, wo, wi, wb, mid, sec, act, gin, outs, outr, gs, gsr, gmid, gb, gm) = refs[22:39]
+    (wg, wgo, turned, send_sems, recv_sems, local_sems) = refs[39:]
+    clips, rows, half = x_ref.shape
+    width = half // 2
+    lanes = mo_ref.shape[3]
+    hidden = wi.shape[3]
+    shard, ctx, tp = place()
+    mv = Movers(send_sems, recv_sems, local_sems)
+    ks = range(4)
+    own_k = [piece_at(shard, tp, 0, j) for j in range(2)]
+    other_k = [piece_at(shard, tp, 1, j) for j in range(2)]
+
+    def fetch(b):
+        return [
+            mv.keep(mo_ref.at[b], ms.at[b, 0]),
+            mv.keep(mp_ref.at[b], ms.at[b, 1]),
+            mv.keep(x_ref.at[b], xs.at[b, 0]),
+            mv.keep(xp_ref.at[b], xs.at[b, 1]),
+            mv.keep(c_ref.at[b], cs.at[b, 0]),
+            mv.keep(cp_ref.at[b], cs.at[b, 1]),
+        ]
+
+    got = [fetch(0)]
+    got_wo = mv.keep(wo_hbm, wo)
+    got_wi = [mv.keep(wi_hbm.at[m], wi.at[m]) for m in ks]
+    got_wb = [mv.keep(wb_hbm.at[m], wb.at[m]) for m in ks]
+    got.append(fetch(1))
+    mv.barrier(["x", "core", "y", "ycore"])
+
+    def row(which, k):
+        return ln_ref[pl.ds(4 * which + chunk_of(shard, k), 1), :]
+
+    def statistics(b):
+        total = 4 * width
+        mean = sum(jnp.sum(mid[b, k], 1, keepdims=True) for k in ks) / total
+        spread = sum(jnp.sum((mid[b, k] - mean) ** 2, 1, keepdims=True) for k in ks) / total
+        return mean, lax.rsqrt(spread + EPSILON)
+
+    def block(b):
+        mv.kept_done(*got[b])
+        mv.kept_done(got_wo)
+        mixed = side_by_side([ms[b, side, m] for side in range(2) for m in ks])
+        for k in ks:
+            weight = jnp.concatenate([wo[m, k, side] for side in range(2) for m in ks], axis=0)
+            mid[b, k] = dot_nn(mixed, weight)
+        for j in range(2):
+            part = slice(j * width, (j + 1) * width)
+            mid[b, own_k[j]] += xs[b, 0, :, part].astype(F32) + bout_ref[0:1, part].astype(F32)
+            mid[b, other_k[j]] += xs[b, 1, :, part].astype(F32) + boutp_ref[0:1, part].astype(F32)
+        mean, inv = statistics(b)
+        for k in ks:
+            sec[b, k] = ((mid[b, k] - mean) * inv * row(0, k) + row(1, k)).astype(BF)
+        for j in range(2):
+            part = slice(j * width, (j + 1) * width)
+            gb[b, own_k[j]] = cs[b, 0, :, part]
+            gb[b, other_k[j]] = cs[b, 1, :, part]
+        normed = side_by_side([sec[b, k] for k in ks])
+        cot = side_by_side([gb[b, k] for k in ks])
+        for m in ks:
+            mv.kept_done(got_wi[m])
+            at = (ctx, flip(ctx, 1), flip(ctx, 2), flip(flip(ctx, 2), 1))[m]
+            inner = bin_ref[pl.ds(at, 1), :] + dot_nn(normed, wi[m].reshape(4 * width, hidden))
+            mv.kept_done(got_wb[m])
+            grad = dot_nt(cot, side_by_side([wb[m, k] for k in ks]))
+            phi = 0.5 + 0.5 * lax.erf(inner * (0.5**0.5))
+            act[b, m] = (inner * phi).astype(BF)
+            slope = phi + inner * (jnp.exp(-0.5 * inner * inner) * ((2 * math.pi) ** -0.5))
+            grad = (grad * slope).astype(BF)
+            gin[b, m] = grad
+            sums = jnp.sum(grad.astype(F32), axis=0, keepdims=True)
+            if b == 0:
+                insum_out[pl.ds(at, 1), :] = sums
+            else:
+                insum_out[pl.ds(at, 1), :] += sums
+        back = side_by_side([gin[b, m] for m in ks])
+        sent = []
+        for k in ks:
+            gs[b, k] = dot_nt(back, side_by_side([wi[m, k] for m in ks])).astype(BF)
+            sent.append(mv.send(gs.at[b, k], gsr.at[b, k], "x"))
+        active = side_by_side([act[b, m] for m in ks])
+        for h, which in enumerate((own_k, other_k)):
+            for j in range(2):
+                weight = jnp.concatenate([wb[m, which[j]] for m in ks], axis=0)
+                outs[b, h, :, j * width : (j + 1) * width] = dot_nn(active, weight).astype(BF)
+        sent.append(mv.send(outs.at[b, 1], outr.at[b], "x"))
+        return sent
+
+    put = []
+
+    def branch(b, sent):
+        mv.arrive(*sent[:4])
+        mv.kept_done(*put)
+        total = 4 * width
+        mean, inv = statistics(b)
+        mean_one = mean_two = 0.0
+        for k in ks:
+            unit = (mid[b, k] - mean) * inv
+            grad = gs[b, k].astype(F32) + gsr[b, k].astype(F32)
+            gain_sum = jnp.sum(grad * unit, 0, keepdims=True)
+            shift_sum = jnp.sum(grad, 0, keepdims=True)
+            for i, term in enumerate((gain_sum, shift_sum)):
+                place_row = pl.ds(4 * i + chunk_of(shard, k), 1)
+                if b == 0:
+                    midsum_out[place_row, :] = term
+                else:
+                    midsum_out[place_row, :] += term
+            scaled = grad * row(0, k)
+            mean_one = mean_one + jnp.sum(scaled, 1, keepdims=True)
+            mean_two = mean_two + jnp.sum(scaled * unit, 1, keepdims=True)
+        mean_one, mean_two = mean_one / total, mean_two / total
+        for k in ks:
+            unit = (mid[b, k] - mean) * inv
+            grad = gs[b, k].astype(F32) + gsr[b, k].astype(F32)
+            full = gb[b, k].astype(F32) + inv * (grad * row(0, k) - mean_one - unit * mean_two)
+            gmid[k] = full
+            low = full.astype(BF)
+            xs[b, k // 2, :, (k % 2) * width : (k % 2 + 1) * width] = low
+            sec_sum = jnp.sum(low.astype(F32), 0, keepdims=True)
+            place_row = pl.ds(8 + chunk_of(shard, k), 1)
+            if b == 0:
+                midsum_out[place_row, :] = sec_sum
+            else:
+                midsum_out[place_row, :] += sec_sum
+        low = side_by_side([xs[b, 0], xs[b, 1]])
+        weight = side_by_side([jnp.concatenate([wo[m, k, 0] for m in ks], axis=0) for k in ks])
+        mixed = dot_nt(low, weight).astype(BF)
+        for m in ks:
+            gm[b, m] = mixed[:, m * lanes : (m + 1) * lanes]
+        mv.send(gm.at[b, 2], d_out.at[b, 2], "y")
+        mv.send(gm.at[b, 3], d_out.at[b, 3], "ycore")
+        mv.send(gm.at[b, 1], d_out.at[b, 1], "core")
+        mv.keep(gm.at[b, 0], d_out.at[b, 0])
+        for j in range(2):
+            put.append(mv.keep(gmid.at[own_k[j]], gmid_out.at[b, j]))
+        cot_sum = jnp.sum(cs[b, 0].astype(F32), 0, keepdims=True)
+        if b == 0:
+            backsum_out[...] = cot_sum
+        else:
+            backsum_out[...] += cot_sum
+
+    def tokens(ref, *at):
+        return jnp.concatenate([ref[(b,) + at] for b in range(clips)], axis=0)
+
+    def big_grads(m, slot):
+        cot = side_by_side([tokens(gb, k) for k in ks])
+        back = dot_tn(tokens(act, m), cot).astype(BF)
+        own = dot_nn(turned[...], tokens(gin, m)).astype(BF)
+        for k in ks:
+            wg[slot, k, :hidden, :] = back[:, k * width : (k + 1) * width]
+            wg[slot, k, hidden : hidden + width, :] = own[k * width : (k + 1) * width, :width]
+            wg[slot, k, hidden + width :, :] = own[k * width : (k + 1) * width, width:]
+        return mv.keep(wg.at[slot], g_out.at[m])
+
+    first = block(0)
+    second = block(1)
+    for k in ks:
+        turned[k * width : (k + 1) * width, :] = tokens(sec, k).T
+    wrote = [big_grads(1, 0), big_grads(3, 1)]
+    branch(0, first)
+    mv.kept_done(wrote[0])
+    wrote.append(big_grads(0, 0))
+    mv.kept_done(wrote[1])
+    wrote.append(big_grads(2, 1))
+    branch(1, second)
+    grads = side_by_side([tokens(xs, i) for i in range(2)])
+    for m in ks:
+        mixed = jnp.concatenate([ms[b, 0, m] for b in range(clips)], axis=0)
+        out = dot_tn(mixed, grads).astype(BF)
+        for k in ks:
+            wgo[m, k] = out[:, k * width : (k + 1) * width]
+    mv.keep(wgo, go_out)
+    for b, sent in enumerate((first, second)):
+        mv.arrive(sent[4])
+        for j in range(2):
+            part = slice(j * width, (j + 1) * width)
+            y_out[b, :, part] = (
+                mid[b, own_k[j]]
+                + outs[b, 0, :, part].astype(F32)
+                + outr[b, :, part].astype(F32)
+                + bback_ref[0:1, part].astype(F32)
+            ).astype(BF)
+    mv.finish()
+
+
+def second_call(x, xp, c, cp, mo, mp, wo, wi, wb, ln, b_in, b_out, b_out_other, b_back):
+    clips, rows, half = x.shape
+    width = half // 2
+    lanes = mo.shape[3]
+    hidden = wi.shape[3]
+    tall = hidden + 2 * width
+    outs = [
+        ((clips, rows, half), BF),
+        ((clips, 2, rows, width), F32),
+        ((clips, 4, rows, lanes), BF),
+        ((4, 4, tall, width), BF),
+        ((4, 4, lanes, width), BF),
+        ((12, width), F32),
+        ((4, hidden), F32),
+        ((1, half), F32),
+    ]
+    small = [ln, b_in, b_out, b_out_other, b_back]
+    return pl.pallas_call(
+        second_body,
+        in_specs=[ANY] * 9 + [whole(a.shape) for a in small],
+        out_specs=[whole(outs[0][0])] + [ANY] * 4 + [whole(o[0]) for o in outs[5:]],
+        out_shape=[jax.ShapeDtypeStruct(shape, kind) for shape, kind in outs],
+        scratch_shapes=[
+            pltpu.VMEM((clips, 2, rows, half), BF),
+            pltpu.VMEM((clips, 2, rows, half), BF),
+            pltpu.VMEM((clips, 2, 4, rows, lanes), BF),
+            pltpu.VMEM(wo.shape, BF),
+            pltpu.VMEM(wi.shape, BF),
+            pltpu.VMEM(wb.shape, BF),
+            pltpu.VMEM((clips, 4, rows, width), F32),
+            pltpu.VMEM((clips, 4, rows, width), BF),
+            pltpu.VMEM((clips, 4, rows, hidden), BF),
+            pltpu.VMEM((clips, 4, rows, hidden), BF),
+            pltpu.VMEM((clips, 2, rows, half), BF),
+            pltpu.VMEM((clips, rows, half), BF),
+            pltpu.VMEM((clips, 4, rows, width), BF),
+            pltpu.VMEM((clips, 4, rows, width), BF),
+            pltpu.VMEM((4, rows, width), F32),
+            pltpu.VMEM((clips, 4, rows, width), BF),
+            pltpu.VMEM((clips, 4, rows, lanes), BF),
+            pltpu.VMEM((2, 4, tall, width), BF),
+            pltpu.VMEM((4, 4, lanes, width), BF),
+            pltpu.VMEM((4 * width, clips * rows), BF),
+            pltpu.SemaphoreType.DMA((24,)),
+            pltpu.SemaphoreType.DMA((24,)),
+            pltpu.SemaphoreType.DMA((40,)),
+        ],
+        compiler_params=pltpu.CompilerParams(
+            vmem_limit_bytes=VMEM_BYTES, collective_id=2, has_side_effects=True
+        ),
+        name="layer_middle",
+    )(x, xp, c, cp, mo, mp, wo, wi, wb, *small)
+
+
+def across(axis, size, distance):
+    pairs = [(i, i ^ distance) for i in range(size)]
+    return lambda value: lax.ppermute(value, axis, pairs)
+
+
+def fast_device(
+    inputs,
+    ln1_gain,
+    ln1_bias,
+    w_qkv,
+    b_qkv,
+    w_out,
+    b_out,
+    ln2_gain,
+    ln2_bias,
+    w_in,
+    b_in,
+    w_back,
+    b_back,
+    cotangent,
+):
+    clips, rows, half = inputs.shape
+    width = half // 2
+    lanes = half // 4
+    hidden = w_in.shape[1] // 4
+    shard, ctx, tp = (lax.axis_index(name) for name in ("shard", "ctx", "tp"))
+    ids = jnp.stack([shard, ctx, tp]).astype(jnp.int32)
+    px = across("tp", 2, 1)
+    p1, p2, p3 = (across("ctx", 4, k) for k in (1, 2, 3))
+    pz = [across("shard", 4, k) for k in (1, 2, 3)]
+
+    def halves(vector):
+        vector = vector.astype(F32)
+        return jnp.concatenate(
+            [
+                lax.dynamic_slice_in_dim(vector, tp * half, half),
+                lax.dynamic_slice_in_dim(vector, (1 - tp) * half, half),
+            ]
+        )
+
+    ln_qkv = jnp.stack([halves(ln1_gain), halves(ln1_bias)])
+    bias_qkv = (
+        lax.dynamic_slice_in_dim(b_qkv, ctx * lanes, lanes, axis=1)
+        .reshape(1, 3 * lanes)
+        .astype(F32)
+    )
+    bias_in = b_in.reshape(4, hidden).astype(F32)
+
+    flat = lambda a: a.reshape(4 * rows, -1)
+    qkv_piece = lax.dynamic_slice_in_dim(w_qkv, ctx * lanes, lanes, axis=2).reshape(
+        width, 3 * lanes
+    )
+    xp, cp, normed, qkv, ot, lse, mo, mp, wq, wo, wi, wb, bias_other, tables = first_call(
+        inputs,
+        cotangent,
+        qkv_piece,
+        w_out,
+        w_in,
+        w_back,
+        bias_qkv,
+        ln_qkv,
+        jnp.broadcast_to(b_out, (16, half)),
+    )
+    cosines, sines = tables[0], tables[1]
+    blocks = [(inputs[b], None, None, None, xp[b]) for b in range(clips)]
+    ln_two = jnp.concatenate([ln2_gain, ln2_bias]).astype(F32).reshape(8, width)
+    output, gmids, arrived, grads, grads_out, mid_total, in_total, back_total_own = second_call(
+        inputs,
+        xp,
+        cotangent,
+        cp,
+        mo,
+        mp,
+        wo,
+        wi,
+        wb,
+        ln_two,
+        bias_in,
+        b_out.reshape(1, half),
+        bias_other,
+        b_back.reshape(1, half),
+    )
+    backs = [[arrived[b, m] for m in range(4)] for b in range(clips)]
+    stage = [
+        (normed[b], qkv[b, 0], qkv[b, 1], qkv[b, 2], ot[b], lse[b], None, None)
+        for b in range(clips)
+    ]
+    whole_grads = jnp.concatenate([grads, grads_out], axis=2)
+    keep = jnp.stack([whole_grads[0], whole_grads[2]])
+    send = jnp.stack([whole_grads[1], whole_grads[3]])
+
+    def add(*terms):
+        return sum(term.astype(F32) for term in terms)
+
+    def over_ctx(keep, send):
+        near = p1(send)
+        far = p2(add(keep[1], near[1]).astype(BF))
+        return add(keep[0], near[0], far).astype(BF)
+
+    def over_shards(stack):
+        return add(stack[0], *(p(stack[k + 1]) for k, p in enumerate(pz)))
+
+    def spread(piece):
+        far = p2(piece)
+        return [piece, p1(piece), far, p1(far)]
+
+    dense = spread(over_shards(over_ctx(keep, send)).astype(BF))
+
+    joins, q_sums, grads_normed = [], [], []
+    for b in range(clips):
+        normed, q, k, v, ot, lse, mo, mp = stage[b]
+        dq, dk, dv = attend_back_call(q, k, v, backs[b], ot, lse)
+        gj, kept, sent, q_sum = joined_call(
+            ids, *(a.reshape(4, rows, lanes) for a in (dq, dk, dv)), cosines, sines, wq
+        )
+        near = p1(sent)
+        cut = rows // 2
+        across_low = px(add(kept[3, :cut], near[3, :cut]).astype(BF))
+        across_high = p2(add(kept[3, cut:], near[3, cut:]).astype(BF))
+        far = add(kept[2], near[2])
+        far = jnp.concatenate([far[:cut] + across_low.astype(F32), far[cut:]]).astype(BF)
+        other = add(kept[1], near[1])
+        other = jnp.concatenate([other[:cut], other[cut:] + across_high.astype(F32)]).astype(BF)
+        grads_normed.append(add(kept[0], near[0], p2(far), px(other)))
+        joins.append(gj)
+        q_sums.append(q_sum)
+
+    qkv_sum = call(
+        qkv_grad_body,
+        [ids, flat(stage[0][0]), flat(joins[0]), flat(stage[1][0]), flat(joins[1])],
+        [((4, width, 3 * lanes), BF)],
+        "qkv_grad",
+        flops=2 * 8 * rows * 2 * half * 3 * lanes * 1.5,
+    )[0]
+    qkv_dense = spread(over_shards(qkv_sum).astype(BF))
+
+    gain_own = ln_qkv[0, :half]
+    input_grads, gain_sum, shift_sum = [], 0.0, 0.0
+    for b in range(clips):
+        one, unused, inv = norm_parts(blocks[b][0].astype(F32), blocks[b][4].astype(F32))
+        grad = grads_normed[b]
+        gain_sum = gain_sum + jnp.sum(grad * one, axis=0)
+        shift_sum = shift_sum + jnp.sum(grad, axis=0)
+        scaled = grad * gain_own
+        stats = jnp.stack([jnp.sum(scaled, axis=1), jnp.sum(scaled * one, axis=1)])
+        stats = (stats + px(stats)) / (2 * half)
+        input_grads.append(
+            jnp.concatenate([gmids[b, 0], gmids[b, 1]], axis=1) + inv * (scaled - stats[0][:, None] - one * stats[1][:, None])
+        )
+
+    def all_sum(vector):
+        vector = vector + sum(p(vector) for p in pz)
+        return vector + p1(vector) + p2(vector) + p3(vector)
+
+    def unroll(pieces):
+        return [lax.dynamic_index_in_dim(pieces, ctx ^ m, 0, False) for m in range(4)]
+
+    q_total = q_sums[0] + q_sums[1]
+    q_total = lax.dynamic_update_slice(
+        jnp.zeros((4, 3, lanes), F32), q_total[None], (ctx, 0, 0)
+    )
+    early = all_sum(jnp.concatenate([in_total.reshape(-1), mid_total.reshape(-1), back_total_own[0]]))
+    late = all_sum(jnp.concatenate([gain_sum, shift_sum, q_total.reshape(-1)]))
+    grad_b_in = early[: 4 * hidden]
+    mid_total = early[4 * hidden : 4 * hidden + 6 * half].reshape(3, 2 * half)
+    grad_b_out = lax.dynamic_slice_in_dim(mid_total[2], tp * half, half)
+    grad_b_back = early[4 * hidden + 6 * half :]
+    grad_b_qkv = (
+        late[2 * half :].reshape(4, 3, lanes).transpose(1, 0, 2).reshape(3, 4 * lanes)
+    )
+    own_ln1 = late[: 2 * half].reshape(2, half)
+    other_ln1 = px(own_ln1)
+
+    def in_order(own, other):
+        return jnp.where(tp == 0, jnp.concatenate([own, other]), jnp.concatenate([other, own]))
+
+    grad_ln1 = [in_order(own_ln1[i], other_ln1[i]) for i in range(2)]
+    grad_ln2 = [mid_total[i] for i in range(2)]
+
+    ordered = unroll(jnp.stack(dense))
+    grad_w_back = jnp.concatenate([p[:hidden] for p in ordered], axis=0).astype(F32)
+    grad_w_in = jnp.concatenate(
+        [p[hidden + i * width : hidden + (i + 1) * width] for p in ordered for i in range(2)],
+        axis=1,
+    ).astype(F32)
+    grad_w_out = jnp.concatenate([p[hidden + 2 * width :] for p in ordered], axis=0).astype(F32)
+    ordered = unroll(jnp.stack(qkv_dense))
+    grad_w_qkv = jnp.concatenate(
+        [p.reshape(width, 3, lanes) for p in ordered], axis=2
+    ).astype(F32)
+    return (
+        output,
+        jnp.stack(input_grads),
+        grad_ln1[0],
+        grad_ln1[1],
+        grad_w_qkv,
+        grad_b_qkv,
+        grad_w_out,
+        grad_b_out,
+        grad_ln2[0],
+        grad_ln2[1],
+        grad_w_in,
+        grad_b_in,
+        grad_w_back,
+        grad_b_back,
+    )
+
+
+def quick_form_fits(mesh):
+    return (mesh.shape["shard"], mesh.shape["ctx"], mesh.shape["tp"]) == (4, 4, 2)
+
+
 def solution(mesh):
     placed = (
         P("shard", "ctx", "tp"),
@@ -430,7 +1451,7 @@
         P("shard", "ctx", "tp"),
     )
     return jax.shard_map(
-        per_device,
+        fast_device if quick_form_fits(mesh) else per_device,
         mesh=mesh,
         in_specs=placed,
         out_specs=(

time: 1390 us -> 559 us (0.40)
  waiting for transfers between devices: 692 us -> 143 us
  matrix products: 286 us -> 0 us
  Pallas kernels: 0 us -> 279 us
  local copies, waits for them, and re-layouts: 212 us -> 48.9 us
  other arithmetic: 116 us -> 42.3 us
  blocking collectives: 54.4 us -> 0 us
  starting transfers between devices: 1.53 us -> 35.6 us
  between operations: 15.5 us -> 1.56 us
    dot_general x40 -> x0, matrix products: 286 us -> none  [the longest x4 37.5 us: absorb_block(): jnp.einsum('cqhd,ckhd->chqk', queries, key_piece, preferred_element_type=...]
    pallas_call x0 -> x7, Pallas kernels: none -> 279 us  [the longest x1 120 us: first_call(): pl.pallas_call(first_body, in_specs=[ANY] * 6 + [whole(b.shape), whole(ln...]
    all_gather x9 -> x0, waiting for transfers between devices: 278 us -> none  [the longest x1 79.1 us: fetch_weights(): lax.all_gather(w_back, 'shard', axis=1, tiled=True)]
    reduce_scatter x8 -> x0, waiting for transfers between devices: 277 us -> none  [the longest x1 79.5 us: per_device(): lax.psum_scatter(summed[2].astype(jnp.bfloat16), 'shard', scatter_dimensi...]
    ppermute x0 -> x39, waiting for transfers between devices: none -> 143 us  [across(): return lambda value: lax.ppermute(value, axis, pairs)]
    psum x3 -> x0, waiting for transfers between devices: 134 us -> none  [the longest x2 126 us: back_total(): return lax.psum(summand.astype(jnp.bfloat16), 'tp').astype(jnp.float32)]
    concatenate x6 -> x4, local copies, waits for them, and re-layouts: 94.2 us -> 2.47 us  [the longest x2 1.38 us: fast_device(): ln_two = jnp.concatenate([ln2_gain, ln2_bias]).astype(F32).reshape(8, width)]
    psum x1 -> x0, blocking collectives: 54.4 us -> none  [per_device(): lax.psum((grad_gain_one, grad_shift_one, grad_b_qkv, grad_b_out, grad_gai...]
  transfers between devices with their start and end apart: 20 -> 39, of which waited for: 14 -> 16; matrix products, arithmetic and copies ran while one was open for 29% -> 13% of each run, Pallas kernels for 0% -> 14%
where the time goes in v2:
time: 559 us; the launch traced here: 550 us
  Pallas kernels  279 us (50%)
  waiting for transfers between devices  143 us (26%)
  local copies, waits for them, and re-layouts  48.9 us (9%)
  other arithmetic  42.3 us (8%)
  starting transfers between devices  35.6 us (6%)
    ppermute x39, waiting for transfers between devices, across(): return lambda value: lax.ppermute(value, axis, pairs)  143 us
    pallas_call x1, Pallas kernels, first_call(): pl.pallas_call(first_body, in_specs=[ANY] * 6 + [whole(b.shape), whole(ln...  120 us
    pallas_call x1, Pallas kernels, second_call(): pl.pallas_call(second_body, in_specs=[ANY] * 9 + [whole(a.shape) for a in...  83.8 us
    pallas_call x5, Pallas kernels, call(): pl.pallas_call(body, in_specs=in_specs or [SMEM] + [whole(a.shape) for a...  74.4 us
    ppermute x39, starting transfers between devices, across(): return lambda value: lax.ppermute(value, axis, pairs)  35.6 us
    unnamed x65, local copies, waits for them, and re-layouts  13.2 us
  transfers between devices with their start and end apart: 39, of which 16 were waited for; matrix products, arithmetic and copies ran while one was open for 13% of the time, Pallas kernels for 14%

profile of v2, /device:TPU:8, one launch (start us, length us, event | category | flops | bytes accessed | tf_op | source)
XLA Modules:
  0.0 549.8 jit_solution(15770210464204080141)
XLA Ops:
  5.4 1.3 reshape.276.refs_10_
  6.7 1.3 reshape.256.refs_11_
  8.0 1.3 reshape.257.refs_13_
  11.3 1.3 broadcast_in_dim.6.refs_8_
  12.6 120.3 %project_and_attend.1 = (bf16[2,512,512]{2,1,0:T(8,128)(2,1)}, bf16[2,512,512]{2,1,0:T(8,128)(2,1)}, bf16[2,4,512,1024]{3,2,1,0:T(8,128)(2,1)}, bf16[2,3,2048,12...) custom-call(bf16[2,512,512]{2,1,0:T(8,128)(2,1)} %refs_0_.3, ...), custom_call_target="tpu_custom_call" | custom-call | tf_op jit(solution)/shard_map/project_and_attend/pallas_call | solution.py:948
  133.0 83.8 %layer_middle.1 = (bf16[2,512,512]{2,1,0:T(8,128)(2,1)}, f32[2,2,512,256]{3,2,1,0:T(8,128)}, bf16[2,4,512,128]{3,2,1,0:T(8,128)(2,1)}, bf16[4,4,1024,256]{3,2,1,...) custom-call(bf16[2,512,512]{2,1,0:T(8,128)(2,1)} %refs_0_.3, ...), custom_call_target="tpu_custom_call" | custom-call | tf_op jit(solution)/shard_map/layer_middle/pallas_call | solution.py:1187
  218.2 1.2 pad_maximum_fusion.8
  219.4 2.4 collective-permute-start.34
  221.9 1.4 collective-permute-start.35
  223.3 7.5 %constant_dynamic-update-slice_fusion.1 = bf16[4,4,1152,256]{3,2,1,0:T(8,128)(2,1)} fusion(bf16[4,4,1024,256]{3,2,1,0:T(8,128)(2,1)} %get-tuple-element.81), kind=kLoop, calls=%fused_computation.159 | loop fusion | bytes 16777216
  231.9 2.7 fusion.68
  234.6 2.6 pad_maximum_fusion
  238.2 3.7 slice_bitcast_fusion.12
  241.9 1.5 slice_bitcast_fusion
  244.3 1.5 slice_bitcast_fusion.1
  246.4 24.7 %attend_back.3 = (f32[2048,128]{1,0:T(8,128)}, f32[2048,128]{1,0:T(8,128)}, f32[2048,128]{1,0:T(8,128)}) custom-call(bf16[2048,128]{1,0:T(8,128)(2,1)} %get-tuple-element.136.q_ref, bf16[2048,128]{1,0:T(8,128)(2,1)} %get-tuple-element.135.k_ref, bf16[2048,128]{1,0:T(8,128)(2,1)} %get-tuple-element.134.v_ref, bf16[512,128]{1,0:T(8,128)(2,1)} %get-tuple-element.164.d0, ...), custom_call_target="tpu_custom_call" | custom-call | flops 21474836480 | bytes 6307840 | tf_op jit(solution)/shard_map/attend_back/pallas_call | solution.py:448
  271.2 7.5 %joined_back.3 = (bf16[4,512,384]{2,1,0:T(8,128)(2,1)}, bf16[4,512,512]{2,1,0:T(8,128)(2,1)}, bf16[4,512,512]{2,1,0:T(8,128)(2,1)}, f32[3,128]{1,0:T(4,128)}) custom-call(s32[3]{0:T(128)} %pad_add_fusion.ids_ref, f32[4,512,128]{2,1,0:T(8,128)} %bitcast.349, f32[4,512,128]{2,1,0:T(8,128)} %bitcast.350, f32[4,512,128]{2,1,0:T(8,128)} %bitcast.351, ...), custom_call_target="tpu_custom_call" | custom-call | flops 3221225472 | bytes 11798028 | tf_op jit(solution)/shard_map/joined_back/pallas_call | solution.py:448
  279.6 6.0 %fusion.69 = (bf16[1,4,512,1024]{3,2,1,0:T(8,128)(2,1)}, bf16[1,4,512,1024]{3,2,1,0:T(8,128)(2,1)}) fusion(bf16[2,4,512,1024]{3,2,1,0:T(8,128)(2,1)} %get-tuple-element.78), kind=kLoop, calls=%fused_computation.190 | loop fusion | bytes 16777216 | tf_op jit(solution)/shard_map/slice | solution.py:1308
  285.6 24.9 %attend_back.2 = (f32[2048,128]{1,0:T(8,128)}, f32[2048,128]{1,0:T(8,128)}, f32[2048,128]{1,0:T(8,128)}) custom-call(bf16[2048,128]{1,0:T(8,128)(2,1)} %get-tuple-element.139.q_ref, bf16[2048,128]{1,0:T(8,128)(2,1)} %get-tuple-element.138.k_ref, bf16[2048,128]{1,0:T(8,128)(2,1)} %get-tuple-element.137.v_ref, bf16[512,128]{1,0:T(8,128)(2,1)} %get-tuple-element.168.d0, ...), custom_call_target="tpu_custom_call" | custom-call | flops 21474836480 | bytes 6307840 | tf_op jit(solution)/shard_map/attend_back/pallas_call | solution.py:448
  310.5 7.3 %joined_back.2 = (bf16[4,512,384]{2,1,0:T(8,128)(2,1)}, bf16[4,512,512]{2,1,0:T(8,128)(2,1)}, bf16[4,512,512]{2,1,0:T(8,128)(2,1)}, f32[3,128]{1,0:T(4,128)}) custom-call(s32[3]{0:T(128)} %pad_add_fusion.ids_ref, f32[4,512,128]{2,1,0:T(8,128)} %bitcast.346, f32[4,512,128]{2,1,0:T(8,128)} %bitcast.347, f32[4,512,128]{2,1,0:T(8,128)} %bitcast.348, ...), custom_call_target="tpu_custom_call" | custom-call | flops 3221225472 | bytes 11798028 | tf_op jit(solution)/shard_map/joined_back/pallas_call | solution.py:448
  317.9 9.9 %qkv_grad.1 = bf16[4,256,384]{2,1,0:T(8,128)(2,1)} custom-call(s32[3]{0:T(128)} %pad_add_fusion.ids_ref, bf16[2048,1024]{1,0:T(8,128)(2,1)} %bitcast.304, bf16[2048,384]{1,0:T(8,128)(2,1)} %bitcast.345, bf16[2048,1024]{1,0:T(8,128)(2,1)} %bitcast.303, bf16[2048,384]{1,0:T(8,128)(2,1)} %bitcast.344), custom_call_target="tpu_custom_call" | custom-call | flops 4831838208 | bytes 12320780 | tf_op jit(solution)/shard_map/qkv_grad/pallas_call | solution.py:448
  327.8 1.9 slice_bitcast_fusion.24
  329.7 1.4 slice_bitcast_fusion.21
  331.1 1.3 fusion.17
  333.9 1.4 add_add_fusion.1
  336.5 1.3 slice.547
  341.7 11.2 %collective-permute-done.20 = bf16[256,384]{1,0:T(8,128)(2,1)S(1)} collective-permute-done((bf16[256,384]{1,0:T(8,128)(2,1)S(1)}, bf16[256,384]{1,0:T(8,128)(2,1)S(1)}, u32[]{:S(2)}, u32[]{:S(2)}) %collective-permute-start.20) | collective-permute-done | bytes 196640 | tf_op jit(solution)/shard_map/ppermute | solution.py:1226
  352.9 1.2 collective-permute-start.37
  354.2 4.4 collective-permute-done.21
  359.7 1.4 collective-permute-start.23
  363.0 4.2 collective-permute-done.23
  367.3 1.2 fusion.52
  368.4 1.7 collective-permute-start.7
  370.1 1.5 convert_add_fusion.2
  371.7 1.4 collective-permute-start.9
  373.2 1.2 fusion.50
  374.3 1.5 convert_add_fusion.4
  375.9 1.3 collective-permute-done.7
  377.2 1.6 collective-permute-start.1
  378.9 1.3 collective-permute-done.9
  380.2 1.4 collective-permute-start.3
  383.4 1.8 collective-permute-done.1
  385.1 1.5 collective-permute-start.8
  386.7 1.6 collective-permute-start.10
  388.3 4.4 fusion.1
  395.1 1.4 collective-permute-start.2
  400.6 1.6 copy.35
  402.2 58.8 %collective-permute-done.2 = bf16[512,512]{1,0:T(8,128)(2,1)} collective-permute-done((bf16[512,512]{1,0:T(8,128)(2,1)}, bf16[512,512]{1,0:T(8,128)(2,1)}, u32[]{:S(2)}, u32[]{:S(2)}) %collective-permute-start.2) | collective-permute-done | bytes 524320 | tf_op jit(solution)/shard_map/ppermute | solution.py:1226
  461.0 3.1 fusion.16
  464.3 2.6 collective-permute-start.13
  467.8 1.2 collective-permute-start.5
  469.1 1.5 collective-permute-done.11
  470.6 4.0 fusion
  474.9 2.2 collective-permute-start.28
  477.1 1.2 collective-permute-start.29
  479.4 16.1 %collective-permute-done.27 = bf16[1152,256]{1,0:T(8,128)(2,1)S(1)} collective-permute-done((bf16[1152,256]{1,0:T(8,128)(2,1)S(1)}, bf16[1152,256]{1,0:T(8,128)(2,1)S(1)}, u32[]{:S(2)}, u32[]{:S(2)}) %collective-permute-start.27) | collective-permute-done | bytes 589856 | tf_op jit(solution)/shard_map/ppermute | solution.py:1226
  495.5 1.2 collective-permute-start.14
  496.7 19.7 %collective-permute-done.28 = bf16[1152,256]{1,0:T(8,128)(2,1)S(1)} collective-permute-done((bf16[1152,256]{1,0:T(8,128)(2,1)S(1)}, bf16[1152,256]{1,0:T(8,128)(2,1)S(1)}, u32[]{:S(2)}, u32[]{:S(2)}) %collective-permute-start.28) | collective-permute-done | bytes 589856 | tf_op jit(solution)/shard_map/ppermute | solution.py:1226
  516.5 10.5 %collective-permute-done.29 = bf16[1152,256]{1,0:T(8,128)(2,1)S(1)} collective-permute-done((bf16[1152,256]{1,0:T(8,128)(2,1)S(1)}, bf16[1152,256]{1,0:T(8,128)(2,1)S(1)}, u32[]{:S(2)}, u32[]{:S(2)}) %collective-permute-start.29) | collective-permute-done | bytes 589856 | tf_op jit(solution)/shard_map/ppermute | solution.py:1226
  530.3 1.5 pad_maximum_fusion.2
  531.8 7.3 %collective-permute-done.16 = f32[2560]{0:T(1024)S(1)} collective-permute-done((f32[2560]{0:T(1024)S(1)}, f32[2560]{0:T(1024)S(1)}, u32[]{:S(2)}, u32[]{:S(2)}) %collective-permute-start.16) | collective-permute-done | bytes 10272 | tf_op jit(solution)/shard_map/ppermute | solution.py:1226
  540.5 2.4 collective-permute-done.18
  544.7 1.6 convert_element_type.325
  546.3 1.5 maximum_convert_fusion
  (188 shorter events, 41.6 us)
Async XLA Ops:
  10.1 122.9 %copy-start.22 = (f32[1024]{0:T(1024)}, f32[1024]{0:T(1024)S(1)}, u32[]{:S(2)}) copy-start(f32[1024]{0:T(1024)S(1)} %pad_maximum_fusion.11) | copy-start | bytes 12292
  218.2 5.1 copy-start.16
  219.4 113.6 %collective-permute-start.33 = (f32[5632]{0:T(1024)}, f32[5632]{0:T(1024)}, u32[]{:S(2)}, u32[]{:S(2)}) collective-permute-start(f32[5632]{0:T(1024)} %pad_maximum_fusion.8), channel_id=1, source_target_pairs={{0,8},{8,0},{16,24},{24,16},{1,9},{9,1},{17,25},{25,17},{2,10},{10... | collective-permute-start | bytes 67592 | tf_op jit(solution)/shard_map/ppermute | solution.py:1226
  219.4 114.5 %collective-permute-start.34 = (f32[5632]{0:T(1024)}, f32[5632]{0:T(1024)}, u32[]{:S(2)}, u32[]{:S(2)}) collective-permute-start(f32[5632]{0:T(1024)} %pad_maximum_fusion.8), channel_id=1, source_target_pairs={{0,16},{8,24},{16,0},{24,8},{1,17},{9,25},{17,1},{25,9},{2,18},{10... | collective-permute-start | bytes 67592 | tf_op jit(solution)/shard_map/ppermute | solution.py:1226
  221.9 112.0 %collective-permute-start.35 = (f32[5632]{0:T(1024)}, f32[5632]{0:T(1024)}, u32[]{:S(2)}, u32[]{:S(2)}) collective-permute-start(f32[5632]{0:T(1024)} %pad_maximum_fusion.8), channel_id=1, source_target_pairs={{0,24},{8,16},{16,8},{24,0},{1,25},{9,17},{17,9},{25,1},{2,26},{10... | collective-permute-start | bytes 67592 | tf_op jit(solution)/shard_map/ppermute | solution.py:1226
  223.3 7.5 %copy-start.15 = (bf16[4,4,128,256]{3,2,1,0:T(8,128)(2,1)S(1)}, bf16[4,4,128,256]{3,2,1,0:T(8,128)(2,1)}, u32[]{:S(2)}) copy-start(bf16[4,4,128,256]{3,2,1,0:T(8,128)(2,1)} %get-tuple-element.82) | copy-start | bytes 3145732
  234.6 2.7 copy-start.14
  237.2 149.5 %collective-permute-start.25 = (bf16[2,4,1152,256]{3,2,1,0:T(8,128)(2,1)}, bf16[2,4,1152,256]{3,2,1,0:T(8,128)(2,1)}, u32[]{:S(2)}, u32[]{:S(2)}) collective-permute-start(bf16[2,4,1152,256]{3,2,1,0:T(8,128)(2,1)} %pad_maximum_fusion), channel_id=1, source_target_pairs={{0,2},{2,0},{4,6},{6,4},{1,3},{3,1},{5,7},{7,5},{8,10},{10,8},{12,... | collective-permute-start | bytes 14155784 | tf_op jit(solution)/shard_map/ppermute | solution.py:1226
  238.2 3.7 copy-start.8
  241.9 1.5 copy-start.17
  241.9 2.4 copy-start.7
  271.1 8.0 %copy-start.3 = (bf16[2,512,512]{2,1,0:T(8,128)(2,1)S(1)}, bf16[2,512,512]{2,1,0:T(8,128)(2,1)}, u32[]{:S(2)}) copy-start(bf16[2,512,512]{2,1,0:T(8,128)(2,1)} %get-tuple-element.50.refs_1_) | copy-start | bytes 3145732
  271.1 8.3 %copy-start.2 = (bf16[2,512,512]{2,1,0:T(8,128)(2,1)S(1)}, bf16[2,512,512]{2,1,0:T(8,128)(2,1)}, u32[]{:S(2)}) copy-start(bf16[2,512,512]{2,1,0:T(8,128)(2,1)} %refs_0_.3) | copy-start | bytes 3145732
  278.7 88.6 %collective-permute-start.6 = (bf16[4,512,512]{2,1,0:T(8,128)(2,1)}, bf16[4,512,512]{2,1,0:T(8,128)(2,1)}, u32[]{:S(2)}, u32[]{:S(2)}) collective-permute-start(bf16[4,512,512]{2,1,0:T(8,128)(2,1)} %get-tuple-element.75), channel_id=1, source_target_pairs={{0,2},{2,0},{4,6},{6,4},{1,3},{3,1},{5,7},{7,5},{8,10},{10,8},{12,... | collective-permute-start | bytes 6291464 | tf_op jit(solution)/shard_map/ppermute | solution.py:1226
  317.9 11.8 %copy-start.6 = (f32[2,2,512,256]{3,2,1,0:T(8,128)S(1)}, f32[2,2,512,256]{3,2,1,0:T(8,128)}, u32[]{:S(2)}) copy-start(f32[2,2,512,256]{3,2,1,0:T(8,128)} %get-tuple-element.59) | copy-start | bytes 6291460
  329.7 2.7 copy-start.18
  329.7 2.7 copy-start.20
  329.7 4.2 copy-start.25
  331.1 36.2 %copy-start.4 = (bf16[4,512,512]{2,1,0:T(8,128)(2,1)S(1)}, bf16[4,512,512]{2,1,0:T(8,128)(2,1)}, u32[]{:S(2)}) copy-start(bf16[4,512,512]{2,1,0:T(8,128)(2,1)} %get-tuple-element.74) | copy-start | bytes 6291460
  333.0 7.1 %collective-permute-start.19 = (bf16[256,384]{1,0:T(8,128)(2,1)}, bf16[256,384]{1,0:T(8,128)(2,1)}, u32[]{:S(2)}, u32[]{:S(2)}) collective-permute-start(bf16[256,384]{1,0:T(8,128)(2,1)} %get-tuple-element.173), channel_id=1, source_target_pairs={{0,8},{8,0},{16,24},{24,16},{1,9},{9,1},{17,25},{25,17},{2,10},{10... | collective-permute-start | bytes 589832 | tf_op jit(solution)/shard_map/ppermute | solution.py:1226
  333.9 37.8 %collective-permute-start = (bf16[4,512,512]{2,1,0:T(8,128)(2,1)}, bf16[4,512,512]{2,1,0:T(8,128)(2,1)}, u32[]{:S(2)}, u32[]{:S(2)}) collective-permute-start(bf16[4,512,512]{2,1,0:T(8,128)(2,1)} %get-tuple-element.70), channel_id=1, source_target_pairs={{0,2},{2,0},{4,6},{6,4},{1,3},{3,1},{5,7},{7,5},{8,10},{10,8},{12,... | collective-permute-start | bytes 6291464 | tf_op jit(solution)/shard_map/ppermute | solution.py:1226
  335.3 3.1 collective-permute-start.36
  338.4 14.5 %collective-permute-start.20 = (bf16[256,384]{1,0:T(8,128)(2,1)S(1)}, bf16[256,384]{1,0:T(8,128)(2,1)S(1)}, u32[]{:S(2)}, u32[]{:S(2)}) collective-permute-start(bf16[256,384]{1,0:T(8,128)(2,1)S(1)} %get-tuple-element.175), channel_id=1, source_target_pairs={{0,16},{8,24},{16,0},{24,8},{1,17},{9,25},{17,1},{25,9},{2,18},{10... | collective-permute-start | bytes 589832 | tf_op jit(solution)/shard_map/ppermute | solution.py:1226
  340.1 18.5 %collective-permute-start.21 = (bf16[256,384]{1,0:T(8,128)(2,1)S(1)}, bf16[256,384]{1,0:T(8,128)(2,1)S(1)}, u32[]{:S(2)}, u32[]{:S(2)}) collective-permute-start(bf16[256,384]{1,0:T(8,128)(2,1)S(1)} %get-tuple-element.174), channel_id=1, source_target_pairs={{0,24},{8,16},{16,8},{24,0},{1,25},{9,17},{17,9},{25,1},{2,26},{10... | collective-permute-start | bytes 589832 | tf_op jit(solution)/shard_map/ppermute | solution.py:1226
  352.9 6.8 %collective-permute-start.37 = (f32[5632]{0:T(1024)}, f32[5632]{0:T(1024)S(1)}, u32[]{:S(2)}, u32[]{:S(2)}) collective-permute-start(f32[5632]{0:T(1024)} %add_add_fusion.1), channel_id=1, source_target_pairs={{0,4},{2,6},{4,0},{6,2},{1,5},{3,7},{5,1},{7,3},{8,12},{10,14},{12... | collective-permute-start | bytes 67592 | tf_op jit(solution)/shard_map/ppermute | solution.py:1226
  358.6 3.6 collective-permute-start.38
  359.7 7.5 %collective-permute-start.23 = (bf16[256,384]{1,0:T(8,128)(2,1)S(1)}, bf16[256,384]{1,0:T(8,128)(2,1)S(1)}, u32[]{:S(2)}, u32[]{:S(2)}) collective-permute-start(bf16[256,384]{1,0:T(8,128)(2,1)S(1)} %fusion.49), channel_id=1, source_target_pairs={{0,4},{2,6},{4,0},{6,2},{1,5},{3,7},{5,1},{7,3},{8,12},{10,14},{12... | collective-permute-start | bytes 589832 | tf_op jit(solution)/shard_map/ppermute | solution.py:1226
  363.0 32.1 %collective-permute-start.22 = (bf16[256,384]{1,0:T(8,128)(2,1)S(1)}, bf16[256,384]{1,0:T(8,128)(2,1)S(1)}, u32[]{:S(2)}, u32[]{:S(2)}) collective-permute-start(bf16[256,384]{1,0:T(8,128)(2,1)S(1)} %fusion.49), channel_id=1, source_target_pairs={{0,2},{2,0},{4,6},{6,4},{1,3},{3,1},{5,7},{7,5},{8,10},{10,8},{12,... | collective-permute-start | bytes 589832 | tf_op jit(solution)/shard_map/ppermute | solution.py:1226
  367.2 29.2 %collective-permute-start.24 = (bf16[256,384]{1,0:T(8,128)(2,1)S(1)}, bf16[256,384]{1,0:T(8,128)(2,1)S(1)}, u32[]{:S(2)}, u32[]{:S(2)}) collective-permute-start(bf16[256,384]{1,0:T(8,128)(2,1)S(1)} %collective-permute-done.23), channel_id=1, source_target_pairs={{0,2},{2,0},{4,6},{6,4},{1,3},{3,1},{5,7},{7,5},{8,10},{10,8},{12,... | collective-permute-start | bytes 589832 | tf_op jit(solution)/shard_map/ppermute | solution.py:1226
  368.4 4.7 copy-start.5
  368.4 8.8 %collective-permute-start.7 = (bf16[256,512]{1,0:T(8,128)(2,1)S(1)}, bf16[256,512]{1,0:T(8,128)(2,1)S(1)}, u32[]{:S(2)}, u32[]{:S(2)}) collective-permute-start(bf16[256,512]{1,0:T(8,128)(2,1)S(1)} %get-tuple-element.126), channel_id=1, source_target_pairs={{0,1},{1,0},{2,3},{3,2},{4,5},{5,4},{6,7},{7,6},{8,9},{9,8},{10,11... | collective-permute-start | bytes 786440 | tf_op jit(solution)/shard_map/ppermute | solution.py:1226
  371.7 8.5 %collective-permute-start.9 = (bf16[256,512]{1,0:T(8,128)(2,1)S(1)}, bf16[256,512]{1,0:T(8,128)(2,1)S(1)}, u32[]{:S(2)}, u32[]{:S(2)}) collective-permute-start(bf16[256,512]{1,0:T(8,128)(2,1)S(1)} %get-tuple-element.127), channel_id=1, source_target_pairs={{0,4},{2,6},{4,0},{6,2},{1,5},{3,7},{5,1},{7,3},{8,12},{10,14},{12... | collective-permute-start | bytes 786440 | tf_op jit(solution)/shard_map/ppermute | solution.py:1226
  377.2 7.9 %collective-permute-start.1 = (bf16[256,512]{1,0:T(8,128)(2,1)S(1)}, bf16[256,512]{1,0:T(8,128)(2,1)S(1)}, u32[]{:S(2)}, u32[]{:S(2)}) collective-permute-start(bf16[256,512]{1,0:T(8,128)(2,1)S(1)} %get-tuple-element.130), channel_id=1, source_target_pairs={{0,1},{1,0},{2,3},{3,2},{4,5},{5,4},{6,7},{7,6},{8,9},{9,8},{10,11... | collective-permute-start | bytes 786440 | tf_op jit(solution)/shard_map/ppermute | solution.py:1226
  380.2 12.4 %collective-permute-start.3 = (bf16[256,512]{1,0:T(8,128)(2,1)S(1)}, bf16[256,512]{1,0:T(8,128)(2,1)S(1)}, u32[]{:S(2)}, u32[]{:S(2)}) collective-permute-start(bf16[256,512]{1,0:T(8,128)(2,1)S(1)} %get-tuple-element.131), channel_id=1, source_target_pairs={{0,4},{2,6},{4,0},{6,2},{1,5},{3,7},{5,1},{7,3},{8,12},{10,14},{12... | collective-permute-start | bytes 786440 | tf_op jit(solution)/shard_map/ppermute | solution.py:1226
  385.1 17.1 %collective-permute-start.8 = (bf16[512,512]{1,0:T(8,128)(2,1)}, bf16[512,512]{1,0:T(8,128)(2,1)}, u32[]{:S(2)}, u32[]{:S(2)}) collective-permute-start(bf16[512,512]{1,0:T(8,128)(2,1)} %pad_maximum_fusion.6), channel_id=1, source_target_pairs={{0,4},{2,6},{4,0},{6,2},{1,5},{3,7},{5,1},{7,3},{8,12},{10,14},{12... | collective-permute-start | bytes 1572872 | tf_op jit(solution)/shard_map/ppermute | solution.py:1226
  386.7 15.5 %collective-permute-start.10 = (bf16[512,512]{1,0:T(8,128)(2,1)}, bf16[512,512]{1,0:T(8,128)(2,1)}, u32[]{:S(2)}, u32[]{:S(2)}) collective-permute-start(bf16[512,512]{1,0:T(8,128)(2,1)} %pad_maximum_fusion.7), channel_id=1, source_target_pairs={{0,1},{1,0},{2,3},{3,2},{4,5},{5,4},{6,7},{7,6},{8,9},{9,8},{10,11... | collective-permute-start | bytes 1572872 | tf_op jit(solution)/shard_map/ppermute | solution.py:1226
  392.7 77.9 %collective-permute-start.26 = (bf16[4,1152,256]{2,1,0:T(8,128)(2,1)}, bf16[4,1152,256]{2,1,0:T(8,128)(2,1)}, u32[]{:S(2)}, u32[]{:S(2)}) collective-permute-start(bf16[4,1152,256]{2,1,0:T(8,128)(2,1)} %fusion.1), channel_id=1, source_target_pairs={{0,4},{2,6},{4,0},{6,2},{1,5},{3,7},{5,1},{7,3},{8,12},{10,14},{12... | collective-permute-start | bytes 7077896 | tf_op jit(solution)/shard_map/ppermute | solution.py:1226
  395.1 65.9 %collective-permute-start.2 = (bf16[512,512]{1,0:T(8,128)(2,1)}, bf16[512,512]{1,0:T(8,128)(2,1)}, u32[]{:S(2)}, u32[]{:S(2)}) collective-permute-start(bf16[512,512]{1,0:T(8,128)(2,1)} %pad_maximum_fusion.4), channel_id=1, source_target_pairs={{0,4},{2,6},{4,0},{6,2},{1,5},{3,7},{5,1},{7,3},{8,12},{10,14},{12... | collective-permute-start | bytes 1572872 | tf_op jit(solution)/shard_map/ppermute | solution.py:1226
  396.5 64.5 %collective-permute-start.4 = (bf16[512,512]{1,0:T(8,128)(2,1)}, bf16[512,512]{1,0:T(8,128)(2,1)}, u32[]{:S(2)}, u32[]{:S(2)}) collective-permute-start(bf16[512,512]{1,0:T(8,128)(2,1)} %pad_maximum_fusion.5), channel_id=1, source_target_pairs={{0,1},{1,0},{2,3},{3,2},{4,5},{5,4},{6,7},{7,6},{8,9},{9,8},{10,11... | collective-permute-start | bytes 1572872 | tf_op jit(solution)/shard_map/ppermute | solution.py:1226
  400.4 60.6 %copy-start.19 = (f32[512]{0:T(512)S(1)}, f32[512]{0:T(512)}, u32[]{:S(2)}) copy-start(f32[512]{0:T(512)} %copy-done.18) | copy-start | bytes 6148
  400.4 60.6 %copy-start.21 = (f32[512]{0:T(512)S(1)}, f32[512]{0:T(512)}, u32[]{:S(2)}) copy-start(f32[512]{0:T(512)} %copy-done.20) | copy-start | bytes 6148
  400.4 60.6 %copy-start.23 = (f32[512]{0:T(512)S(1)}, f32[512]{0:T(512)}, u32[]{:S(2)}) copy-start(f32[512]{0:T(512)} %add_rsqrt_fusion) | copy-start | bytes 6148
  400.4 60.6 %copy-start.24 = (f32[1,512]{1,0:T(1,128)S(1)}, f32[1,512]{1,0:T(1,128)}, u32[]{:S(2)}) copy-start(f32[1,512]{1,0:T(1,128)} %slice.547) | copy-start | bytes 6148
  464.2 64.2 %collective-permute-start.12 = (f32[2560]{0:T(1024)S(1)}, f32[2560]{0:T(1024)S(1)}, u32[]{:S(2)}, u32[]{:S(2)}) collective-permute-start(f32[2560]{0:T(1024)S(1)} %pad_maximum_fusion.9), channel_id=1, source_target_pairs={{0,8},{8,0},{16,24},{24,16},{1,9},{9,1},{17,25},{25,17},{2,10},{10... | collective-permute-start | bytes 30728 | tf_op jit(solution)/shard_map/ppermute | solution.py:1226
  464.3 64.1 %collective-permute-start.13 = (f32[2560]{0:T(1024)S(1)}, f32[2560]{0:T(1024)S(1)}, u32[]{:S(2)}, u32[]{:S(2)}) collective-permute-start(f32[2560]{0:T(1024)S(1)} %pad_maximum_fusion.9), channel_id=1, source_target_pairs={{0,16},{8,24},{16,0},{24,8},{1,17},{9,25},{17,1},{25,9},{2,18},{10... | collective-permute-start | bytes 30728 | tf_op jit(solution)/shard_map/ppermute | solution.py:1226
  466.9 3.7 collective-permute-start.11
  467.8 9.3 %collective-permute-start.5 = (f32[2,512]{1,0:T(2,128)S(1)}, f32[2,512]{1,0:T(2,128)S(1)}, u32[]{:S(2)}, u32[]{:S(2)}) collective-permute-start(f32[2,512]{1,0:T(2,128)S(1)} %pad_maximum_fusion.13), channel_id=1, source_target_pairs={{0,1},{1,0},{2,3},{3,2},{4,5},{5,4},{6,7},{7,6},{8,9},{9,8},{10,11... | collective-permute-start | bytes 12296 | tf_op jit(solution)/shard_map/ppermute | solution.py:1226
  474.6 3.8 copy-start.9
  474.6 3.8 copy-start.10
  474.6 3.8 copy-start.11
  474.6 3.8 copy-start.12
  474.8 20.7 %collective-permute-start.27 = (bf16[1152,256]{1,0:T(8,128)(2,1)S(1)}, bf16[1152,256]{1,0:T(8,128)(2,1)S(1)}, u32[]{:S(2)}, u32[]{:S(2)}) collective-permute-start(bf16[1152,256]{1,0:T(8,128)(2,1)S(1)} %get-tuple-element.148), channel_id=1, source_target_pairs={{0,8},{8,0},{16,24},{24,16},{1,9},{9,1},{17,25},{25,17},{2,10},{10... | collective-permute-start | bytes 1769480 | tf_op jit(solution)/shard_map/ppermute | solution.py:1226
  474.9 41.5 %collective-permute-start.28 = (bf16[1152,256]{1,0:T(8,128)(2,1)S(1)}, bf16[1152,256]{1,0:T(8,128)(2,1)S(1)}, u32[]{:S(2)}, u32[]{:S(2)}) collective-permute-start(bf16[1152,256]{1,0:T(8,128)(2,1)S(1)} %get-tuple-element.150), channel_id=1, source_target_pairs={{0,16},{8,24},{16,0},{24,8},{1,17},{9,25},{17,1},{25,9},{2,18},{10... | collective-permute-start | bytes 1769480 | tf_op jit(solution)/shard_map/ppermute | solution.py:1226
  477.1 49.9 %collective-permute-start.29 = (bf16[1152,256]{1,0:T(8,128)(2,1)S(1)}, bf16[1152,256]{1,0:T(8,128)(2,1)S(1)}, u32[]{:S(2)}, u32[]{:S(2)}) collective-permute-start(bf16[1152,256]{1,0:T(8,128)(2,1)S(1)} %get-tuple-element.149), channel_id=1, source_target_pairs={{0,24},{8,16},{16,8},{24,0},{1,25},{9,17},{17,9},{25,1},{2,26},{10... | collective-permute-start | bytes 1769480 | tf_op jit(solution)/shard_map/ppermute | solution.py:1226
  495.5 32.9 %collective-permute-start.14 = (f32[2560]{0:T(1024)S(1)}, f32[2560]{0:T(1024)S(1)}, u32[]{:S(2)}, u32[]{:S(2)}) collective-permute-start(f32[2560]{0:T(1024)S(1)} %pad_maximum_fusion.9), channel_id=1, source_target_pairs={{0,24},{8,16},{16,8},{24,0},{1,25},{9,17},{17,9},{25,1},{2,26},{10... | collective-permute-start | bytes 30728 | tf_op jit(solution)/shard_map/ppermute | solution.py:1226
  527.3 12.1 %collective-permute-start.31 = (bf16[1152,256]{1,0:T(8,128)(2,1)S(1)}, bf16[1152,256]{1,0:T(8,128)(2,1)S(1)}, u32[]{:S(2)}, u32[]{:S(2)}) collective-permute-start(bf16[1152,256]{1,0:T(8,128)(2,1)S(1)} %fusion.4), channel_id=1, source_target_pairs={{0,4},{2,6},{4,0},{6,2},{1,5},{3,7},{5,1},{7,3},{8,12},{10,14},{12... | collective-permute-start | bytes 1769480 | tf_op jit(solution)/shard_map/ppermute | solution.py:1226
  528.4 3.4 collective-permute-start.15
  528.5 10.7 %collective-permute-start.16 = (f32[2560]{0:T(1024)S(1)}, f32[2560]{0:T(1024)S(1)}, u32[]{:S(2)}, u32[]{:S(2)}) collective-permute-start(f32[2560]{0:T(1024)S(1)} %add_add_fusion.3), channel_id=1, source_target_pairs={{0,4},{2,6},{4,0},{6,2},{1,5},{3,7},{5,1},{7,3},{8,12},{10,14},{12... | collective-permute-start | bytes 30728 | tf_op jit(solution)/shard_map/ppermute | solution.py:1226
  529.6 9.5 %collective-permute-start.17 = (f32[2560]{0:T(1024)S(1)}, f32[2560]{0:T(1024)S(1)}, u32[]{:S(2)}, u32[]{:S(2)}) collective-permute-start(f32[2560]{0:T(1024)S(1)} %add_add_fusion.3), channel_id=1, source_target_pairs={{0,6},{2,4},{4,2},{6,0},{1,7},{3,5},{5,3},{7,1},{8,14},{10,12},{12... | collective-permute-start | bytes 30728 | tf_op jit(solution)/shard_map/ppermute | solution.py:1226
  539.2 3.7 collective-permute-start.18
  539.3 4.8 collective-permute-start.30
  539.4 4.6 collective-permute-start.32
  546.2 2.3 copy-start.13
  546.3 3.3 copy-start.1
  (1 other events, 1.1 us)
